TPU v7x, 512 devices: a whole 4x8x8 slice. The times are simulated.
512 devices in a mesh: ctx: 64 (over z, x, core), head: 8 (over y).
Axes of the slice: x: 4, y: 8, z: 8, core: 2. Of those that a mesh axis runs over, the one named last changes fastest.
Arguments:
- queries: bfloat16 [8192, 4096], P('ctx', 'head'), may hold values from -60 to 60
- keys: bfloat16 [8192, 1024], P('ctx', 'head'), may hold values from -50 to 50
- values: bfloat16 [8192, 1024], P('ctx', 'head'), may hold values from -6 to 6
- vertical: int32 [8, 32], P('head'), may hold values from 0 to 127, as said below
- offsets: int32 [32, 64], P('head'), may hold values from 0 to 127, as said below
- send_order: int32 [64, 64], P('ctx'), may hold values from 0 to 63, each once within a row
- out_weight: bfloat16 [4096, 4096], P('head'), may hold values from -0.125 to 0.125
Outputs:
- output: bfloat16 [8192, 4096], P('ctx', 'head')
Inputs may be any that keep to these rules, and one draw needn't show every extreme that they name: `vertical`: each row holds 32 distinct block numbers in increasing order; of one row, at most 2 lie among the blocks of the positions of one index of ctx (2 blocks), and some index holds exactly 2 of them. Each row holds 64 distinct offsets and always contains 0, 1 and 127. `send_order`: each row is a permutation of the piece numbers.
All inputs are finite; a program needn't handle non-finite values.
Results may differ from a plain program's by a relative error of at most 0.0055.
Values may be sent and summed in bfloat16 or wider, within the bound.
No kernel may reach another device: no remote copies, remote signals or barrier semaphores. Data moves between devices by JAX's collectives and lax.ppermute only.
A program may use at most 64 MiB of HBM per device.

v0:
```python
import math

import jax
import jax.numpy as jnp
from jax import lax
from jax.sharding import PartitionSpec as P

HEAD_SIZE = 128
BLK = 64
NV = 32


def shifted_2(block, axis, distance):
    devices = range(lax.axis_size(axis))
    route = [(i - distance, i) for i in devices if i - distance in devices]
    return lax.ppermute(block, axis, route)


def local(queries, keys, values, vertical, offsets, send_order, out_weight):
    ctx_count = lax.axis_size("ctx")
    place_index = lax.axis_index("ctx")
    shard_rows = queries.shape[0]
    kv_local = keys.shape[1] // HEAD_SIZE
    q_local = queries.shape[1] // HEAD_SIZE
    query_group_width = q_local // kv_local
    per_dev = shard_rows // BLK
    score_scale = 1.0 / math.sqrt(HEAD_SIZE)
    kv_pair = jnp.stack([keys, values])
    stacked = kv_pair.reshape(2, per_dev, BLK, kv_local, HEAD_SIZE)
    owner_dev = vertical // per_dev
    within_dev = vertical % per_dev
    block_pick = within_dev[:, :, None] == jnp.arange(per_dev)[None, None, :]
    owned = (owner_dev == place_index)[:, :, None] & block_pick
    slots = jnp.einsum(
        "gnb,xbkgd->xgnkd", owned.astype(jnp.bfloat16), stacked, preferred_element_type=jnp.float32
    )
    vert_kv = lax.psum(slots, "ctx").astype(jnp.bfloat16)
    vert_keys = vert_kv[0].reshape(kv_local, NV * BLK, HEAD_SIZE)
    vert_vals = vert_kv[1].reshape(kv_local, NV * BLK, HEAD_SIZE)
    vert_pos = (vertical[:, :, None] * BLK + jnp.arange(BLK)[None, None, :]).reshape(
        kv_local, NV * BLK
    )
    earlier_kv = shifted_2(kv_pair, "ctx", 1)
    band_kv = jnp.concatenate([earlier_kv, kv_pair], axis=1).reshape(
        2, 2 * shard_rows, kv_local, HEAD_SIZE
    )
    band_pos = (place_index - 1) * shard_rows + jnp.arange(2 * shard_rows)
    query_pos = place_index * shard_rows + jnp.arange(shard_rows)
    in_vert = jnp.any((band_pos // BLK)[None, :, None] == vertical[:, None, :], axis=2)
    shifted = jnp.arange(3 * shard_rows) - shard_rows
    offset_table = jnp.any(offsets[:, None, :] == shifted[None, :, None], axis=2)
    lag_index = (
        jnp.arange(shard_rows)[:, None] - jnp.arange(2 * shard_rows)[None, :] + 2 * shard_rows
    )
    slash_mask = jnp.take(offset_table, lag_index, axis=1).reshape(
        kv_local, query_group_width, shard_rows, 2 * shard_rows
    )
    grouped = queries.reshape(shard_rows, kv_local, query_group_width, HEAD_SIZE)
    vert_scores = (
        jnp.einsum("igrd,gkd->grik", grouped, vert_keys, preferred_element_type=jnp.float32)
        * score_scale
    )
    band_scores = (
        jnp.einsum("igrd,kgd->grik", grouped, band_kv[0], preferred_element_type=jnp.float32)
        * score_scale
    )
    vert_mask = vert_pos[:, None, None, :] <= query_pos[None, None, :, None]
    band_mask = (
        slash_mask
        & jnp.logical_not(in_vert)[:, None, None, :]
        & (band_pos >= 0)[None, None, None, :]
    )
    row_max = jnp.maximum(
        jnp.max(jnp.where(vert_mask, vert_scores, -jnp.inf), axis=3),
        jnp.max(jnp.where(band_mask, band_scores, -jnp.inf), axis=3),
    )
    vert_weights = jnp.where(vert_mask, jnp.exp(vert_scores - row_max[..., None]), 0.0)
    band_weights = jnp.where(band_mask, jnp.exp(band_scores - row_max[..., None]), 0.0)
    row_total = jnp.sum(vert_weights, axis=3) + jnp.sum(band_weights, axis=3)
    weighted = jnp.einsum(
        "grik,gkd->grid",
        vert_weights.astype(jnp.bfloat16),
        vert_vals,
        preferred_element_type=jnp.float32,
    )
    weighted = weighted + jnp.einsum(
        "grik,kgd->grid",
        band_weights.astype(jnp.bfloat16),
        band_kv[1],
        preferred_element_type=jnp.float32,
    )
    attended = (
        (weighted / row_total[..., None])
        .transpose(2, 0, 1, 3)
        .reshape(shard_rows, q_local * HEAD_SIZE)
    )
    attended = attended.astype(jnp.bfloat16)
    piece_rows = shard_rows // ctx_count
    row_parts = attended.reshape(ctx_count, piece_rows, attended.shape[1])
    outgoing = jnp.take(row_parts, send_order[0], axis=0)
    arrived = lax.all_to_all(outgoing, "ctx", split_axis=0, concat_axis=0, tiled=True)
    partial_sums = jnp.dot(
        arrived.reshape(shard_rows, attended.shape[1]),
        out_weight,
        preferred_element_type=jnp.float32,
    )
    return lax.psum_scatter(partial_sums, "head", scatter_dimension=1, tiled=True).astype(
        jnp.bfloat16
    )


def solution(mesh):
    placed = (
        P("ctx", "head"),
        P("ctx", "head"),
        P("ctx", "head"),
        P("head", None),
        P("head", None),
        P("ctx", None),
        P("head", None),
    )
    return jax.shard_map(
        local, mesh=mesh, in_specs=placed, out_specs=P("ctx", "head"), check_vma=False
    )
```

profile of v0, /device:TPU:1, one launch (start us, length us, event | category | flops | bytes accessed | tf_op | source)
XLA Modules:
  0.0 490.9 jit_solution(2220783036985413741)
XLA Ops:
  6.5 0.0 copy-start
  6.5 0.0 copy-start.2
  6.5 0.0 copy-start.1
  6.5 0.0 reduce-scatter.2.cloned.1.call-start
  6.5 1.5 pad_maximum_fusion
  8.0 4.5 collective-permute-start
  12.6 0.7 broadcast_multiply_fusion
  13.2 0.7 fusion.38
  13.9 0.7 fusion.39
  14.6 0.7 compare_and_fusion
  15.2 0.7 compare_bitcast_fusion
  15.9 0.7 compare_reduce_fusion.1
  16.7 0.1 copy.41
  16.8 0.8 compare_reduce_fusion
  17.6 0.2 copy.27
  17.8 111.7 %gather_fusion = pred[32768,4]{1,0:T(32,128)(4,1)} fusion(pred[4,384]{0,1:T(8,128)(4,1)S(1)} %copy.27, s32[32768]{0:T(1024)S(1)} %broadcast_clamp_fusion), kind=kCustom, calls=%fused_computation | custom fusion | bytes 393216 | tf_op jit(solution)/shard_map/jit(_take)/gather | solution.py:55
  129.5 13.1 %copy.29 = pred[128,256,4]{0,1,2:T(32,128)(4,1)S(1)} copy(pred[128,256,4]{2,1,0:T(32,128)(4,1)} %bitcast.120) | data formatting | bytes 262144 | tf_op jit(solution)/shard_map/jit(_take)/gather | solution.py:55
  142.6 0.1 broadcast_reduce_fusion
  142.7 0.1 add.148
  142.8 0.1 add.150
  142.9 0.0 copy-done.2
  142.9 0.0 copy-done.1
  143.0 0.5 convolution_bitcast_fusion
  143.5 270.1 %all-reduce.1 = bf16[2,1,32,64,128]{4,2,3,0,1:T(8,128)(2,1)S(1)} all-reduce(f32[2,1,32,64,128]{4,2,3,0,1:T(8,128)S(1)} %convolution_bitcast_fusion), channel_id=1, replica_groups=mesh['ctx'=64,'head'=8] {'ctx'}, use_global_device_ids=true, to_apply=%region_0.1 | all-reduce | flops 524288 | bytes 3145728 | tf_op jit(solution)/shard_map/psum | solution.py:37
  413.5 0.1 fusion.46
  413.6 0.2 copy.25
  413.8 0.2 copy.31
  414.1 0.3 broadcast_compare_fusion
  414.4 0.0 copy-done
  414.4 0.7 fusion
  415.1 0.0 collective-permute-done
  415.2 0.9 maximum_maximum_fusion
  416.0 0.3 select_reduce_fusion
  416.3 0.2 fusion.15
  416.5 0.9 fusion.3
  417.4 1.2 fusion.6
  418.6 0.4 fusion.12
  419.0 0.1 copy.34
  419.1 0.1 convert_element_type.32
  419.2 0.8 gather_fusion.1
  420.0 0.2 broadcast_select_fusion
  420.2 22.6 %all_to_all.5 = bf16[64,2,512]{2,1,0:T(2,128)(2,1)S(1)} all-to-all(bf16[64,2,512]{2,1,0:T(2,128)(2,1)S(1)} %broadcast_select_fusion), channel_id=1, replica_groups=mesh['ctx'=64,'head'=8] {'ctx'}, dimensions={0} | all-to-all | bytes 262144 | tf_op jit(solution)/shard_map/all_to_all | solution.py:101
  442.8 0.1 reshape.436
  442.9 4.3 fusion.47
  447.1 0.0 reduce-scatter.2.cloned.1.call-update
  447.1 35.3 %reduce-scatter.2.cloned.1.call-done = f32[128,512]{1,0:T(8,128)} async-done(((f32[128,4096]{1,0:T(8,128)}), f32[128,512]{1,0:T(8,128)}) %reduce-scatter.2.cloned.1.call-update) | async-done | bytes 262160 | tf_op jit(solution)/shard_map/reduce_scatter | solution.py:107
  482.4 1.6 convert_element_type.33
  (15 shorter events, 0.2 us)
Async XLA Ops:
  6.5 407.9 %copy-start = (bf16[128,512]{1,0:T(8,128)(2,1)S(1)}, bf16[128,512]{1,0:T(8,128)(2,1)}, u32[]{:S(2)}) copy-start(bf16[128,512]{1,0:T(8,128)(2,1)} %param.7) | copy-start | bytes 393220
  6.5 136.3 %copy-start.2 = (bf16[128,128]{1,0:T(8,128)(2,1)S(1)}, bf16[128,128]{1,0:T(8,128)(2,1)}, u32[]{:S(2)}) copy-start(bf16[128,128]{1,0:T(8,128)(2,1)} %param.8) | copy-start | bytes 98308
  6.5 136.4 %copy-start.1 = (bf16[128,128]{1,0:T(8,128)(2,1)S(1)}, bf16[128,128]{1,0:T(8,128)(2,1)}, u32[]{:S(2)}) copy-start(bf16[128,128]{1,0:T(8,128)(2,1)} %param.9) | copy-start | bytes 98308
  6.5 475.9 %reduce-scatter.2.cloned.1.call-start = ((), (), s32[]{:S(2)}) async-start(), calls=%async_computation.2 | async-start | bytes 2359296 | tf_op jit(solution)/shard_map/reduce_scatter | solution.py:107
  8.0 407.1 %collective-permute-start = (bf16[2,128,128]{2,1,0:T(8,128)(2,1)}, bf16[2,128,128]{2,1,0:T(8,128)(2,1)}, u32[]{:S(2)}, u32[]{:S(2)}) collective-permute-start(bf16[2,128,128]{2,1,0:T(8,128)(2,1)} %pad_maximum_fusion), channel_id=1, source_target_pairs={{0,8},{8,16},{16,24},{24,32},{32,40},{40,48},{48,56},{56,64},{64,7... | collective-permute-start | bytes 196616 | tf_op jit(solution)/shard_map/ppermute | solution.py:16
Sparse Core Ops, SparseCore 0:
  447.3 35.1 reduce-scatter.1
where the time goes:
time: 494 us; the launch traced here: 491 us
  blocking collectives  293 us (59%)
  local copies, waits for them, and re-layouts  127 us (26%)
  waiting for transfers between devices  35.3 us (7%)
  between operations  13.6 us (3%)
  other arithmetic  10.6 us (2%)
  matrix products  7.29 us (1%)
    psum x1, blocking collectives, local(): vert_kv = lax.psum(slots, 'ctx').astype(jnp.bfloat16)  270 us
    gather x2, local copies, waits for them, and re-layouts, local(): jnp.take(offset_table, lag_index, axis=1)  125 us
    reduce_scatter x1, waiting for transfers between devices, local(): lax.psum_scatter(partial_sums, 'head', scatter_dimension=1, tiled=True)  35.3 us
    all_to_all x1, blocking collectives, local(): lax.all_to_all(outgoing, 'ctx', split_axis=0, concat_axis=0, tiled=True)  22.6 us
  transfers between devices with their start and end apart: 2, of which 1 were waited for; matrix products, arithmetic and copies ran while one was open for 27% of the time, Pallas kernels for 0%

commit v1 on v0

v1 whole, which is shorter than its diff:
```python
import math

import jax
import jax.numpy as jnp
from jax import lax
from jax.experimental import pallas as pl
from jax.experimental.pallas import tpu as pltpu
from jax.sharding import Mesh, PartitionSpec as P

HEAD = 128
BLK = 64
NV = 32
CTX = ("z", "x", "c")
VMEM = pl.BlockSpec(memory_space=pltpu.VMEM)
SMEM = pl.BlockSpec(memory_space=pltpu.SMEM)
F32 = jnp.float32
BF16 = jnp.bfloat16


def iota(shape, dim):
    return lax.broadcasted_iota(jnp.int32, shape, dim)


def select_kernel(vert, recv, out):
    rows = 2 * NV
    row = iota((rows, HEAD), 0)
    want = jnp.zeros((rows, HEAD), jnp.int32)
    for n in range(NV):
        want = jnp.where(row % NV == n, vert[0, n] * 2 + row // NV, want)
    lane = iota((rows, HEAD), 1)
    picked = jnp.zeros((rows, HEAD), F32)
    for half in range(2):
        one_hot = jnp.where(want == lane + half * HEAD, 1.0, 0.0).astype(BF16)
        picked += jnp.dot(one_hot, recv[pl.ds(half * HEAD, HEAD), :], preferred_element_type=F32)
    picked = picked.astype(BF16)
    for z in range(out.shape[0]):
        out[z] = picked


def dot_t(a, b):
    return lax.dot_general(a, b, (((1,), (1,)), ((), ())), preferred_element_type=F32)


def attention_kernel(place, vert, offsets, q, mine, other, prev, keys, values, target, out):
    rows = q.shape[0]
    band = 2 * rows
    ctx, core = place[0], place[1]
    base = ctx * rows
    lag = rows - iota((8, band), 1)
    table = jnp.zeros((8, band), F32)
    offs = offsets[...]
    for k in range(offs.shape[1]):
        table = jnp.where(offs[:, k : k + 1] == lag, 1.0, table)
    band_block = (base - rows) // BLK + iota((1, band), 1) // BLK
    closed = band_block < 0
    lane = iota((1, HEAD), 1)
    vpos = jnp.zeros((1, HEAD), jnp.int32)
    for n in range(NV):
        block = vert[0, n]
        closed = closed | (band_block == block)
        vpos = jnp.where(lane % NV == n, block * BLK, vpos)
    vpos = vpos + (lane // NV) * 8 - base
    parts = mine.shape[0] * mine.shape[2] // HEAD
    pos_mine, pos_other = [], []
    for m in range(parts):
        step = (m % 2) * 32 + (m // 2) * 2
        pos_mine.append(vpos + (step + core))
        pos_other.append(vpos + (step + 1 - core))
    query = iota((rows, 1), 0)
    mask_mine = jnp.concatenate(pos_mine, axis=1) <= query
    mask_other = jnp.concatenate(pos_other, axis=1) <= query
    k1 = mine[:, 0].reshape(-1, HEAD)
    v1 = mine[:, 1].reshape(-1, HEAD)
    k2 = other[:, 0].reshape(-1, HEAD)
    v2 = other[:, 1].reshape(-1, HEAD)
    kb = jnp.concatenate([prev[0], keys[...]], axis=0)
    vb = jnp.concatenate([prev[1], values[...]], axis=0)
    low = -jnp.inf
    factor = math.log2(math.e) / math.sqrt(HEAD)
    done = []
    for h in range(q.shape[1] // HEAD):
        qh = q[:, h * HEAD : (h + 1) * HEAD]
        spread = jnp.broadcast_to(table[h : h + 1], (rows, band))
        slash = pltpu.roll(spread, 0, 1, stride=1, stride_axis=0)
        mask_band = (slash > 0.5) & jnp.logical_not(closed)
        s0 = jnp.where(mask_band, dot_t(qh, kb), low)
        s1 = jnp.where(mask_mine, dot_t(qh, k1), low)
        s2 = jnp.where(mask_other, dot_t(qh, k2), low)
        top = jnp.maximum(
            jnp.maximum(jnp.max(s1, axis=1, keepdims=True), jnp.max(s2, axis=1, keepdims=True)),
            jnp.max(s0, axis=1, keepdims=True),
        )
        p0 = jnp.exp2((s0 - top) * factor)
        p1 = jnp.exp2((s1 - top) * factor)
        p2 = jnp.exp2((s2 - top) * factor)
        total = (
            jnp.sum(p0, axis=1, keepdims=True)
            + jnp.sum(p1, axis=1, keepdims=True)
            + jnp.sum(p2, axis=1, keepdims=True)
        )
        o = jnp.dot(p0.astype(BF16), vb, preferred_element_type=F32)
        o += jnp.dot(p1.astype(BF16), v1, preferred_element_type=F32)
        o += jnp.dot(p2.astype(BF16), v2, preferred_element_type=F32)
        done.append((o / total).astype(BF16))
    attended = jnp.concatenate(done, axis=1)
    one_hot = jnp.where(iota((rows, rows), 0) == target[...], 1.0, 0.0).astype(BF16)
    out[...] = lax.dot_general(
        one_hot, attended, (((0,), (0,)), ((), ())), preferred_element_type=F32
    ).astype(BF16)


def project_kernel(arrived, weight, out, held):
    rows = held.shape[0]

    @pl.when(pl.program_id(0) == 0)
    def _():
        new = iota((rows, rows), 0)
        old = (new % 16 // 2) * 16 + (new // 16) * 2 + new % 2
        one_hot = jnp.where(iota((rows, rows), 1) == old, 1.0, 0.0).astype(BF16)
        held[...] = jnp.dot(one_hot, arrived[...], preferred_element_type=F32).astype(BF16)

    part = jnp.dot(held[...], weight[...], preferred_element_type=F32).astype(BF16)
    out[...] = part.reshape(out.shape)


def local(queries, keys, values, vertical, offsets, send_order, out_weight):
    z_n, x_n, c_n, y_n = (lax.axis_size(a) for a in ("z", "x", "c", "y"))
    rows = queries.shape[0]
    n_ctx = z_n * x_n * c_n
    ctx = lax.axis_index(CTX)
    core = lax.axis_index("c")
    place = jnp.stack([ctx, core]).astype(jnp.int32)

    prev = lax.ppermute(jnp.stack([keys, values]), CTX, [(i, i + 1) for i in range(n_ctx - 1)])

    lanes = jnp.concatenate([keys[:BLK], values[:BLK], keys[BLK:], values[BLK:]], axis=1)
    recv = lax.all_to_all(lanes.reshape(n_ctx, 4, HEAD), CTX, 0, 0, tiled=True)
    picked = pl.pallas_call(
        select_kernel,
        out_shape=jax.ShapeDtypeStruct((z_n, 2 * NV, HEAD), BF16),
        in_specs=[SMEM, VMEM],
        out_specs=VMEM,
        name="select_rows",
    )(vertical, recv.reshape(4 * n_ctx, HEAD))
    by_z = lax.all_to_all(picked, "z", 0, 0, tiled=True)
    by_x = lax.all_to_all(jnp.broadcast_to(by_z[None], (x_n,) + by_z.shape), "x", 0, 0, tiled=True)
    mine = by_x.reshape(x_n * z_n, 2, NV, HEAD)
    other = lax.ppermute(mine, "c", [(0, 1), (1, 0)])

    order = send_order.reshape(z_n, x_n * c_n).T.reshape(1, n_ctx)
    target = (order[:, :, None] * 2 + jnp.arange(2)[None, None, :]).reshape(1, rows)
    padded = jnp.concatenate([offsets, offsets], axis=0)
    attended = pl.pallas_call(
        attention_kernel,
        out_shape=jax.ShapeDtypeStruct(queries.shape, BF16),
        in_specs=[SMEM, SMEM] + [VMEM] * 8,
        out_specs=VMEM,
        name="attention",
        compiler_params=pltpu.CompilerParams(vmem_limit_bytes=48 * 1024 * 1024),
    )(place, vertical, padded, queries, mine, other, prev, keys, values, target)

    arrived = lax.all_to_all(
        attended.reshape(x_n * c_n, z_n * 2, queries.shape[1]), ("x", "c"), 0, 0, tiled=True
    ).reshape(rows, queries.shape[1])
    width = out_weight.shape[1] // y_n
    partial = pl.pallas_call(
        project_kernel,
        grid=(y_n,),
        out_shape=jax.ShapeDtypeStruct((z_n, y_n, rows // z_n, width), BF16),
        in_specs=[
            pl.BlockSpec(arrived.shape, lambda j: (0, 0)),
            pl.BlockSpec((out_weight.shape[0], width), lambda j: (0, j)),
        ],
        out_specs=pl.BlockSpec((z_n, 1, rows // z_n, width), lambda j: (0, j, 0, 0)),
        scratch_shapes=[pltpu.VMEM(arrived.shape, BF16)],
        name="project",
    )(arrived, out_weight)
    sums = lax.all_to_all(
        partial.reshape(z_n * y_n, rows // z_n, width), ("z", "y"), 0, 0, tiled=True
    ).reshape(z_n, y_n, rows // z_n, width)
    return jnp.sum(sums.astype(F32), axis=1).astype(BF16).reshape(rows, width)


def solution(mesh):
    cut = Mesh(mesh.devices.reshape(8, 4, 2, 8), ("z", "x", "c", "y"))
    placed = (
        P(CTX, "y"),
        P(CTX, "y"),
        P(CTX, "y"),
        P("y", None),
        P("y", None),
        P(CTX, None),
        P("y", None),
    )
    return jax.shard_map(
        local, mesh=cut, in_specs=placed, out_specs=P(CTX, "y"), check_vma=False
    )
```

time: 494 us -> 124 us (0.25)
  blocking collectives: 293 us -> 95.7 us
  local copies, waits for them, and re-layouts: 127 us -> 4.58 us
  waiting for transfers between devices: 35.3 us -> 0.01 us
  between operations: 13.6 us -> 0.09 us
  Pallas kernels: 0 us -> 11.8 us
  other arithmetic: 10.6 us -> 3.14 us
  matrix products: 7.29 us -> 0 us
    psum x1 -> x0, blocking collectives: 270 us -> none  [local(): vert_kv = lax.psum(slots, 'ctx').astype(jnp.bfloat16)]
    gather x3 -> x0, local copies, waits for them, and re-layouts: 126 us -> none  [the longest x2 125 us: local(): jnp.take(offset_table, lag_index, axis=1)]
    all_to_all x1 -> x5, blocking collectives: 22.6 us -> 95.7 us  [the longest x1 39.9 us: local(): lax.all_to_all(partial.reshape(z_n * y_n, rows // z_n, width), ('z', 'y')...]
    reduce_scatter x1 -> x0, waiting for transfers between devices: 35.3 us -> none  [local(): lax.psum_scatter(partial_sums, 'head', scatter_dimension=1, tiled=True)]
    pallas_call x0 -> x3, Pallas kernels: none -> 11.8 us  [the longest x1 6.87 us: local(): pl.pallas_call(project_kernel, grid=(y_n,), out_shape=jax.ShapeDtypeStruc...]
    dot_general x6 -> x0, matrix products: 7.29 us -> none  [the longest x1 4.26 us: local(): jnp.dot(arrived.reshape(shard_rows, attended.shape[1]), out_weight, prefe...]
  transfers between devices with their start and end apart: 2 -> 2, of which waited for: 1 -> 0; matrix products, arithmetic and copies ran while one was open for 27% -> 2% of each run, Pallas kernels for 0% -> 0%
where the time goes in v1:
time: 124 us; the launch traced here: 122 us
  blocking collectives  95.7 us (77%)
  Pallas kernels  11.8 us (10%)
  starting transfers between devices  6.52 us (5%)
  local copies, waits for them, and re-layouts  4.58 us (4%)
  other arithmetic  3.14 us (3%)
    all_to_all x1, blocking collectives, local(): lax.all_to_all(partial.reshape(z_n * y_n, rows // z_n, width), ('z', 'y')...  39.9 us
    all_to_all x1, blocking collectives, local(): recv = lax.all_to_all(lanes.reshape(n_ctx, 4, HEAD), CTX, 0, 0, tiled=True)  24.8 us
    all_to_all x1, blocking collectives, local(): by_z = lax.all_to_all(picked, 'z', 0, 0, tiled=True)  11.7 us
    all_to_all x1, blocking collectives, local(): lax.all_to_all(jnp.broadcast_to(by_z[None], (x_n,) + by_z.shape), 'x', 0,...  10.3 us
    all_to_all x1, blocking collectives, local(): lax.all_to_all(attended.reshape(x_n * c_n, z_n * 2, queries.shape[1]), ('...  9 us
    pallas_call x1, Pallas kernels, local(): pl.pallas_call(project_kernel, grid=(y_n,), out_shape=jax.ShapeDtypeStruc...  6.87 us
    ppermute x1, starting transfers between devices, local(): other = lax.ppermute(mine, 'c', [(0, 1), (1, 0)])  4.44 us
    pallas_call x1, Pallas kernels, local(): pl.pallas_call(attention_kernel, out_shape=jax.ShapeDtypeStruct(queries.s...  3.29 us
  transfers between devices with their start and end apart: 2, of which 0 were waited for; matrix products, arithmetic and copies ran while one was open for 2% of the time, Pallas kernels for 0%

profile of v1, /device:TPU:1, one launch (start us, length us, event | category | flops | bytes accessed | tf_op | source)
XLA Modules:
  0.0 121.9 jit_solution(4855047096540429945)
XLA Ops:
  0.0 0.8 fusion
  0.8 24.8 %all_to_all.25 = bf16[64,4,128]{2,1,0:T(4,128)(2,1)} all-to-all(bf16[64,4,128]{2,1,0:T(4,128)(2,1)S(1)} %reshape.69), channel_id=1, replica_groups=mesh['z'=8,'x'=4,'c'=2,'y'=8] {'z','x','c'}, dimensions={0} | all-to-all | bytes 131072 | tf_op jit(solution)/shard_map/all_to_all | solution.py:137
  25.6 1.7 %select_rows.1 = bf16[8,64,128]{2,1,0:T(8,128)(2,1)} custom-call(s32[1,32]{1,0:T(1,128)} %vert.3, bf16[256,128]{1,0:T(8,128)(2,1)} %bitcast.22), custom_call_target="tpu_custom_call" | custom-call | tf_op jit(solution)/shard_map/select_rows/pallas_call | solution.py:138
  27.3 11.7 %all_to_all.26 = bf16[8,64,128]{2,1,0:T(8,128)(2,1)S(1)} all-to-all(bf16[8,64,128]{2,1,0:T(8,128)(2,1)} %select_rows.1), channel_id=1, replica_groups=mesh['z'=8,'x'=4,'c'=2,'y'=8] {'z'}, dimensions={0} | all-to-all | bytes 262144 | tf_op jit(solution)/shard_map/all_to_all | solution.py:145
  39.0 0.1 broadcast_in_dim.2
  39.1 10.3 %all_to_all.27 = bf16[4,8,64,128]{3,2,1,0:T(8,128)(2,1)S(1)} all-to-all(bf16[4,8,64,128]{3,2,1,0:T(8,128)(2,1)S(1)} %broadcast_in_dim.2), channel_id=1, replica_groups=mesh['z'=8,'x'=4,'c'=2,'y'=8] {'x'}, dimensions={0} | all-to-all | bytes 1048576 | tf_op jit(solution)/shard_map/all_to_all | solution.py:146
  49.4 4.4 %collective-permute-start = (bf16[32,2,32,128]{3,2,1,0:T(8,128)(2,1)S(1)}, bf16[32,2,32,128]{3,2,1,0:T(8,128)(2,1)S(1)}, u32[]{:S(2)}, u32[]{:S(2)}) collective-permute-start(bf16[32,2,32,128]{3,2,1,0:T(8,128)(2,1)S(1)} %bitcast.15), channel_id=1, source_target_pairs={{0,8},{8,0},{1,9},{9,1},{2,10},{10,2},{3,11},{11,3},{4,12},{12,4},... | collective-permute-start | bytes 1572872 | tf_op jit(solution)/shard_map/ppermute | solution.py:148
  53.8 0.8 pad_maximum_fusion.1
  54.6 2.1 %collective-permute-start.1 = (bf16[2,128,128]{2,1,0:T(8,128)(2,1)S(1)}, bf16[2,128,128]{2,1,0:T(8,128)(2,1)S(1)}, u32[]{:S(2)}, u32[]{:S(2)}) collective-permute-start(bf16[2,128,128]{2,1,0:T(8,128)(2,1)S(1)} %pad_maximum_fusion.1), channel_id=1, source_target_pairs={{0,8},{8,16},{16,24},{24,32},{32,40},{40,48},{48,56},{56,64},{64,7... | collective-permute-start | bytes 196616 | tf_op jit(solution)/shard_map/ppermute | solution.py:134
  56.7 0.7 multiply_reduce_fusion
  57.4 0.1 mul.30
  57.5 0.1 copy.9
  57.5 0.1 mul.32
  57.6 0.1 add.34
  57.7 0.1 add.35
  57.9 0.1 add.37
  58.0 0.8 pad_add_fusion.offsets
  58.8 0.1 pad_add_fusion.1.place
  58.9 0.0 collective-permute-done.1.prev
  58.9 0.0 collective-permute-done.other
  58.9 0.0 copy-start
  58.9 0.8 copy-done
  59.6 0.0 copy-start.1
  59.6 0.8 copy-done.1
  60.4 0.0 copy-start.2
  60.4 0.9 copy-done.2
  61.3 0.0 copy-start.3
  61.3 0.7 copy-done.3
  61.9 3.3 %attention.1 = bf16[128,512]{1,0:T(8,128)(2,1)S(1)} custom-call(s32[2]{0:T(128)S(1)} %pad_add_fusion.1.place, s32[1,32]{1,0:T(1,128)S(1)} %copy-done.3, s32[8,64]{1,0:T(8,128)S(1)} %pad_add_fusion.offsets, bf16[128,512]{1,0:T(8,128)(2,1)S(1)} %copy-done.2, bf16[32,2,32,128]{3,2,1,0:T(8,128)(2,1)S(1)} %bitcast.16, ...), custom_call_target="tpu_custom_call" | custom-call | tf_op jit(solution)/shard_map/attention/pallas_call | solution.py:153
  65.2 9.0 %all_to_all.28 = bf16[8,16,512]{2,1,0:T(8,128)(2,1)} all-to-all(bf16[8,16,512]{2,1,0:T(8,128)(2,1)S(1)} %bitcast.17), channel_id=1, replica_groups=mesh['z'=8,'x'=4,'c'=2,'y'=8] {'x','c'}, dimensions={0} | all-to-all | bytes 262144 | tf_op jit(solution)/shard_map/all_to_all | solution.py:162
  74.2 6.9 %project.1 = bf16[8,8,16,512]{3,2,1,0:T(8,128)(2,1)} custom-call(bf16[128,512]{1,0:T(8,128)(2,1)} %bitcast.21, bf16[512,4096]{1,0:T(8,128)(2,1)} %weight.1), custom_call_target="tpu_custom_call" | custom-call | tf_op jit(solution)/shard_map/project/pallas_call | solution.py:166
  81.1 39.9 %all_to_all.29 = bf16[64,16,512]{2,1,0:T(8,128)(2,1)S(1)} all-to-all(bf16[64,16,512]{2,1,0:T(8,128)(2,1)} %bitcast.20), channel_id=1, replica_groups=mesh['z'=8,'x'=4,'c'=2,'y'=8] {'z','y'}, dimensions={0} | all-to-all | bytes 2097152 | tf_op jit(solution)/shard_map/all_to_all | solution.py:178
  121.1 0.8 bitcast_reduce_fusion
  (4 shorter events, 0.0 us)
Async XLA Ops:
  49.4 9.5 %collective-permute-start = (bf16[32,2,32,128]{3,2,1,0:T(8,128)(2,1)S(1)}, bf16[32,2,32,128]{3,2,1,0:T(8,128)(2,1)S(1)}, u32[]{:S(2)}, u32[]{:S(2)}) collective-permute-start(bf16[32,2,32,128]{3,2,1,0:T(8,128)(2,1)S(1)} %bitcast.15), channel_id=1, source_target_pairs={{0,8},{8,0},{1,9},{9,1},{2,10},{10,2},{3,11},{11,3},{4,12},{12,4},... | collective-permute-start | bytes 1572872 | tf_op jit(solution)/shard_map/ppermute | solution.py:148
  54.6 4.3 %collective-permute-start.1 = (bf16[2,128,128]{2,1,0:T(8,128)(2,1)S(1)}, bf16[2,128,128]{2,1,0:T(8,128)(2,1)S(1)}, u32[]{:S(2)}, u32[]{:S(2)}) collective-permute-start(bf16[2,128,128]{2,1,0:T(8,128)(2,1)S(1)} %pad_maximum_fusion.1), channel_id=1, source_target_pairs={{0,8},{8,16},{16,24},{24,32},{32,40},{40,48},{48,56},{56,64},{64,7... | collective-permute-start | bytes 196616 | tf_op jit(solution)/shard_map/ppermute | solution.py:134
  58.9 0.8 copy-start
  59.6 0.8 copy-start.1
  60.4 0.9 copy-start.2
  61.3 0.7 copy-start.3

commit v2 on v1

v2 whole, which is shorter than its diff:
```python
import math

import jax
import jax.numpy as jnp
from jax import lax
from jax.experimental import pallas as pl
from jax.experimental.pallas import tpu as pltpu
from jax.sharding import Mesh, PartitionSpec as P

HEAD = 128
BLK = 64
NV = 32
CTX = ("z", "x", "c")
VMEM = pl.BlockSpec(memory_space=pltpu.VMEM)
SMEM = pl.BlockSpec(memory_space=pltpu.SMEM)
HBM = pl.BlockSpec(memory_space=pltpu.HBM)
F32 = jnp.float32
BF16 = jnp.bfloat16


def iota(shape, dim):
    return lax.broadcasted_iota(jnp.int32, shape, dim)


def pick(one_hot, rows):
    one_hot = jnp.where(one_hot, 1.0, 0.0).astype(BF16)
    return jnp.dot(one_hot, rows, preferred_element_type=F32).astype(BF16)


def select_kernel(vert, recv, out):
    rows = 2 * NV
    count = recv.shape[0]
    row = iota((rows, 1), 0)
    want = jnp.zeros((rows, 1), jnp.int32)
    for n in range(NV):
        want = jnp.where(row % NV == n, vert[0, n] * 2, want)
    want = want + row // NV
    held = recv[...]
    picked = pick(iota((rows, count), 1) == want, held)
    ahead = pick(iota((count, count), 1) == (iota((count, 1), 0) + (count - 4)) % count, held)
    for chip in range(out.shape[0]):
        out[chip, :rows] = picked
        out[chip, rows:] = ahead[chip * 8 : chip * 8 + 8]


def dot_t(a, b):
    return lax.dot_general(a, b, (((1,), (1,)), ((), ())), preferred_element_type=F32)


def attention_kernel(
    place, vert, q_in, keys_in, values_in, offsets_in, order_in, weight_in, mine, other, out, weight,
    q, keys, values, offsets, order, sems,
):
    moves = [
        pltpu.make_async_copy(a, b, sems.at[i])
        for i, (a, b) in enumerate(
            [(q_in, q), (keys_in, keys), (values_in, values), (offsets_in, offsets), (order_in, order), (weight_in, weight)]
        )
    ]
    for move in moves:
        move.start()
    rows = q.shape[0]
    heads = q.shape[1] // HEAD
    band = 2 * rows
    ctx, core = place[0], place[1]
    base = ctx * rows
    band_block = (base - rows) // BLK + iota((1, band), 1) // BLK
    closed = band_block < 0
    lane = iota((1, HEAD), 1)
    vpos = jnp.zeros((1, HEAD), jnp.int32)
    for n in range(NV):
        block = vert[0, n]
        closed = closed | (band_block == block)
        vpos = jnp.where(lane % NV == n, block * BLK, vpos)
    vpos = vpos + (lane // NV) * 2 - base
    parts = mine.shape[0] * NV // HEAD
    mask_at = [
        jnp.concatenate([vpos + (m * (2 * HEAD // NV) + side) for m in range(parts)], axis=1)
        for side in (core, 1 - core)
    ]
    query = iota((rows, 1), 0)
    mask_mine = mask_at[0] <= query
    mask_other = mask_at[1] <= query
    k1 = mine[:, :NV].reshape(-1, HEAD)
    v1 = mine[:, NV : 2 * NV].reshape(-1, HEAD)
    k2 = other[:, :NV].reshape(-1, HEAD)
    v2 = other[:, NV : 2 * NV].reshape(-1, HEAD)
    at = iota((band, 1), 0)
    k_of = at % BLK
    source = (k_of // 2) * 8 + core * 4 + (at // BLK % 2) * 2 + at // rows
    from_mine = jnp.where(k_of % 2 == core, source, -1)
    from_other = jnp.where(k_of % 2 == core, -1, source)
    cols = iota((band, band), 1)
    ahead = pick(cols == from_mine, mine[:, 2 * NV :].reshape(-1, HEAD)) + pick(
        cols == from_other, other[:, 2 * NV :].reshape(-1, HEAD)
    )
    for move in moves[:5]:
        move.wait()
    kb = jnp.concatenate([ahead[:rows], keys[...]], axis=0)
    vb = jnp.concatenate([ahead[rows:], values[...]], axis=0)
    lag = rows - iota((heads, band), 1)
    table = jnp.zeros((heads, band), F32)
    offs = offsets[...]
    for k in range(offs.shape[1]):
        table = jnp.where(offs[:, k : k + 1] == lag, 1.0, table)
    low = -jnp.inf
    factor = math.log2(math.e) / math.sqrt(HEAD)
    done = []
    for h in range(heads):
        qh = q[:, h * HEAD : (h + 1) * HEAD]
        spread = jnp.broadcast_to(table[h : h + 1], (rows, band))
        slash = pltpu.roll(spread, 0, 1, stride=1, stride_axis=0)
        mask_band = (slash > 0.5) & jnp.logical_not(closed)
        s0 = jnp.where(mask_band, dot_t(qh, kb), low)
        s1 = jnp.where(mask_mine, dot_t(qh, k1), low)
        s2 = jnp.where(mask_other, dot_t(qh, k2), low)
        top = jnp.maximum(
            jnp.maximum(jnp.max(s1, axis=1, keepdims=True), jnp.max(s2, axis=1, keepdims=True)),
            jnp.max(s0, axis=1, keepdims=True),
        )
        p0 = jnp.exp2((s0 - top) * factor)
        p1 = jnp.exp2((s1 - top) * factor)
        p2 = jnp.exp2((s2 - top) * factor)
        total = (
            jnp.sum(p0, axis=1, keepdims=True)
            + jnp.sum(p1, axis=1, keepdims=True)
            + jnp.sum(p2, axis=1, keepdims=True)
        )
        o = jnp.dot(p0.astype(BF16), vb, preferred_element_type=F32)
        o += jnp.dot(p1.astype(BF16), v1, preferred_element_type=F32)
        o += jnp.dot(p2.astype(BF16), v2, preferred_element_type=F32)
        done.append((o / total).astype(BF16))
    lanes = rows * heads
    spread = iota((order.shape[1], lanes), 0) == iota((order.shape[1], lanes), 1) // (2 * heads)
    target = jnp.dot(
        order[...].astype(F32).astype(BF16),
        jnp.where(spread, 1.0, 0.0).astype(BF16),
        preferred_element_type=F32,
    ).astype(jnp.int32)
    row = iota((1, lanes), 1)
    target = target * 2 + row % 2 + (row // 2 % heads) * rows
    one_hot = jnp.where(iota((lanes, lanes), 0) == target, 1.0, 0.0).astype(BF16)
    moved = lax.dot_general(
        one_hot,
        jnp.concatenate(done, axis=0),
        (((0,), (0,)), ((), ())),
        preferred_element_type=F32,
    ).astype(BF16)
    out[...] = moved.reshape(out.shape)
    moves[5].wait()


def project_kernel(arrived, weight, out):
    heads = arrived.shape[1] // 2
    rows = out.shape[1]
    held = arrived[...].reshape(-1, HEAD)
    row = iota((rows, 1), 0)
    at = iota((rows, rows * heads), 1)
    full = jnp.concatenate(
        [pick(at == (row // 2) * (2 * heads) + h * 2 + row % 2, held) for h in range(heads)], axis=1
    )
    width = out.shape[2]
    for j in range(out.shape[0]):
        out[j] = jnp.dot(
            full, weight[:, j * width : (j + 1) * width], preferred_element_type=F32
        ).astype(BF16)


def local(queries, keys, values, vertical, offsets, send_order, out_weight):
    z_n, x_n, c_n, y_n = (lax.axis_size(a) for a in ("z", "x", "c", "y"))
    rows = queries.shape[0]
    heads = queries.shape[1] // HEAD
    n_ctx = z_n * x_n * c_n
    chips = z_n * x_n
    place = jnp.stack([lax.axis_index(CTX), lax.axis_index("c")]).astype(jnp.int32)

    lanes = jnp.concatenate([keys[:BLK], values[:BLK], keys[BLK:], values[BLK:]], axis=1)
    recv = lax.all_to_all(lanes.reshape(n_ctx, 4, HEAD), CTX, 0, 0, tiled=True)
    picked = pl.pallas_call(
        select_kernel,
        out_shape=jax.ShapeDtypeStruct((chips, 2 * NV + 8, HEAD), BF16),
        in_specs=[SMEM, VMEM],
        out_specs=VMEM,
        name="select_rows",
    )(vertical, recv.reshape(4 * n_ctx, HEAD))
    mine = lax.all_to_all(picked, ("z", "x"), 0, 0, tiled=True)
    other = lax.ppermute(mine, "c", [(0, 1), (1, 0)])

    attended, weight = pl.pallas_call(
        attention_kernel,
        out_shape=[
            jax.ShapeDtypeStruct((n_ctx, 2 * heads, HEAD), BF16),
            jax.ShapeDtypeStruct(out_weight.shape, BF16),
        ],
        in_specs=[SMEM, SMEM] + [HBM] * 6 + [VMEM] * 2,
        out_specs=[VMEM, VMEM],
        scratch_shapes=[
            pltpu.VMEM(queries.shape, BF16),
            pltpu.VMEM(keys.shape, BF16),
            pltpu.VMEM(values.shape, BF16),
            pltpu.VMEM(offsets.shape, jnp.int32),
            pltpu.VMEM(send_order.shape, jnp.int32),
            pltpu.SemaphoreType.DMA((6,)),
        ],
        name="attention",
        compiler_params=pltpu.CompilerParams(vmem_limit_bytes=32 * 1024 * 1024),
    )(place, vertical, queries, keys, values, offsets, send_order, out_weight, mine, other)

    arrived = lax.all_to_all(attended, CTX, 0, 0, tiled=True)
    width = out_weight.shape[1] // y_n
    partial = pl.pallas_call(
        project_kernel,
        out_shape=jax.ShapeDtypeStruct((y_n, rows, width), BF16),
        in_specs=[VMEM, VMEM],
        out_specs=VMEM,
        name="project",
        compiler_params=pltpu.CompilerParams(vmem_limit_bytes=32 * 1024 * 1024),
    )(arrived, weight)
    sums = lax.all_to_all(partial, "y", 0, 0, tiled=True)
    return jnp.sum(sums.astype(F32), axis=0).astype(BF16)


def solution(mesh):
    cut = Mesh(mesh.devices.reshape(8, 4, 2, 8), ("z", "x", "c", "y"))
    placed = (
        P(CTX, "y"),
        P(CTX, "y"),
        P(CTX, "y"),
        P("y", None),
        P("y", None),
        P(CTX, None),
        P("y", None),
    )
    return jax.shard_map(
        local, mesh=cut, in_specs=placed, out_specs=P(CTX, "y"), check_vma=False
    )
```

time: 124 us -> 119 us (0.960); the launches traced: 122 us -> 118 us
  Pallas kernels: 11.8 us -> 7.31 us
  local copies, waits for them, and re-layouts: 4.58 us -> 7.39 us
  starting transfers between devices: 6.52 us -> 3.99 us
  other arithmetic: 3.14 us -> 0.9 us
  waiting for transfers between devices: 0.01 us -> 1.52 us
  blocking collectives: 95.7 us -> 97.2 us
    pallas_call x3, Pallas kernels: 11.8 us -> 7.31 us  [the longest x1 4.52 us: local(): pl.pallas_call(attention_kernel, out_shape=[jax.ShapeDtypeStruct((n_ctx,...]
    unnamed x8 -> x14, local copies, waits for them, and re-layouts: 3.07 us -> 6.6 us
    ppermute x1 -> x0, starting transfers between devices: 2.08 us -> none  [local(): lax.ppermute(jnp.stack([keys, values]), CTX, [(i, i + 1) for i in range(n...]
    all_to_all x4 -> x3, blocking collectives: 70.9 us -> 72.4 us  [the longest x1 34.4 us: local(): sums = lax.all_to_all(partial, 'y', 0, 0, tiled=True)]
    ppermute x1, waiting for transfers between devices: 0.01 us -> 1.52 us  [local(): other = lax.ppermute(mine, 'c', [(0, 1), (1, 0)])]
  transfers between devices with their start and end apart: 2 -> 1, of which waited for: 0 -> 1; matrix products, arithmetic and copies ran while one was open for 2% -> 0% of each run, Pallas kernels for 0% -> 0%
where the time goes in v2:
time: 119 us; the launch traced here: 118 us
  blocking collectives  97.2 us (82%)
  local copies, waits for them, and re-layouts  7.39 us (6%)
  Pallas kernels  7.31 us (6%)
  starting transfers between devices  3.99 us (3%)
  waiting for transfers between devices  1.52 us (1%)
    all_to_all x1, blocking collectives, local(): sums = lax.all_to_all(partial, 'y', 0, 0, tiled=True)  34.4 us
    all_to_all x1, blocking collectives, local(): recv = lax.all_to_all(lanes.reshape(n_ctx, 4, HEAD), CTX, 0, 0, tiled=True)  24.8 us
    all_to_all x1, blocking collectives, local(): mine = lax.all_to_all(picked, ('z', 'x'), 0, 0, tiled=True)  21.7 us
    all_to_all x1, blocking collectives, local(): arrived = lax.all_to_all(attended, CTX, 0, 0, tiled=True)  16.3 us
    unnamed x14, local copies, waits for them, and re-layouts  6.6 us
    pallas_call x1, Pallas kernels, local(): pl.pallas_call(attention_kernel, out_shape=[jax.ShapeDtypeStruct((n_ctx,...  4.52 us
    ppermute x1, starting transfers between devices, local(): other = lax.ppermute(mine, 'c', [(0, 1), (1, 0)])  3.99 us
  transfers between devices with their start and end apart: 1, of which 1 were waited for; matrix products, arithmetic and copies ran while one was open for 0% of the time, Pallas kernels for 0%

profile of v2, /device:TPU:1, one launch (start us, length us, event | category | flops | bytes accessed | tf_op | source)
XLA Modules:
  0.0 118.4 jit_solution(222804575240081864)
XLA Ops:
  0.0 0.8 fusion
  0.8 24.8 %all_to_all.20 = bf16[64,4,128]{2,1,0:T(4,128)(2,1)} all-to-all(bf16[64,4,128]{2,1,0:T(4,128)(2,1)S(1)} %reshape.6), channel_id=1, replica_groups=mesh['z'=8,'x'=4,'c'=2,'y'=8] {'z','x','c'}, dimensions={0} | all-to-all | bytes 131072 | tf_op jit(solution)/shard_map/all_to_all | solution.py:178
  25.6 1.9 %select_rows.1 = bf16[32,72,128]{2,1,0:T(8,128)(2,1)} custom-call(s32[1,32]{1,0:T(1,128)} %vert.3, bf16[256,128]{1,0:T(8,128)(2,1)} %bitcast.3), custom_call_target="tpu_custom_call" | custom-call | tf_op jit(solution)/shard_map/select_rows/pallas_call | solution.py:179
  27.5 21.7 %all_to_all.21.mine = bf16[32,72,128]{2,1,0:T(8,128)(2,1)S(1)} all-to-all(bf16[32,72,128]{2,1,0:T(8,128)(2,1)} %select_rows.1), channel_id=1, replica_groups=mesh['z'=8,'x'=4,'c'=2,'y'=8] {'z','x'}, dimensions={0} | all-to-all | bytes 1179648 | tf_op jit(solution)/shard_map/all_to_all | solution.py:186
  49.2 4.0 %collective-permute-start = (bf16[32,72,128]{2,1,0:T(8,128)(2,1)S(1)}, bf16[32,72,128]{2,1,0:T(8,128)(2,1)S(1)}, u32[]{:S(2)}, u32[]{:S(2)}) collective-permute-start(bf16[32,72,128]{2,1,0:T(8,128)(2,1)S(1)} %all_to_all.21.mine), channel_id=1, source_target_pairs={{0,8},{8,0},{1,9},{9,1},{2,10},{10,2},{3,11},{11,3},{4,12},{12,4},... | collective-permute-start | bytes 1769480 | tf_op jit(solution)/shard_map/ppermute | solution.py:187
  53.2 0.1 pad_add_fusion.place
  53.3 1.5 %collective-permute-done.other = bf16[32,72,128]{2,1,0:T(8,128)(2,1)S(1)} collective-permute-done((bf16[32,72,128]{2,1,0:T(8,128)(2,1)S(1)}, bf16[32,72,128]{2,1,0:T(8,128)(2,1)S(1)}, u32[]{:S(2)}, u32[]{:S(2)}) %collective-permute-start) | collective-permute-done | bytes 589856 | tf_op jit(solution)/shard_map/ppermute | solution.py:187
  54.8 0.0 copy-start
  54.8 2.2 %copy-done = bf16[512,4096]{1,0:T(8,128)(2,1)S(1)} copy-done((bf16[512,4096]{1,0:T(8,128)(2,1)S(1)}, bf16[512,4096]{1,0:T(8,128)(2,1)}, u32[]{:S(2)}) %copy-start) | copy-done | bytes 4194328
  57.0 0.0 copy-start.1
  57.0 0.8 copy-done.1
  57.7 0.0 copy-start.2
  57.7 0.8 copy-done.2
  58.5 0.0 copy-start.3
  58.5 0.9 copy-done.3
  59.4 0.0 copy-start.4
  59.4 0.7 copy-done.4
  60.1 0.0 copy-start.5
  60.1 0.7 copy-done.5
  60.7 0.0 copy-start.6
  60.7 0.7 copy-done.6
  61.4 4.5 %attention.1 = (bf16[64,8,128]{2,1,0:T(8,128)(2,1)S(1)}, bf16[512,4096]{1,0:T(8,128)(2,1)S(1)}) custom-call(s32[2]{0:T(128)S(1)} %pad_add_fusion.place, s32[1,32]{1,0:T(1,128)S(1)} %copy-done.5, bf16[128,512]{1,0:T(8,128)(2,1)S(1)} %copy-done.3, bf16[128,128]{1,0:T(8,128)(2,1)S(1)} %copy-done.1, bf16[128,128]{1,0:T(8,128)(2,1)S(1)} %copy-done.2, ...), custom_call_target="tpu_custom_call" | custom-call | tf_op jit(solution)/shard_map/attention/pallas_call | solution.py:189
  65.9 16.3 %all_to_all.22.arrived = bf16[64,8,128]{2,1,0:T(8,128)(2,1)S(1)} all-to-all(bf16[64,8,128]{2,1,0:T(8,128)(2,1)S(1)} %get-tuple-element.7), channel_id=1, replica_groups=mesh['z'=8,'x'=4,'c'=2,'y'=8] {'z','x','c'}, dimensions={0} | all-to-all | bytes 262144 | tf_op jit(solution)/shard_map/all_to_all | solution.py:209
  82.2 0.9 project.1
  83.1 34.4 %all_to_all.23 = bf16[8,128,512]{2,1,0:T(8,128)(2,1)S(1)} all-to-all(bf16[8,128,512]{2,1,0:T(8,128)(2,1)S(1)} %project.1), channel_id=1, replica_groups=mesh['z'=8,'x'=4,'c'=2,'y'=8] {'y'}, dimensions={0} | all-to-all | bytes 2097152 | tf_op jit(solution)/shard_map/all_to_all | solution.py:219
  117.6 0.8 reduce_sum.12
  (2 shorter events, 0.0 us)
Async XLA Ops:
  49.2 5.6 %collective-permute-start = (bf16[32,72,128]{2,1,0:T(8,128)(2,1)S(1)}, bf16[32,72,128]{2,1,0:T(8,128)(2,1)S(1)}, u32[]{:S(2)}, u32[]{:S(2)}) collective-permute-start(bf16[32,72,128]{2,1,0:T(8,128)(2,1)S(1)} %all_to_all.21.mine), channel_id=1, source_target_pairs={{0,8},{8,0},{1,9},{9,1},{2,10},{10,2},{3,11},{11,3},{4,12},{12,4},... | collective-permute-start | bytes 1769480 | tf_op jit(solution)/shard_map/ppermute | solution.py:187
  54.8 2.2 %copy-start = (bf16[512,4096]{1,0:T(8,128)(2,1)S(1)}, bf16[512,4096]{1,0:T(8,128)(2,1)}, u32[]{:S(2)}) copy-start(bf16[512,4096]{1,0:T(8,128)(2,1)} %weight_in.1) | copy-start | bytes 12582916
  57.0 0.8 copy-start.1
  57.7 0.8 copy-start.2
  58.5 0.9 copy-start.3
  59.4 0.7 copy-start.4
  60.1 0.7 copy-start.5
  60.7 0.7 copy-start.6

commit v3 on v1

v3 whole, which is shorter than its diff:
```python
import math

import jax
import jax.numpy as jnp
from jax import lax
from jax.experimental import pallas as pl
from jax.experimental.pallas import tpu as pltpu
from jax.sharding import Mesh, PartitionSpec as P

HEAD = 128
BLK = 64
NV = 32
CTX = ("z", "x", "c")
VMEM = pl.BlockSpec(memory_space=pltpu.VMEM)
HBM = pl.BlockSpec(memory_space=pltpu.HBM)
F32 = jnp.float32
BF16 = jnp.bfloat16
LOW = -1e30
FACTOR = math.log2(math.e) / math.sqrt(HEAD)
ORDER, VERT, PLACE, CORE = 4, 5, 6, 7


def iota(shape, dim):
    return lax.broadcasted_iota(jnp.int32, shape, dim)


def bits(mask):
    return jnp.where(mask, 1.0, 0.0).astype(BF16)


def pick(mask, rows):
    return jnp.dot(bits(mask), rows, preferred_element_type=F32).astype(BF16)


def pick_t(mask, rows):
    return lax.dot_general(
        bits(mask), rows, (((0,), (0,)), ((), ())), preferred_element_type=F32
    ).astype(BF16)


def dot_t(a, b):
    return lax.dot_general(a, b, (((1,), (1,)), ((), ())), preferred_element_type=F32)


def by_destination(order, rows, heads):
    lanes = rows * heads
    count = rows // 2
    spread = bits(iota((count, lanes), 0) == iota((count, lanes), 1) // (2 * heads))
    piece = jnp.dot(order.astype(F32).astype(BF16), spread, preferred_element_type=F32)
    at = iota((1, lanes), 1)
    target = piece.astype(jnp.int32) * 2 + at % 2 + (at // 2 % heads) * rows
    return iota((lanes, lanes), 0) == target


def head_rows(ref, first, heads):
    return jnp.concatenate(
        [ref[:, (first + h) * HEAD : (first + h + 1) * HEAD] for h in range(heads)], axis=0
    )


def pack_kernel(ints, qkv, out, kv):
    rows = qkv.shape[0]
    heads = qkv.shape[1] // HEAD - 2
    count = rows // 2
    order = ints[ORDER : ORDER + 1, :count]
    kv[...] = qkv[:, heads * HEAD :]
    moved = pick_t(by_destination(order, rows, heads), head_rows(qkv, 0, heads))
    out[:, :8] = moved.reshape(count, 8, HEAD)
    new = iota((8 * count, 1), 0)
    slot = new % 8
    source = jnp.where(slot < 4, (slot % 2) * rows + (slot // 2) * BLK + new // 8, -1)
    kv_rows = jnp.dot(
        bits(iota((8 * count, 2 * rows), 1) == source),
        head_rows(qkv, heads, 2),
        preferred_element_type=F32,
    )
    diagonal = iota((count, count), 0) == iota((count, count), 1)
    number = jnp.sum(jnp.where(diagonal, order.astype(F32), 0.0), axis=1, keepdims=True)
    number = jnp.broadcast_to(number, (count, HEAD)).astype(BF16)
    owner = jnp.where(slot == 4, new // 8, -1)
    numbers = jnp.dot(
        bits(iota((8 * count, count), 1) == owner), number, preferred_element_type=F32
    )
    out[:, 8:] = (kv_rows + numbers).astype(BF16).reshape(count, 8, HEAD)


def split3(x):
    high = x.astype(BF16).astype(F32)
    middle = (x - high).astype(BF16).astype(F32)
    return high, middle, x - high - middle


def band_kernel(ints, qkv, prev, recv, out):
    rows = qkv.shape[0]
    heads = qkv.shape[1] // HEAD - 2
    count = rows // 2
    chips = out.shape[0]
    band = 2 * rows
    vert = ints[VERT : VERT + 1, :]
    ctx = ints[PLACE : PLACE + 1, :1]
    lane = iota((1, 2 * NV), 1)
    block = vert[:, : 2 * NV]
    want = (block // 2) * 8 + (block % 2) * 2 + lane // NV
    held = recv[:, 8:].reshape(8 * count, HEAD)
    picked = pick_t(iota((8 * count, 2 * NV), 0) == want, held)
    closed = jnp.zeros((1, band), F32)
    part = iota((1, band), 1) // BLK
    for j in range(band // BLK):
        number = ctx * (rows // BLK) + (j - rows // BLK)
        hit = jnp.max(jnp.where(vert == number, 1.0, 0.0), axis=1, keepdims=True)
        hit = jnp.where(number < 0, 1.0, hit)
        closed = jnp.where(part == j, hit, closed)
    lag = rows - iota((heads, band), 1)
    table = jnp.zeros((heads, band), F32)
    offs = ints[:heads, :BLK]
    for k in range(BLK):
        table = jnp.where(offs[:, k : k + 1] == lag, 1.0, table)
    kb = jnp.concatenate([prev[:, :HEAD], qkv[:, heads * HEAD : (heads + 1) * HEAD]], axis=0)
    vb = jnp.concatenate([prev[:, HEAD:], qkv[:, (heads + 1) * HEAD :]], axis=0)
    lanes = iota((rows, HEAD), 1) % 8
    done = []
    for h in range(heads):
        spread = jnp.broadcast_to(table[h : h + 1], (rows, band))
        slash = pltpu.roll(spread, 0, 1, stride=1, stride_axis=0)
        mask = (slash > 0.5) & (closed < 0.5)
        s = jnp.where(mask, dot_t(qkv[:, h * HEAD : (h + 1) * HEAD], kb), LOW)
        top = jnp.max(s, axis=1, keepdims=True)
        p = jnp.where(mask, jnp.exp2((s - top) * FACTOR), 0.0)
        total = jnp.sum(p, axis=1, keepdims=True)
        o = jnp.dot(p.astype(BF16), vb, preferred_element_type=F32)
        o = o / jnp.where(total > 0.0, total, 1.0)
        sums = jnp.zeros((rows, HEAD), F32)
        for j, term in enumerate(split3(top) + split3(total)):
            sums = jnp.where(lanes == j, term, sums)
        done.append(jnp.concatenate([o.astype(BF16), sums.astype(BF16)], axis=1))
    order = ints[ORDER : ORDER + 1, :count]
    moved = pick_t(by_destination(order, rows, heads), jnp.concatenate(done, axis=0))
    size = 8 * count
    own = iota((size, HEAD), 1) // 8 == iota((size, HEAD), 0) % 8
    sums = jnp.where(own, moved[:, HEAD:].astype(F32), 0.0).astype(BF16)
    new = iota((8 * chips, 1), 0)
    owner = jnp.where(new % 8 < 2, (new // 8) * 2 + new % 8, -1)
    sums = pick(iota((8 * chips, size), 1) // 8 == owner, sums)
    out[:, 2 * NV : 2 * NV + 16] = moved[:, :HEAD].reshape(chips, 16, HEAD)
    out[:, 2 * NV + 16 :] = sums.reshape(chips, 8, HEAD)
    for chip in range(chips):
        out[chip, : 2 * NV] = picked


def finish_kernel(ints, recv, mine, other, weight_in, out, weight, sem):
    move = pltpu.make_async_copy(weight_in, weight, sem)
    move.start()
    count = recv.shape[0]
    chips = mine.shape[0]
    size = 8 * count
    rows = out.shape[1]
    heads = size // rows
    vert = ints[VERT : VERT + 1, :]
    core = ints[CORE : CORE + 1, :1]
    first = core == 0
    vpos = vert * BLK + (iota((1, HEAD), 1) // NV) * 2
    step = 2 * HEAD // NV
    parts = chips * NV // HEAD
    pos_mine = jnp.concatenate([vpos + core + m * step for m in range(parts)], axis=1)
    pos_other = jnp.concatenate([vpos + (1 - core) + m * step for m in range(parts)], axis=1)
    slot = iota((count, 8, HEAD), 1)
    number = jnp.sum(
        jnp.where(slot == 4, recv[:, 8:].astype(F32), 0.0), axis=1, keepdims=True
    )
    number = jnp.broadcast_to(number, (count, 8, HEAD)).reshape(size, HEAD)[:, :1]
    at = iota((size, 1), 0)
    qpos = (at // 8) * rows + number.astype(jnp.int32) * 2 + at % 2

    def by_owner(cut):
        a, b = cut(mine), cut(other)
        return jnp.concatenate([jnp.where(first, a, b), jnp.where(first, b, a)], axis=1)

    base = 2 * NV

    def slash_rows(ref):
        return jnp.where(
            first, ref[:, base : base + 8].astype(F32), ref[:, base + 8 : base + 16].astype(F32)
        )

    def sums_row(ref):
        tail = ref[:, base + 16 :].astype(F32)
        which = iota(tail.shape, 1)
        row = jnp.sum(jnp.where(which == core, tail, 0.0), axis=1, keepdims=True)
        return jnp.broadcast_to(row, tail.shape)

    slash = by_owner(slash_rows).reshape(size, HEAD)
    sums = by_owner(sums_row).reshape(size, HEAD)
    lane = iota((size, HEAD), 1)
    own = lane // 8 == iota((size, HEAD), 0) % 8
    top_b = jnp.sum(jnp.where(own & (lane % 8 < 3), sums, 0.0), axis=1, keepdims=True)
    total_b = jnp.sum(jnp.where(own & (lane % 8 >= 3), sums, 0.0), axis=1, keepdims=True)

    q = recv[:, :8].reshape(size, HEAD)
    k1 = mine[:, :NV].reshape(-1, HEAD)
    v1 = mine[:, NV : 2 * NV].reshape(-1, HEAD)
    k2 = other[:, :NV].reshape(-1, HEAD)
    v2 = other[:, NV : 2 * NV].reshape(-1, HEAD)
    done = []
    for b in range(heads):
        cut = slice(b * rows, (b + 1) * rows)
        s1 = jnp.where(pos_mine <= qpos[cut], dot_t(q[cut], k1), -jnp.inf)
        s2 = jnp.where(pos_other <= qpos[cut], dot_t(q[cut], k2), -jnp.inf)
        top = jnp.maximum(jnp.max(s1, axis=1, keepdims=True), jnp.max(s2, axis=1, keepdims=True))
        top = jnp.maximum(top, top_b[cut])
        p1 = jnp.exp2((s1 - top) * FACTOR)
        p2 = jnp.exp2((s2 - top) * FACTOR)
        share = total_b[cut] * jnp.exp2((top_b[cut] - top) * FACTOR)
        total = jnp.sum(p1, axis=1, keepdims=True) + jnp.sum(p2, axis=1, keepdims=True) + share
        o = jnp.dot(p1.astype(BF16), v1, preferred_element_type=F32)
        o += jnp.dot(p2.astype(BF16), v2, preferred_element_type=F32)
        o += share * slash[cut]
        done.append((o / total).astype(BF16))
    attended = jnp.concatenate(done, axis=0)
    row = iota((rows, 1), 0)
    cols = iota((rows, size), 1)
    full = jnp.concatenate(
        [pick(cols == (row // 2) * 8 + h * 2 + row % 2, attended) for h in range(heads)], axis=1
    )
    width = out.shape[2]
    move.wait()
    for j in range(out.shape[0]):
        out[j] = jnp.dot(
            full, weight[:, j * width : (j + 1) * width], preferred_element_type=F32
        ).astype(BF16)


def local(queries, keys, values, vertical, offsets, send_order, out_weight):
    z_n, x_n, c_n, y_n = (lax.axis_size(a) for a in ("z", "x", "c", "y"))
    rows = queries.shape[0]
    n_ctx = z_n * x_n * c_n
    chips = z_n * x_n
    params = pltpu.CompilerParams(vmem_limit_bytes=50 * 1024 * 1024)

    qkv = jnp.concatenate([queries, keys, values], axis=1)
    pad = ((0, 0), (0, HEAD - offsets.shape[1]))
    ints = jnp.concatenate(
        [
            jnp.pad(offsets, pad),
            jnp.pad(send_order, pad),
            jnp.tile(vertical, (1, HEAD // NV)),
            jnp.full((1, HEAD), lax.axis_index(CTX), jnp.int32),
            jnp.full((1, HEAD), lax.axis_index("c"), jnp.int32),
        ],
        axis=0,
    )
    packed, kv = pl.pallas_call(
        pack_kernel,
        out_shape=[
            jax.ShapeDtypeStruct((n_ctx, 16, HEAD), BF16),
            jax.ShapeDtypeStruct((rows, 2 * HEAD), BF16),
        ],
        in_specs=[VMEM, VMEM],
        out_specs=[VMEM, VMEM],
        name="pack",
    )(ints, qkv)
    prev = lax.ppermute(kv, CTX, [(i, i + 1) for i in range(n_ctx - 1)])
    recv = lax.all_to_all(packed, CTX, 0, 0, tiled=True)
    parts = pl.pallas_call(
        band_kernel,
        out_shape=jax.ShapeDtypeStruct((chips, 2 * NV + 24, HEAD), BF16),
        in_specs=[VMEM] * 4,
        out_specs=VMEM,
        name="slash",
        compiler_params=pltpu.CompilerParams(vmem_limit_bytes=32 * 1024 * 1024),
    )(ints, qkv, prev, recv)
    mine = lax.all_to_all(parts, ("z", "x"), 0, 0, tiled=True)
    other = lax.ppermute(mine, "c", [(0, 1), (1, 0)])
    width = out_weight.shape[1] // y_n
    partial = pl.pallas_call(
        finish_kernel,
        out_shape=jax.ShapeDtypeStruct((y_n, rows, width), BF16),
        in_specs=[VMEM] * 4 + [HBM],
        out_specs=VMEM,
        scratch_shapes=[pltpu.VMEM(out_weight.shape, BF16), pltpu.SemaphoreType.DMA],
        name="finish",
        compiler_params=params,
    )(ints, recv, mine, other, out_weight)
    sums = lax.all_to_all(partial, "y", 0, 0, tiled=True)
    return jnp.sum(sums.astype(F32), axis=0).astype(BF16)


def solution(mesh):
    cut = Mesh(mesh.devices.reshape(8, 4, 2, 8), ("z", "x", "c", "y"))
    placed = (
        P(CTX, "y"),
        P(CTX, "y"),
        P(CTX, "y"),
        P("y", None),
        P("y", None),
        P(CTX, None),
        P("y", None),
    )
    return jax.shard_map(
        local, mesh=cut, in_specs=placed, out_specs=P(CTX, "y"), check_vma=False
    )
```

time: 124 us -> 111 us (0.90)
  blocking collectives: 95.7 us -> 58.1 us
  starting transfers between devices: 6.52 us -> 22.8 us
  waiting for transfers between devices: 0.01 us -> 11.4 us
  local copies, waits for them, and re-layouts: 4.58 us -> 7.47 us
  Pallas kernels: 11.8 us -> 9.28 us
  other arithmetic: 3.14 us -> 0.81 us
    all_to_all x5 -> x2, blocking collectives: 95.7 us -> 58.1 us  [the longest x1 34.6 us: local(): sums = lax.all_to_all(partial, 'y', 0, 0, tiled=True)]
    all_to_all x0 -> x1, starting transfers between devices: none -> 14.8 us  [local(): recv = lax.all_to_all(packed, CTX, 0, 0, tiled=True)]
    all_to_all x0 -> x1, waiting for transfers between devices: none -> 7.81 us  [local(): recv = lax.all_to_all(packed, CTX, 0, 0, tiled=True)]
    pallas_call x3, Pallas kernels: 11.8 us -> 9.28 us  [the longest x1 5.26 us: local(): pl.pallas_call(finish_kernel, out_shape=jax.ShapeDtypeStruct((y_n, rows,...]
    ppermute x1, waiting for transfers between devices: 0.01 us -> 1.81 us  [local(): prev = lax.ppermute(kv, CTX, [(i, i + 1) for i in range(n_ctx - 1)])]
    ppermute x1, waiting for transfers between devices: 0.01 us -> 1.8 us  [local(): other = lax.ppermute(mine, 'c', [(0, 1), (1, 0)])]
    ppermute x1, starting transfers between devices: 2.08 us -> 3.54 us  [local(): prev = lax.ppermute(kv, CTX, [(i, i + 1) for i in range(n_ctx - 1)])]
    concatenate x0 -> x2, local copies, waits for them, and re-layouts: none -> 1.4 us  [the longest x1 0.77 us: local(): qkv = jnp.concatenate([queries, keys, values], axis=1)]
  transfers between devices with their start and end apart: 2 -> 3, of which waited for: 0 -> 3; matrix products, arithmetic and copies ran while one was open for 2% -> 0% of each run, Pallas kernels for 0% -> 0%
where the time goes in v3:
time: 111 us; the launch traced here: 110 us
  blocking collectives  58.1 us (52%)
  starting transfers between devices  22.8 us (21%)
  waiting for transfers between devices  11.4 us (10%)
  Pallas kernels  9.28 us (8%)
  local copies, waits for them, and re-layouts  7.47 us (7%)
    all_to_all x1, blocking collectives, local(): sums = lax.all_to_all(partial, 'y', 0, 0, tiled=True)  34.6 us
    all_to_all x1, blocking collectives, local(): mine = lax.all_to_all(parts, ('z', 'x'), 0, 0, tiled=True)  23.5 us
    all_to_all x1, starting transfers between devices, local(): recv = lax.all_to_all(packed, CTX, 0, 0, tiled=True)  14.8 us
    all_to_all x1, waiting for transfers between devices, local(): recv = lax.all_to_all(packed, CTX, 0, 0, tiled=True)  7.81 us
    pallas_call x1, Pallas kernels, local(): pl.pallas_call(finish_kernel, out_shape=jax.ShapeDtypeStruct((y_n, rows,...  5.26 us
    ppermute x1, starting transfers between devices, local(): other = lax.ppermute(mine, 'c', [(0, 1), (1, 0)])  4.41 us
    unnamed x10, local copies, waits for them, and re-layouts  3.97 us
    ppermute x1, starting transfers between devices, local(): prev = lax.ppermute(kv, CTX, [(i, i + 1) for i in range(n_ctx - 1)])  3.54 us
  transfers between devices with their start and end apart: 3, of which 3 were waited for; matrix products, arithmetic and copies ran while one was open for 0% of the time, Pallas kernels for 0%

profile of v3, /device:TPU:1, one launch (start us, length us, event | category | flops | bytes accessed | tf_op | source)
XLA Modules:
  0.0 109.9 jit_solution(13786028730927075091)
XLA Ops:
  0.0 0.7 tile.12
  0.7 0.1 tile.13
  0.7 0.7 pad.9
  1.4 0.7 pad.8
  2.1 0.9 constant_dynamic-update-slice_fusion.2
  3.0 0.8 constant_dynamic-update-slice_fusion.1
  3.8 0.8 constant_dynamic-update-slice_fusion.qkv
  4.6 0.0 copy-start
  4.6 0.6 concatenate.6.ints
  5.2 0.0 copy-done
  5.2 2.3 %pack.1 = (bf16[64,16,128]{2,1,0:T(8,128)(2,1)}, bf16[128,256]{1,0:T(8,128)(2,1)}) custom-call(s32[8,128]{1,0:T(8,128)} %concatenate.6.ints, bf16[128,768]{1,0:T(8,128)(2,1)} %copy-done), custom_call_target="tpu_custom_call" | custom-call | tf_op jit(solution)/shard_map/pack/pallas_call | solution.py:251
  7.5 14.8 %all-to-all-start = ((bf16[64,16,128]{2,1,0:T(8,128)(2,1)}), bf16[64,16,128]{2,1,0:T(8,128)(2,1)S(1)}, u32[]{:S(2)}, u32[]{:S(2)}) async-start(bf16[64,16,128]{2,1,0:T(8,128)(2,1)} %get-tuple-element.7), calls=%async_computation | async-start | bytes 524288 | tf_op jit(solution)/shard_map/all_to_all | solution.py:262
  22.3 3.5 %collective-permute-start = (bf16[128,256]{1,0:T(8,128)(2,1)}, bf16[128,256]{1,0:T(8,128)(2,1)S(1)}, u32[]{:S(2)}, u32[]{:S(2)}) collective-permute-start(bf16[128,256]{1,0:T(8,128)(2,1)} %get-tuple-element.8), channel_id=1, source_target_pairs={{0,8},{8,16},{16,24},{24,32},{32,40},{40,48},{48,56},{56,64},{64,7... | collective-permute-start | bytes 196616 | tf_op jit(solution)/shard_map/ppermute | solution.py:261
  25.9 1.8 %collective-permute-done.prev = bf16[128,256]{1,0:T(8,128)(2,1)S(1)} collective-permute-done((bf16[128,256]{1,0:T(8,128)(2,1)}, bf16[128,256]{1,0:T(8,128)(2,1)S(1)}, u32[]{:S(2)}, u32[]{:S(2)}) %collective-permute-start) | collective-permute-done | bytes 65568 | tf_op jit(solution)/shard_map/ppermute | solution.py:261
  27.7 7.8 %all-to-all-done.recv = bf16[64,16,128]{2,1,0:T(8,128)(2,1)S(1)} async-done(((bf16[64,16,128]{2,1,0:T(8,128)(2,1)}), bf16[64,16,128]{2,1,0:T(8,128)(2,1)S(1)}, u32[]{:S(2)}, u32[]{:S(2)}) %all-to-all-start) | async-done | bytes 262176 | tf_op jit(solution)/shard_map/all_to_all | solution.py:262
  35.5 0.0 copy-start.1
  35.5 0.9 copy-done.1
  36.4 0.0 copy-start.2
  36.4 0.7 copy-done.2
  37.1 1.7 %slash.1 = bf16[32,88,128]{2,1,0:T(8,128)(2,1)S(1)} custom-call(s32[8,128]{1,0:T(8,128)S(1)} %copy-done.2, bf16[128,768]{1,0:T(8,128)(2,1)S(1)} %copy-done.1, bf16[128,256]{1,0:T(8,128)(2,1)S(1)} %collective-permute-done.prev, bf16[64,16,128]{2,1,0:T(8,128)(2,1)S(1)} %all-to-all-done.recv), custom_call_target="tpu_custom_call" | custom-call | tf_op jit(solution)/shard_map/slash/pallas_call | solution.py:263
  38.9 23.5 %all_to_all.15.mine = bf16[32,88,128]{2,1,0:T(8,128)(2,1)S(1)} all-to-all(bf16[32,88,128]{2,1,0:T(8,128)(2,1)S(1)} %slash.1), channel_id=1, replica_groups=mesh['z'=8,'x'=4,'c'=2,'y'=8] {'z','x'}, dimensions={0} | all-to-all | bytes 1441792 | tf_op jit(solution)/shard_map/all_to_all | solution.py:271
  62.4 4.4 %collective-permute-start.1 = (bf16[32,88,128]{2,1,0:T(8,128)(2,1)S(1)}, bf16[32,88,128]{2,1,0:T(8,128)(2,1)S(1)}, u32[]{:S(2)}, u32[]{:S(2)}) collective-permute-start(bf16[32,88,128]{2,1,0:T(8,128)(2,1)S(1)} %all_to_all.15.mine), channel_id=1, source_target_pairs={{0,8},{8,0},{1,9},{9,1},{2,10},{10,2},{3,11},{11,3},{4,12},{12,4},... | collective-permute-start | bytes 2162696 | tf_op jit(solution)/shard_map/ppermute | solution.py:272
  66.8 1.8 %collective-permute-done.1.other = bf16[32,88,128]{2,1,0:T(8,128)(2,1)S(1)} collective-permute-done((bf16[32,88,128]{2,1,0:T(8,128)(2,1)S(1)}, bf16[32,88,128]{2,1,0:T(8,128)(2,1)S(1)}, u32[]{:S(2)}, u32[]{:S(2)}) %collective-permute-start.1) | collective-permute-done | bytes 720928 | tf_op jit(solution)/shard_map/ppermute | solution.py:272
  68.6 0.0 copy-start.3
  68.6 0.7 copy-done.3
  69.3 5.3 %finish.1 = bf16[8,128,512]{2,1,0:T(8,128)(2,1)S(1)} custom-call(s32[8,128]{1,0:T(8,128)S(1)} %copy-done.3, bf16[64,16,128]{2,1,0:T(8,128)(2,1)S(1)} %all-to-all-done.recv, bf16[32,88,128]{2,1,0:T(8,128)(2,1)S(1)} %all_to_all.15.mine, bf16[32,88,128]{2,1,0:T(8,128)(2,1)S(1)} %collective-permute-done.1.other, bf16[512,4096]{1,0:T(8,128)(2,1)} %weight_in.1), custom_call_target="tpu_custom_call" | custom-call | tf_op jit(solution)/shard_map/finish/pallas_call | solution.py:274
  74.6 34.6 %all_to_all.16 = bf16[8,128,512]{2,1,0:T(8,128)(2,1)S(1)} all-to-all(bf16[8,128,512]{2,1,0:T(8,128)(2,1)S(1)} %finish.1), channel_id=1, replica_groups=mesh['z'=8,'x'=4,'c'=2,'y'=8] {'y'}, dimensions={0} | all-to-all | bytes 2097152 | tf_op jit(solution)/shard_map/all_to_all | solution.py:283
  109.1 0.8 reduce_sum.12
  (2 shorter events, 0.0 us)
Async XLA Ops:
  4.6 0.7 copy-start
  7.5 28.0 %all-to-all-start = ((bf16[64,16,128]{2,1,0:T(8,128)(2,1)}), bf16[64,16,128]{2,1,0:T(8,128)(2,1)S(1)}, u32[]{:S(2)}, u32[]{:S(2)}) async-start(bf16[64,16,128]{2,1,0:T(8,128)(2,1)} %get-tuple-element.7), calls=%async_computation | async-start | bytes 524288 | tf_op jit(solution)/shard_map/all_to_all | solution.py:262
  22.3 5.4 %collective-permute-start = (bf16[128,256]{1,0:T(8,128)(2,1)}, bf16[128,256]{1,0:T(8,128)(2,1)S(1)}, u32[]{:S(2)}, u32[]{:S(2)}) collective-permute-start(bf16[128,256]{1,0:T(8,128)(2,1)} %get-tuple-element.8), channel_id=1, source_target_pairs={{0,8},{8,16},{16,24},{24,32},{32,40},{40,48},{48,56},{56,64},{64,7... | collective-permute-start | bytes 196616 | tf_op jit(solution)/shard_map/ppermute | solution.py:261
  35.5 0.9 copy-start.1
  36.4 0.7 copy-start.2
  62.4 6.2 %collective-permute-start.1 = (bf16[32,88,128]{2,1,0:T(8,128)(2,1)S(1)}, bf16[32,88,128]{2,1,0:T(8,128)(2,1)S(1)}, u32[]{:S(2)}, u32[]{:S(2)}) collective-permute-start(bf16[32,88,128]{2,1,0:T(8,128)(2,1)S(1)} %all_to_all.15.mine), channel_id=1, source_target_pairs={{0,8},{8,0},{1,9},{9,1},{2,10},{10,2},{3,11},{11,3},{4,12},{12,4},... | collective-permute-start | bytes 2162696 | tf_op jit(solution)/shard_map/ppermute | solution.py:272
  68.6 0.7 copy-start.3

commit v4 on v3

v4 whole, which is shorter than its diff:
```python
import math

import jax
import jax.numpy as jnp
from jax import lax
from jax.experimental import pallas as pl
from jax.experimental.pallas import tpu as pltpu
from jax.sharding import Mesh, PartitionSpec as P

HEAD = 128
BLK = 64
NV = 32
CTX = ("z", "x", "c")
VMEM = pl.BlockSpec(memory_space=pltpu.VMEM)
HBM = pl.BlockSpec(memory_space=pltpu.HBM)
F32 = jnp.float32
BF16 = jnp.bfloat16
LOW = -1e30
FACTOR = math.log2(math.e) / math.sqrt(HEAD)
SMEM = pl.BlockSpec(memory_space=pltpu.SMEM)
MIB = 1024 * 1024
VERT, WANT, CORE = 0, 1, 2


def iota(shape, dim):
    return lax.broadcasted_iota(jnp.int32, shape, dim)


def bits(mask):
    return jnp.where(mask, 1.0, 0.0).astype(BF16)


def pick(mask, rows):
    return jnp.dot(bits(mask), rows, preferred_element_type=F32).astype(BF16)


def pick_t(mask, rows):
    return lax.dot_general(
        bits(mask), rows, (((0,), (0,)), ((), ())), preferred_element_type=F32
    ).astype(BF16)


def dot_t(a, b):
    return lax.dot_general(a, b, (((1,), (1,)), ((), ())), preferred_element_type=F32)


def by_destination(order, rows, heads):
    lanes = rows * heads
    count = rows // 2
    spread = bits(iota((count, lanes), 0) == iota((count, lanes), 1) // (2 * heads))
    piece = jnp.dot(order.astype(F32).astype(BF16), spread, preferred_element_type=F32)
    at = iota((1, lanes), 1)
    target = piece.astype(jnp.int32) * 2 + at % 2 + (at // 2 % heads) * rows
    return iota((lanes, lanes), 0) == target


def head_rows(ref, heads):
    return jnp.concatenate([ref[:, h * HEAD : (h + 1) * HEAD] for h in range(heads)], axis=0)


def load(pairs, sems):
    moves = [pltpu.make_async_copy(a, b, sems.at[i]) for i, (a, b) in enumerate(pairs)]
    for move in moves:
        move.start()
    for move in moves:
        move.wait()


def pack_kernel(q_in, keys_in, values_in, order_in, out, kv, q, keys, values, order, sems):
    load([(q_in, q), (keys_in, keys), (values_in, values), (order_in, order)], sems)
    rows = q.shape[0]
    heads = q.shape[1] // HEAD
    count = rows // 2
    kv[:, :HEAD] = keys[...]
    kv[:, HEAD:] = values[...]
    moved = pick_t(by_destination(order[...], rows, heads), head_rows(q, heads))
    out[:, :8] = moved.reshape(count, 8, HEAD)
    new = iota((8 * count, 1), 0)
    slot = new % 8
    source = jnp.where(slot < 4, (slot % 2) * rows + (slot // 2) * BLK + new // 8, -1)
    kv_rows = jnp.dot(
        bits(iota((8 * count, 2 * rows), 1) == source),
        jnp.concatenate([keys[...], values[...]], axis=0),
        preferred_element_type=F32,
    )
    diagonal = iota((count, count), 0) == iota((count, count), 1)
    number = jnp.sum(jnp.where(diagonal, order[...].astype(F32), 0.0), axis=1, keepdims=True)
    number = jnp.broadcast_to(number, (count, HEAD)).astype(BF16)
    owner = jnp.where(slot == 4, new // 8, -1)
    numbers = jnp.dot(
        bits(iota((8 * count, count), 1) == owner), number, preferred_element_type=F32
    )
    out[:, 8:] = (kv_rows + numbers).astype(BF16).reshape(count, 8, HEAD)


def split3(x):
    high = x.astype(BF16).astype(F32)
    middle = (x - high).astype(BF16).astype(F32)
    return high, middle, x - high - middle


def band_kernel(
    place, q_in, keys_in, values_in, order_in, offsets_in, vert_in, prev_in, out, ints,
    q, keys, values, order, offsets, vertical, prev, sems,
):
    load(
        [(q_in, q), (keys_in, keys), (values_in, values), (order_in, order), (offsets_in, offsets), (vert_in, vertical), (prev_in, prev)],
        sems,
    )
    rows = q.shape[0]
    heads = q.shape[1] // HEAD
    count = rows // 2
    chips = out.shape[0]
    band = 2 * rows
    ctx, core = place[0], place[1]
    spread = bits(iota((NV, HEAD), 0) == iota((NV, HEAD), 1) % NV)
    vert = jnp.dot(
        vertical[...].astype(F32).astype(BF16), spread, preferred_element_type=F32
    ).astype(jnp.int32)
    table_row = iota(ints.shape, 0)
    want = (vert // 2) * 8 + (vert % 2) * 2 + iota((1, HEAD), 1) // NV
    ints[...] = jnp.where(
        table_row == VERT, vert, jnp.where(table_row == WANT, want, jnp.where(table_row == CORE, core, 0))
    )
    closed = jnp.zeros((1, band), F32)
    part = iota((1, band), 1) // BLK
    for j in range(band // BLK):
        number = ctx * (rows // BLK) + (j - rows // BLK)
        hit = jnp.max(jnp.where(vert == number, 1.0, 0.0), axis=1, keepdims=True)
        hit = jnp.where(number < 0, 1.0, hit)
        closed = jnp.where(part == j, hit, closed)
    lag = rows - iota((heads, band), 1)
    table = jnp.zeros((heads, band), F32)
    offs = offsets[...]
    for k in range(offs.shape[1]):
        table = jnp.where(offs[:, k : k + 1] == lag, 1.0, table)
    kb = jnp.concatenate([prev[:, :HEAD], keys[...]], axis=0)
    vb = jnp.concatenate([prev[:, HEAD:], values[...]], axis=0)
    lanes = iota((rows, HEAD), 1) % 8
    done = []
    for h in range(heads):
        spread = jnp.broadcast_to(table[h : h + 1], (rows, band))
        slash = pltpu.roll(spread, 0, 1, stride=1, stride_axis=0)
        mask = (slash > 0.5) & (closed < 0.5)
        s = jnp.where(mask, dot_t(q[:, h * HEAD : (h + 1) * HEAD], kb), LOW)
        top = jnp.max(s, axis=1, keepdims=True)
        p = jnp.where(mask, jnp.exp2((s - top) * FACTOR), 0.0)
        total = jnp.sum(p, axis=1, keepdims=True)
        o = jnp.dot(p.astype(BF16), vb, preferred_element_type=F32)
        o = o / jnp.where(total > 0.0, total, 1.0)
        sums = jnp.zeros((rows, HEAD), F32)
        for j, term in enumerate(split3(top) + split3(total)):
            sums = jnp.where(lanes == j, term, sums)
        done.append(jnp.concatenate([o.astype(BF16), sums.astype(BF16)], axis=1))
    moved = pick_t(by_destination(order[...], rows, heads), jnp.concatenate(done, axis=0))
    size = 8 * count
    own = iota((size, HEAD), 1) // 8 == iota((size, HEAD), 0) % 8
    sums = jnp.where(own, moved[:, HEAD:].astype(F32), 0.0).astype(BF16)
    new = iota((8 * chips, 1), 0)
    owner = jnp.where(new % 8 < 2, (new // 8) * 2 + new % 8, -1)
    sums = pick(iota((8 * chips, size), 1) // 8 == owner, sums)
    out[:, :16] = moved[:, :HEAD].reshape(chips, 16, HEAD)
    out[:, 16:] = sums.reshape(chips, 8, HEAD)


def select_kernel(ints, recv, slash, out, kept):
    kept[...] = ints[...]
    want = ints[WANT : WANT + 1, : 2 * NV]
    held = recv[:, 8:].reshape(-1, HEAD)
    picked = pick_t(iota((held.shape[0], 2 * NV), 0) == want, held)
    out[:, 2 * NV :] = slash[...]
    for chip in range(out.shape[0]):
        out[chip, : 2 * NV] = picked


def key_positions(ints, core, chips):
    vpos = ints[VERT : VERT + 1, :] * BLK + (iota((1, HEAD), 1) // NV) * 2 + core
    step = 2 * HEAD // NV
    return jnp.concatenate([vpos + m * step for m in range(chips * NV // HEAD)], axis=1)


def row_positions(recv, rows):
    tail = recv[:, 8:].astype(F32)
    size = 8 * tail.shape[0]
    number = jnp.sum(jnp.where(iota(tail.shape, 1) == 4, tail, 0.0), axis=1, keepdims=True)
    number = jnp.broadcast_to(number, tail.shape).reshape(size, HEAD)[:, :1]
    at = iota((size, 1), 0)
    return (at // 8) * rows + number.astype(jnp.int32) * 2 + at % 2


def half_kernel(ints, recv, mine, out):
    core = ints[CORE : CORE + 1, :1]
    size = out.shape[0]
    rows = 2 * recv.shape[0]
    pos = key_positions(ints, core, mine.shape[0])
    qpos = row_positions(recv, rows)
    q = recv[:, :8].reshape(size, HEAD)
    keys = mine[:, :NV].reshape(-1, HEAD)
    vals = mine[:, NV : 2 * NV].reshape(-1, HEAD)
    lane = iota((rows, HEAD), 1)
    for b in range(size // rows):
        cut = slice(b * rows, (b + 1) * rows)
        s = jnp.where(pos <= qpos[cut], dot_t(q[cut], keys), -jnp.inf)
        top = jnp.maximum(jnp.max(s, axis=1, keepdims=True), LOW)
        p = jnp.exp2((s - top) * FACTOR)
        total = jnp.sum(p, axis=1, keepdims=True)
        out[cut, :HEAD] = jnp.dot(p.astype(BF16), vals, preferred_element_type=F32)
        out[cut, HEAD:] = jnp.where(lane == 0, top, total)


def finish_kernel(ints, recv, mine, other, half, weight_in, out, weight, sem):
    move = pltpu.make_async_copy(weight_in, weight, sem)
    move.start()
    count = recv.shape[0]
    size = 8 * count
    rows = out.shape[1]
    heads = size // rows
    core = ints[CORE : CORE + 1, :1]
    first = core == 0
    pos = key_positions(ints, 1 - core, mine.shape[0])
    qpos = row_positions(recv, rows)

    def by_owner(cut):
        a, b = cut(mine), cut(other)
        return jnp.concatenate([jnp.where(first, a, b), jnp.where(first, b, a)], axis=1)

    base = 2 * NV

    def slash_rows(ref):
        return jnp.where(
            first, ref[:, base : base + 8].astype(F32), ref[:, base + 8 : base + 16].astype(F32)
        )

    def sums_row(ref):
        tail = ref[:, base + 16 :].astype(F32)
        which = iota(tail.shape, 1)
        row = jnp.sum(jnp.where(which == core, tail, 0.0), axis=1, keepdims=True)
        return jnp.broadcast_to(row, tail.shape)

    slash = by_owner(slash_rows).reshape(size, HEAD)
    sums = by_owner(sums_row).reshape(size, HEAD)
    lane = iota((size, HEAD), 1)
    own = lane // 8 == iota((size, HEAD), 0) % 8
    top_b = jnp.sum(jnp.where(own & (lane % 8 < 3), sums, 0.0), axis=1, keepdims=True)
    total_b = jnp.sum(jnp.where(own & (lane % 8 >= 3), sums, 0.0), axis=1, keepdims=True)

    q = recv[:, :8].reshape(size, HEAD)
    keys = other[:, :NV].reshape(-1, HEAD)
    vals = other[:, NV : 2 * NV].reshape(-1, HEAD)
    done = []
    for b in range(heads):
        cut = slice(b * rows, (b + 1) * rows)
        s = jnp.where(pos <= qpos[cut], dot_t(q[cut], keys), -jnp.inf)
        top_a = half[cut, HEAD : HEAD + 1]
        top = jnp.maximum(jnp.max(s, axis=1, keepdims=True), jnp.maximum(top_a, top_b[cut]))
        p = jnp.exp2((s - top) * FACTOR)
        share_a = jnp.exp2((top_a - top) * FACTOR)
        share_b = total_b[cut] * jnp.exp2((top_b[cut] - top) * FACTOR)
        total = jnp.sum(p, axis=1, keepdims=True) + share_a * half[cut, HEAD + 1 : HEAD + 2] + share_b
        o = jnp.dot(p.astype(BF16), vals, preferred_element_type=F32)
        o += share_a * half[cut, :HEAD] + share_b * slash[cut]
        done.append((o / total).astype(BF16))
    attended = jnp.concatenate(done, axis=0)
    row = iota((rows, 1), 0)
    cols = iota((rows, size), 1)
    full = jnp.concatenate(
        [pick(cols == (row // 2) * 8 + h * 2 + row % 2, attended) for h in range(heads)], axis=1
    )
    width = out.shape[2]
    move.wait()
    for j in range(out.shape[0]):
        out[j] = jnp.dot(
            full, weight[:, j * width : (j + 1) * width], preferred_element_type=F32
        ).astype(BF16)


def local(queries, keys, values, vertical, offsets, send_order, out_weight):
    z_n, x_n, c_n, y_n = (lax.axis_size(a) for a in ("z", "x", "c", "y"))
    rows = queries.shape[0]
    n_ctx = z_n * x_n * c_n
    chips = z_n * x_n
    large = pltpu.CompilerParams(vmem_limit_bytes=60 * MIB)
    small = pltpu.CompilerParams(vmem_limit_bytes=16 * MIB)
    place = jnp.stack([lax.axis_index(CTX), lax.axis_index("c")]).astype(jnp.int32)
    held = [pltpu.VMEM(a.shape, a.dtype) for a in (queries, keys, values, send_order)]

    packed, kv = pl.pallas_call(
        pack_kernel,
        out_shape=[
            jax.ShapeDtypeStruct((n_ctx, 16, HEAD), BF16),
            jax.ShapeDtypeStruct((rows, 2 * HEAD), BF16),
        ],
        in_specs=[HBM] * 4,
        out_specs=[VMEM, VMEM],
        scratch_shapes=held + [pltpu.SemaphoreType.DMA((4,))],
        name="pack",
        compiler_params=large,
    )(queries, keys, values, send_order)
    recv = lax.all_to_all(packed, CTX, 0, 0, tiled=True)
    prev = lax.ppermute(kv, CTX, [(i, i + 1) for i in range(n_ctx - 1)])
    slash, ints = pl.pallas_call(
        band_kernel,
        out_shape=[
            jax.ShapeDtypeStruct((chips, 24, HEAD), BF16),
            jax.ShapeDtypeStruct((8, HEAD), jnp.int32),
        ],
        in_specs=[SMEM] + [HBM] * 7,
        out_specs=[VMEM, VMEM],
        scratch_shapes=held
        + [pltpu.VMEM(a.shape, a.dtype) for a in (offsets, vertical, prev)]
        + [pltpu.SemaphoreType.DMA((7,))],
        name="slash",
        compiler_params=large,
    )(place, queries, keys, values, send_order, offsets, vertical, prev)
    parts, ints = pl.pallas_call(
        select_kernel,
        out_shape=[
            jax.ShapeDtypeStruct((chips, 2 * NV + 24, HEAD), BF16),
            jax.ShapeDtypeStruct(ints.shape, jnp.int32),
        ],
        in_specs=[VMEM] * 3,
        out_specs=[VMEM, VMEM],
        name="select",
        compiler_params=small,
    )(ints, recv, slash)
    mine = lax.all_to_all(parts, ("z", "x"), 0, 0, tiled=True)
    other = lax.ppermute(mine, "c", [(0, 1), (1, 0)])
    half = pl.pallas_call(
        half_kernel,
        out_shape=jax.ShapeDtypeStruct((8 * n_ctx, 2 * HEAD), F32),
        in_specs=[VMEM] * 3,
        out_specs=VMEM,
        name="half",
        compiler_params=pltpu.CompilerParams(vmem_limit_bytes=32 * MIB),
        cost_estimate=pl.CostEstimate(flops=300000000, bytes_accessed=2000000, transcendentals=500000),
    )(ints, recv, mine)
    width = out_weight.shape[1] // y_n
    partial = pl.pallas_call(
        finish_kernel,
        out_shape=jax.ShapeDtypeStruct((y_n, rows, width), BF16),
        in_specs=[VMEM] * 5 + [HBM],
        out_specs=VMEM,
        scratch_shapes=[pltpu.VMEM(out_weight.shape, BF16), pltpu.SemaphoreType.DMA],
        name="finish",
        compiler_params=pltpu.CompilerParams(vmem_limit_bytes=50 * MIB),
    )(ints, recv, mine, other, half, out_weight)
    sums = lax.all_to_all(partial, "y", 0, 0, tiled=True)
    return jnp.sum(sums.astype(F32), axis=0).astype(BF16)


def solution(mesh):
    cut = Mesh(mesh.devices.reshape(8, 4, 2, 8), ("z", "x", "c", "y"))
    placed = (
        P(CTX, "y"),
        P(CTX, "y"),
        P(CTX, "y"),
        P("y", None),
        P("y", None),
        P(CTX, None),
        P("y", None),
    )
    return jax.shard_map(
        local, mesh=cut, in_specs=placed, out_specs=P(CTX, "y"), check_vma=False
    )
```

time: 111 us -> 106 us (0.955)
  waiting for transfers between devices: 11.4 us -> 4.61 us
  local copies, waits for them, and re-layouts: 7.47 us -> 2.24 us
  Pallas kernels: 9.28 us -> 12.8 us
  blocking collectives: 58.1 us -> 61.1 us
    all_to_all x1, waiting for transfers between devices: 7.81 us -> 3.28 us  [local(): recv = lax.all_to_all(packed, CTX, 0, 0, tiled=True)]
    pallas_call x1 -> x3, Pallas kernels: 1.75 us -> 5.73 us  [the longest x1 3.89 us: local(): pl.pallas_call(band_kernel, out_shape=[jax.ShapeDtypeStruct((chips, 24, H...]
    all_to_all x1, blocking collectives: 23.5 us -> 26.5 us  [local(): mine = lax.all_to_all(parts, ('z', 'x'), 0, 0, tiled=True)]
    unnamed x10 -> x6, local copies, waits for them, and re-layouts: 3.97 us -> 2.24 us
    ppermute x1, waiting for transfers between devices: 1.8 us -> 0.19 us  [local(): other = lax.ppermute(mine, 'c', [(0, 1), (1, 0)])]
    concatenate x2 -> x0, local copies, waits for them, and re-layouts: 1.4 us -> none  [the longest x1 0.77 us: local(): qkv = jnp.concatenate([queries, keys, values], axis=1)]
    pad x2 -> x0, local copies, waits for them, and re-layouts: 1.35 us -> none  [the longest x1 0.69 us: local(): jnp.pad(offsets, pad)]
  transfers between devices with their start and end apart: 3 -> 3, of which waited for: 3 -> 3; matrix products, arithmetic and copies ran while one was open for 0% -> 1% of each run, Pallas kernels for 0% -> 5%
where the time goes in v4:
time: 106 us
  blocking collectives  61.1 us (58%)
  starting transfers between devices  23.3 us (22%)
  Pallas kernels  12.8 us (12%)
  waiting for transfers between devices  4.61 us (4%)
  local copies, waits for them, and re-layouts  2.24 us (2%)
  other arithmetic  1.46 us (1%)
    all_to_all x1, blocking collectives, local(): sums = lax.all_to_all(partial, 'y', 0, 0, tiled=True)  34.6 us
    all_to_all x1, blocking collectives, local(): mine = lax.all_to_all(parts, ('z', 'x'), 0, 0, tiled=True)  26.5 us
    all_to_all x1, starting transfers between devices, local(): recv = lax.all_to_all(packed, CTX, 0, 0, tiled=True)  14.8 us
    ppermute x1, starting transfers between devices, local(): other = lax.ppermute(mine, 'c', [(0, 1), (1, 0)])  4.94 us
    pallas_call x1, Pallas kernels, local(): pl.pallas_call(finish_kernel, out_shape=jax.ShapeDtypeStruct((y_n, rows,...  4.8 us
    pallas_call x1, Pallas kernels, local(): pl.pallas_call(band_kernel, out_shape=[jax.ShapeDtypeStruct((chips, 24, H...  3.89 us
    ppermute x1, starting transfers between devices, local(): prev = lax.ppermute(kv, CTX, [(i, i + 1) for i in range(n_ctx - 1)])  3.54 us
    all_to_all x1, waiting for transfers between devices, local(): recv = lax.all_to_all(packed, CTX, 0, 0, tiled=True)  3.28 us
  transfers between devices with their start and end apart: 3, of which 3 were waited for; matrix products, arithmetic and copies ran while one was open for 1% of the time, Pallas kernels for 5%

profile of v4, /device:TPU:1, one launch (start us, length us, event | category | flops | bytes accessed | tf_op | source)
XLA Modules:
  0.0 105.6 jit_solution(8863806489952733511)
XLA Ops:
  0.0 2.3 %pack.1 = (bf16[64,16,128]{2,1,0:T(8,128)(2,1)}, bf16[128,256]{1,0:T(8,128)(2,1)}) custom-call(bf16[128,512]{1,0:T(8,128)(2,1)} %q_in.3, bf16[128,128]{1,0:T(8,128)(2,1)} %keys_in.3, bf16[128,128]{1,0:T(8,128)(2,1)} %values_in.3, s32[1,64]{1,0:T(1,128)} %order_in.3), custom_call_target="tpu_custom_call" | custom-call | tf_op jit(solution)/shard_map/pack/pallas_call | solution.py:287
  2.3 14.8 %all-to-all-start = ((bf16[64,16,128]{2,1,0:T(8,128)(2,1)}), bf16[64,16,128]{2,1,0:T(8,128)(2,1)S(1)}, u32[]{:S(2)}, u32[]{:S(2)}) async-start(bf16[64,16,128]{2,1,0:T(8,128)(2,1)} %get-tuple-element.13), calls=%async_computation | async-start | bytes 524288 | tf_op jit(solution)/shard_map/all_to_all | solution.py:299
  17.1 3.5 %collective-permute-start = (bf16[128,256]{1,0:T(8,128)(2,1)}, bf16[128,256]{1,0:T(8,128)(2,1)S(1)}, u32[]{:S(2)}, u32[]{:S(2)}) collective-permute-start(bf16[128,256]{1,0:T(8,128)(2,1)} %get-tuple-element.11), channel_id=1, source_target_pairs={{0,8},{8,16},{16,24},{24,32},{32,40},{40,48},{48,56},{56,64},{64,7... | collective-permute-start | bytes 196616 | tf_op jit(solution)/shard_map/ppermute | solution.py:300
  20.7 0.7 pad_add_fusion.place
  21.4 1.1 %collective-permute-done.prev_in = bf16[128,256]{1,0:T(8,128)(2,1)S(1)} collective-permute-done((bf16[128,256]{1,0:T(8,128)(2,1)}, bf16[128,256]{1,0:T(8,128)(2,1)S(1)}, u32[]{:S(2)}, u32[]{:S(2)}) %collective-permute-start) | collective-permute-done | bytes 65568 | tf_op jit(solution)/shard_map/ppermute | solution.py:300
  22.5 0.0 copy-start.2
  22.5 0.6 copy-done.2
  23.1 3.9 %slash.1 = (bf16[32,24,128]{2,1,0:T(8,128)(2,1)}, s32[8,128]{1,0:T(8,128)}) custom-call(s32[2]{0:T(128)} %pad_add_fusion.place, bf16[128,512]{1,0:T(8,128)(2,1)} %q_in.3, bf16[128,128]{1,0:T(8,128)(2,1)} %keys_in.3, bf16[128,128]{1,0:T(8,128)(2,1)} %values_in.3, s32[1,64]{1,0:T(1,128)} %order_in.3, s32[4,64]{1,0:T(4,128)} %offsets_in.1, s32[1,32]{1,0:T(1,128)} %vert_in.1, ...), custom_call_target="tpu_custom_call" | custom-call | tf_op jit(solution)/shard_map/slash/pallas_call | solution.py:301
  27.0 3.3 %all-to-all-done.recv = bf16[64,16,128]{2,1,0:T(8,128)(2,1)S(1)} async-done(((bf16[64,16,128]{2,1,0:T(8,128)(2,1)}), bf16[64,16,128]{2,1,0:T(8,128)(2,1)S(1)}, u32[]{:S(2)}, u32[]{:S(2)}) %all-to-all-start) | async-done | bytes 262176 | tf_op jit(solution)/shard_map/all_to_all | solution.py:299
  30.3 0.0 copy-start
  30.3 0.9 copy-done
  31.2 0.0 copy-start.1
  31.2 0.7 copy-done.1
  31.9 0.2 select.1
  32.2 26.5 %all_to_all.15.mine = bf16[32,88,128]{2,1,0:T(8,128)(2,1)S(1)} all-to-all(bf16[32,88,128]{2,1,0:T(8,128)(2,1)S(1)} %get-tuple-element.16), channel_id=1, replica_groups=mesh['z'=8,'x'=4,'c'=2,'y'=8] {'z','x'}, dimensions={0} | all-to-all | bytes 1441792 | tf_op jit(solution)/shard_map/all_to_all | solution.py:326
  58.7 4.9 %collective-permute-start.1 = (bf16[32,88,128]{2,1,0:T(8,128)(2,1)S(1)}, bf16[32,88,128]{2,1,0:T(8,128)(2,1)S(1)}, u32[]{:S(2)}, u32[]{:S(2)}) collective-permute-start(bf16[32,88,128]{2,1,0:T(8,128)(2,1)S(1)} %all_to_all.15.mine), channel_id=1, source_target_pairs={{0,8},{8,0},{1,9},{9,1},{2,10},{10,2},{3,11},{11,3},{4,12},{12,4},... | collective-permute-start | bytes 2162696 | tf_op jit(solution)/shard_map/ppermute | solution.py:327
  63.6 1.6 %half.1 = f32[512,256]{1,0:T(8,128)S(1)} custom-call(s32[8,128]{1,0:T(8,128)S(1)} %get-tuple-element.15.ints, bf16[64,16,128]{2,1,0:T(8,128)(2,1)S(1)} %all-to-all-done.recv, bf16[32,88,128]{2,1,0:T(8,128)(2,1)S(1)} %all_to_all.15.mine), custom_call_target="tpu_custom_call" | custom-call | flops 300000000 | bytes 2000000 | tf_op jit(solution)/shard_map/half/pallas_call | solution.py:328
  65.2 0.2 collective-permute-done.1.other
  65.4 4.8 %finish.1 = bf16[8,128,512]{2,1,0:T(8,128)(2,1)S(1)} custom-call(s32[8,128]{1,0:T(8,128)S(1)} %get-tuple-element.15.ints, bf16[64,16,128]{2,1,0:T(8,128)(2,1)S(1)} %all-to-all-done.recv, bf16[32,88,128]{2,1,0:T(8,128)(2,1)S(1)} %all_to_all.15.mine, bf16[32,88,128]{2,1,0:T(8,128)(2,1)S(1)} %collective-permute-done.1.other, f32[512,256]{1,0:T(8,128)S(1)} %half.1, ...), custom_call_target="tpu_custom_call" | custom-call | tf_op jit(solution)/shard_map/finish/pallas_call | solution.py:338
  70.2 34.6 %all_to_all.16 = bf16[8,128,512]{2,1,0:T(8,128)(2,1)S(1)} all-to-all(bf16[8,128,512]{2,1,0:T(8,128)(2,1)S(1)} %finish.1), channel_id=1, replica_groups=mesh['z'=8,'x'=4,'c'=2,'y'=8] {'y'}, dimensions={0} | all-to-all | bytes 2097152 | tf_op jit(solution)/shard_map/all_to_all | solution.py:347
  104.8 0.8 reduce_sum.12
Async XLA Ops:
  2.3 28.0 %all-to-all-start = ((bf16[64,16,128]{2,1,0:T(8,128)(2,1)}), bf16[64,16,128]{2,1,0:T(8,128)(2,1)S(1)}, u32[]{:S(2)}, u32[]{:S(2)}) async-start(bf16[64,16,128]{2,1,0:T(8,128)(2,1)} %get-tuple-element.13), calls=%async_computation | async-start | bytes 524288 | tf_op jit(solution)/shard_map/all_to_all | solution.py:299
  17.1 5.4 %collective-permute-start = (bf16[128,256]{1,0:T(8,128)(2,1)}, bf16[128,256]{1,0:T(8,128)(2,1)S(1)}, u32[]{:S(2)}, u32[]{:S(2)}) collective-permute-start(bf16[128,256]{1,0:T(8,128)(2,1)} %get-tuple-element.11), channel_id=1, source_target_pairs={{0,8},{8,16},{16,24},{24,32},{32,40},{40,48},{48,56},{56,64},{64,7... | collective-permute-start | bytes 196616 | tf_op jit(solution)/shard_map/ppermute | solution.py:300
  22.5 0.6 copy-start.2
  30.3 0.9 copy-start
  31.2 0.7 copy-start.1
  58.7 6.7 %collective-permute-start.1 = (bf16[32,88,128]{2,1,0:T(8,128)(2,1)S(1)}, bf16[32,88,128]{2,1,0:T(8,128)(2,1)S(1)}, u32[]{:S(2)}, u32[]{:S(2)}) collective-permute-start(bf16[32,88,128]{2,1,0:T(8,128)(2,1)S(1)} %all_to_all.15.mine), channel_id=1, source_target_pairs={{0,8},{8,0},{1,9},{9,1},{2,10},{10,2},{3,11},{11,3},{4,12},{12,4},... | collective-permute-start | bytes 2162696 | tf_op jit(solution)/shard_map/ppermute | solution.py:327

commit v5 on v4

--- a/solution.py
+++ b/solution.py
@@ -11,13 +11,13 @@
 BLK = 64
 NV = 32
 CTX = ("z", "x", "c")
+Y = ("yh", "yl")
 VMEM = pl.BlockSpec(memory_space=pltpu.VMEM)
 HBM = pl.BlockSpec(memory_space=pltpu.HBM)
 F32 = jnp.float32
 BF16 = jnp.bfloat16
 LOW = -1e30
 FACTOR = math.log2(math.e) / math.sqrt(HEAD)
-SMEM = pl.BlockSpec(memory_space=pltpu.SMEM)
 MIB = 1024 * 1024
 VERT, WANT, CORE = 0, 1, 2
 
@@ -66,8 +66,23 @@
         move.wait()
 
 
-def pack_kernel(q_in, keys_in, values_in, order_in, out, kv, q, keys, values, order, sems):
+def columns(ref, j, parity):
+    width = ref.shape[1] // 8
+    start = pl.multiple_of((2 * j + parity) * width, width)
+    return ref.at[:, pl.ds(start, width)]
+
+
+def pack_kernel(
+    q_in, keys_in, values_in, order_in, weight_in, out, kv, sent, q, keys, values, order, sems, wsems
+):
     load([(q_in, q), (keys_in, keys), (values_in, values), (order_in, order)], sems)
+    parity = lax.axis_index("yl")
+    moves = [
+        pltpu.make_async_copy(columns(weight_in, j, 1 - parity), sent.at[j], wsems.at[j])
+        for j in range(sent.shape[0])
+    ]
+    for move in moves:
+        move.start()
     rows = q.shape[0]
     heads = q.shape[1] // HEAD
     count = rows // 2
@@ -91,6 +106,8 @@
         bits(iota((8 * count, count), 1) == owner), number, preferred_element_type=F32
     )
     out[:, 8:] = (kv_rows + numbers).astype(BF16).reshape(count, 8, HEAD)
+    for move in moves:
+        move.wait()
 
 
 def split3(x):
@@ -100,7 +117,7 @@
 
 
 def band_kernel(
-    place, q_in, keys_in, values_in, order_in, offsets_in, vert_in, prev_in, out, ints,
+    q_in, keys_in, values_in, order_in, offsets_in, vert_in, prev_in, out, ints,
     q, keys, values, order, offsets, vertical, prev, sems,
 ):
     load(
@@ -112,7 +129,7 @@
     count = rows // 2
     chips = out.shape[0]
     band = 2 * rows
-    ctx, core = place[0], place[1]
+    ctx, core = lax.axis_index(CTX), lax.axis_index("c")
     spread = bits(iota((NV, HEAD), 0) == iota((NV, HEAD), 1) % NV)
     vert = jnp.dot(
         vertical[...].astype(F32).astype(BF16), spread, preferred_element_type=F32
@@ -208,12 +225,10 @@
         out[cut, HEAD:] = jnp.where(lane == 0, top, total)
 
 
-def finish_kernel(ints, recv, mine, other, half, weight_in, out, weight, sem):
-    move = pltpu.make_async_copy(weight_in, weight, sem)
-    move.start()
+def finish_kernel(ints, recv, mine, other, half, out):
     count = recv.shape[0]
     size = 8 * count
-    rows = out.shape[1]
+    rows = out.shape[0]
     heads = size // rows
     core = ints[CORE : CORE + 1, :1]
     first = core == 0
@@ -263,55 +278,75 @@
     attended = jnp.concatenate(done, axis=0)
     row = iota((rows, 1), 0)
     cols = iota((rows, size), 1)
-    full = jnp.concatenate(
-        [pick(cols == (row // 2) * 8 + h * 2 + row % 2, attended) for h in range(heads)], axis=1
-    )
-    width = out.shape[2]
-    move.wait()
+    for h in range(heads):
+        rows_h = pick(cols == (row // 2) * 8 + h * 2 + row % 2, attended)
+        out[:, h * HEAD : (h + 1) * HEAD] = rows_h
+
+
+def own_kernel(full, weight_in, theirs_in, out, theirs, weight, sems):
+    n = out.shape[0]
+    parity = lax.axis_index("yl")
+    moves = [
+        pltpu.make_async_copy(columns(weight_in, j, parity), weight.at[j], sems.at[j])
+        for j in range(n)
+    ]
+    late = pltpu.make_async_copy(theirs_in, theirs, sems.at[n])
+    for move in moves:
+        move.start()
+    late.start()
+    for j in range(n):
+        moves[j].wait()
+        out[j] = jnp.dot(full[...], weight[j], preferred_element_type=F32)
+    late.wait()
+
+
+def both_kernel(own, full, weight, out):
     for j in range(out.shape[0]):
-        out[j] = jnp.dot(
-            full, weight[:, j * width : (j + 1) * width], preferred_element_type=F32
-        ).astype(BF16)
+        part = own[j] + jnp.dot(full[...], weight[j], preferred_element_type=F32)
+        out[j] = part.astype(BF16)
 
 
 def local(queries, keys, values, vertical, offsets, send_order, out_weight):
-    z_n, x_n, c_n, y_n = (lax.axis_size(a) for a in ("z", "x", "c", "y"))
+    z_n, x_n, c_n, pairs = (lax.axis_size(a) for a in ("z", "x", "c", "yh"))
     rows = queries.shape[0]
     n_ctx = z_n * x_n * c_n
     chips = z_n * x_n
     large = pltpu.CompilerParams(vmem_limit_bytes=60 * MIB)
     small = pltpu.CompilerParams(vmem_limit_bytes=16 * MIB)
-    place = jnp.stack([lax.axis_index(CTX), lax.axis_index("c")]).astype(jnp.int32)
+    width = out_weight.shape[1] // (2 * pairs)
+    quarter = (pairs, out_weight.shape[0], width)
     held = [pltpu.VMEM(a.shape, a.dtype) for a in (queries, keys, values, send_order)]
 
-    packed, kv = pl.pallas_call(
+    packed, kv, sent = pl.pallas_call(
         pack_kernel,
         out_shape=[
             jax.ShapeDtypeStruct((n_ctx, 16, HEAD), BF16),
             jax.ShapeDtypeStruct((rows, 2 * HEAD), BF16),
+            jax.ShapeDtypeStruct(quarter, BF16),
         ],
-        in_specs=[HBM] * 4,
-        out_specs=[VMEM, VMEM],
-        scratch_shapes=held + [pltpu.SemaphoreType.DMA((4,))],
+        in_specs=[HBM] * 5,
+        out_specs=[VMEM, VMEM, HBM],
+        scratch_shapes=held + [pltpu.SemaphoreType.DMA((4,)), pltpu.SemaphoreType.DMA((pairs,))],
         name="pack",
         compiler_params=large,
-    )(queries, keys, values, send_order)
+    )(queries, keys, values, send_order, out_weight)
     recv = lax.all_to_all(packed, CTX, 0, 0, tiled=True)
     prev = lax.ppermute(kv, CTX, [(i, i + 1) for i in range(n_ctx - 1)])
+    theirs = lax.ppermute(sent, "yl", [(0, 1), (1, 0)])
     slash, ints = pl.pallas_call(
         band_kernel,
         out_shape=[
             jax.ShapeDtypeStruct((chips, 24, HEAD), BF16),
             jax.ShapeDtypeStruct((8, HEAD), jnp.int32),
         ],
-        in_specs=[SMEM] + [HBM] * 7,
+        in_specs=[HBM] * 7,
         out_specs=[VMEM, VMEM],
         scratch_shapes=held
         + [pltpu.VMEM(a.shape, a.dtype) for a in (offsets, vertical, prev)]
         + [pltpu.SemaphoreType.DMA((7,))],
         name="slash",
         compiler_params=large,
-    )(place, queries, keys, values, send_order, offsets, vertical, prev)
+    )(queries, keys, values, send_order, offsets, vertical, prev)
     parts, ints = pl.pallas_call(
         select_kernel,
         out_shape=[
@@ -334,31 +369,51 @@
         compiler_params=pltpu.CompilerParams(vmem_limit_bytes=32 * MIB),
         cost_estimate=pl.CostEstimate(flops=300000000, bytes_accessed=2000000, transcendentals=500000),
     )(ints, recv, mine)
-    width = out_weight.shape[1] // y_n
+    full = pl.pallas_call(
+        finish_kernel,
+        out_shape=jax.ShapeDtypeStruct(queries.shape, BF16),
+        in_specs=[VMEM] * 5,
+        out_specs=VMEM,
+        name="finish",
+        compiler_params=pltpu.CompilerParams(vmem_limit_bytes=32 * MIB),
+    )(ints, recv, mine, other, half)
+    theirs_full = lax.ppermute(full, "yl", [(0, 1), (1, 0)])
+    own, weight = pl.pallas_call(
+        own_kernel,
+        out_shape=[
+            jax.ShapeDtypeStruct((pairs, rows, width), F32),
+            jax.ShapeDtypeStruct(quarter, BF16),
+        ],
+        in_specs=[VMEM, HBM, HBM],
+        out_specs=[VMEM, VMEM],
+        scratch_shapes=[pltpu.VMEM(quarter, BF16), pltpu.SemaphoreType.DMA((pairs + 1,))],
+        name="project_own",
+        compiler_params=pltpu.CompilerParams(vmem_limit_bytes=48 * MIB),
+        cost_estimate=pl.CostEstimate(flops=300000000, bytes_accessed=8000000, transcendentals=0),
+    )(full, out_weight, theirs)
     partial = pl.pallas_call(
-        finish_kernel,
-        out_shape=jax.ShapeDtypeStruct((y_n, rows, width), BF16),
-        in_specs=[VMEM] * 5 + [HBM],
+        both_kernel,
+        out_shape=jax.ShapeDtypeStruct((pairs, rows, width), BF16),
+        in_specs=[VMEM] * 3,
         out_specs=VMEM,
-        scratch_shapes=[pltpu.VMEM(out_weight.shape, BF16), pltpu.SemaphoreType.DMA],
-        name="finish",
-        compiler_params=pltpu.CompilerParams(vmem_limit_bytes=50 * MIB),
-    )(ints, recv, mine, other, half, out_weight)
-    sums = lax.all_to_all(partial, "y", 0, 0, tiled=True)
+        name="project_both",
+        compiler_params=pltpu.CompilerParams(vmem_limit_bytes=32 * MIB),
+    )(own, theirs_full, weight)
+    sums = lax.all_to_all(partial, "yh", 0, 0, tiled=True)
     return jnp.sum(sums.astype(F32), axis=0).astype(BF16)
 
 
 def solution(mesh):
-    cut = Mesh(mesh.devices.reshape(8, 4, 2, 8), ("z", "x", "c", "y"))
+    cut = Mesh(mesh.devices.reshape(8, 4, 2, 4, 2), CTX + Y)
     placed = (
-        P(CTX, "y"),
-        P(CTX, "y"),
-        P(CTX, "y"),
-        P("y", None),
-        P("y", None),
+        P(CTX, Y),
+        P(CTX, Y),
+        P(CTX, Y),
+        P(Y, None),
+        P(Y, None),
         P(CTX, None),
-        P("y", None),
+        P(Y, None),
     )
     return jax.shard_map(
-        local, mesh=cut, in_specs=placed, out_specs=P(CTX, "y"), check_vma=False
-    )
+        local, mesh=cut, in_specs=placed, out_specs=P(CTX, Y), check_vma=False
+    )

time: 106 us -> 178 us (1.68); the launches traced: 106 us -> 175 us
  Pallas kernels: 12.8 us -> 76.9 us
  blocking collectives: 61.1 us -> 19.7 us
  waiting for transfers between devices: 4.61 us -> 39 us
  starting transfers between devices: 23.3 us -> 36.5 us
    pallas_call x1, Pallas kernels: 2.28 us -> 66.3 us  [local(): pl.pallas_call(pack_kernel, out_shape=[jax.ShapeDtypeStruct((n_ctx, 16, H...]
    all_to_all x2 -> x1, blocking collectives: 61.1 us -> 19.7 us  [local(): sums = lax.all_to_all(partial, 'yh', 0, 0, tiled=True)]
    ppermute x0 -> x2, waiting for transfers between devices: none -> 16.9 us  [the longest x1 16.2 us: local(): theirs = lax.ppermute(sent, 'yl', [(0, 1), (1, 0)])]
    all_to_all x0 -> x1, waiting for transfers between devices: none -> 16.1 us  [local(): mine = lax.all_to_all(parts, ('z', 'x'), 0, 0, tiled=True)]
    all_to_all x0 -> x1, starting transfers between devices: none -> 6.73 us  [local(): mine = lax.all_to_all(parts, ('z', 'x'), 0, 0, tiled=True)]
    ppermute x0 -> x2, starting transfers between devices: none -> 6.41 us  [the longest x1 3.21 us: local(): theirs_full = lax.ppermute(full, 'yl', [(0, 1), (1, 0)])]
    pallas_call x1 -> x3, Pallas kernels: 4.8 us -> 4.67 us  [the longest x1 2.21 us: local(): pl.pallas_call(finish_kernel, out_shape=jax.ShapeDtypeStruct(queries.shap...]
  transfers between devices with their start and end apart: 3 -> 6, of which waited for: 3 -> 6; matrix products, arithmetic and copies ran while one was open for 1% -> 0% of each run, Pallas kernels for 5% -> 5%
where the time goes in v5:
time: 178 us; the launch traced here: 175 us
  Pallas kernels  76.9 us (43%)
  waiting for transfers between devices  39 us (22%)
  starting transfers between devices  36.5 us (21%)
  blocking collectives  19.7 us (11%)
  local copies, waits for them, and re-layouts  2.23 us (1%)
    pallas_call x1, Pallas kernels, local(): pl.pallas_call(pack_kernel, out_shape=[jax.ShapeDtypeStruct((n_ctx, 16, H...  66.3 us
    all_to_all x1, blocking collectives, local(): sums = lax.all_to_all(partial, 'yh', 0, 0, tiled=True)  19.7 us
    ppermute x1, waiting for transfers between devices, local(): theirs = lax.ppermute(sent, 'yl', [(0, 1), (1, 0)])  16.2 us
    all_to_all x1, waiting for transfers between devices, local(): mine = lax.all_to_all(parts, ('z', 'x'), 0, 0, tiled=True)  16.1 us
    all_to_all x1, starting transfers between devices, local(): recv = lax.all_to_all(packed, CTX, 0, 0, tiled=True)  14.8 us
    all_to_all x1, starting transfers between devices, local(): mine = lax.all_to_all(parts, ('z', 'x'), 0, 0, tiled=True)  6.73 us
    ppermute x1, starting transfers between devices, local(): other = lax.ppermute(mine, 'c', [(0, 1), (1, 0)])  4.93 us
    all_to_all x1, waiting for transfers between devices, local(): recv = lax.all_to_all(packed, CTX, 0, 0, tiled=True)  3.94 us
  transfers between devices with their start and end apart: 6, of which 6 were waited for; matrix products, arithmetic and copies ran while one was open for 0% of the time, Pallas kernels for 5%

profile of v5, /device:TPU:1, one launch (start us, length us, event | category | flops | bytes accessed | tf_op | source)
XLA Modules:
  0.0 175.1 jit_solution(8634959950959614332)
XLA Ops:
  0.0 66.3 %pack.1 = (bf16[64,16,128]{2,1,0:T(8,128)(2,1)}, bf16[128,256]{1,0:T(8,128)(2,1)}, bf16[4,512,512]{2,1,0:T(8,128)(2,1)}) custom-call(bf16[128,512]{1,0:T(8,128)(2,1)} %q_in.3, bf16[128,128]{1,0:T(8,128)(2,1)} %keys_in.3, bf16[128,128]{1,0:T(8,128)(2,1)} %values_in.3, s32[1,64]{1,0:T(1,128)} %order_in.3, bf16[512,4096]{1,0:T(8,128)(2,1)} %weight_in.3), custom_call_target="tpu_custom_call" | custom-call | tf_op jit(solution)/shard_map/pack/pallas_call | solution.py:320
  66.3 14.8 %all-to-all-start = ((bf16[64,16,128]{2,1,0:T(8,128)(2,1)}), bf16[64,16,128]{2,1,0:T(8,128)(2,1)S(1)}, u32[]{:S(2)}, u32[]{:S(2)}) async-start(bf16[64,16,128]{2,1,0:T(8,128)(2,1)} %get-tuple-element.16), calls=%async_computation | async-start | bytes 524288 | tf_op jit(solution)/shard_map/all_to_all | solution.py:333
  81.2 3.5 %collective-permute-start = (bf16[128,256]{1,0:T(8,128)(2,1)}, bf16[128,256]{1,0:T(8,128)(2,1)S(1)}, u32[]{:S(2)}, u32[]{:S(2)}) collective-permute-start(bf16[128,256]{1,0:T(8,128)(2,1)} %get-tuple-element.14), channel_id=1, source_target_pairs={{0,8},{8,16},{16,24},{24,32},{32,40},{40,48},{48,56},{56,64},{64,7... | collective-permute-start | bytes 196616 | tf_op jit(solution)/shard_map/ppermute | solution.py:334
  84.7 1.8 %collective-permute-done.prev_in = bf16[128,256]{1,0:T(8,128)(2,1)S(1)} collective-permute-done((bf16[128,256]{1,0:T(8,128)(2,1)}, bf16[128,256]{1,0:T(8,128)(2,1)S(1)}, u32[]{:S(2)}, u32[]{:S(2)}) %collective-permute-start) | collective-permute-done | bytes 65568 | tf_op jit(solution)/shard_map/ppermute | solution.py:334
  86.5 0.0 copy-start.2
  86.5 0.6 copy-done.2
  87.2 3.2 %slash.1 = (bf16[32,24,128]{2,1,0:T(8,128)(2,1)}, s32[8,128]{1,0:T(8,128)}) custom-call(bf16[128,512]{1,0:T(8,128)(2,1)} %q_in.3, bf16[128,128]{1,0:T(8,128)(2,1)} %keys_in.3, bf16[128,128]{1,0:T(8,128)(2,1)} %values_in.3, s32[1,64]{1,0:T(1,128)} %order_in.3, s32[4,64]{1,0:T(4,128)} %offsets_in.1, s32[1,32]{1,0:T(1,128)} %vert_in.1, bf16[128,256]{1,0:T(8,128)(2,1)} %copy-done.2), custom_call_target="tpu_custom_call" | custom-call | tf_op jit(solution)/shard_map/slash/pallas_call | solution.py:336
  90.4 3.9 %all-to-all-done.recv = bf16[64,16,128]{2,1,0:T(8,128)(2,1)S(1)} async-done(((bf16[64,16,128]{2,1,0:T(8,128)(2,1)}), bf16[64,16,128]{2,1,0:T(8,128)(2,1)S(1)}, u32[]{:S(2)}, u32[]{:S(2)}) %all-to-all-start) | async-done | bytes 262176 | tf_op jit(solution)/shard_map/all_to_all | solution.py:333
  94.4 0.0 copy-start
  94.4 0.9 copy-done
  95.3 0.0 copy-start.1
  95.3 0.7 copy-done.1
  96.0 1.1 select.1
  97.1 6.7 %all-to-all-start.1 = ((bf16[32,88,128]{2,1,0:T(8,128)(2,1)}), bf16[32,88,128]{2,1,0:T(8,128)(2,1)S(1)}, u32[]{:S(2)}, u32[]{:S(2)}) async-start(bf16[32,88,128]{2,1,0:T(8,128)(2,1)} %get-tuple-element.19), calls=%async_computation.1 | async-start | bytes 1441792 | tf_op jit(solution)/shard_map/all_to_all | solution.py:361
  103.8 3.2 %collective-permute-start.2 = (bf16[4,512,512]{2,1,0:T(8,128)(2,1)}, bf16[4,512,512]{2,1,0:T(8,128)(2,1)S(1)}, u32[]{:S(2)}, u32[]{:S(2)}) collective-permute-start(bf16[4,512,512]{2,1,0:T(8,128)(2,1)} %get-tuple-element.20), channel_id=1, source_target_pairs={{0,1},{1,0},{2,3},{3,2},{4,5},{5,4},{6,7},{7,6},{8,9},{9,8},{10,11... | collective-permute-start | bytes 6291464 | tf_op jit(solution)/shard_map/ppermute | solution.py:335
  107.0 16.1 %all-to-all-done.1.mine = bf16[32,88,128]{2,1,0:T(8,128)(2,1)S(1)} async-done(((bf16[32,88,128]{2,1,0:T(8,128)(2,1)}), bf16[32,88,128]{2,1,0:T(8,128)(2,1)S(1)}, u32[]{:S(2)}, u32[]{:S(2)}) %all-to-all-start.1) | async-done | bytes 720928 | tf_op jit(solution)/shard_map/all_to_all | solution.py:361
  123.1 4.9 %collective-permute-start.1 = (bf16[32,88,128]{2,1,0:T(8,128)(2,1)S(1)}, bf16[32,88,128]{2,1,0:T(8,128)(2,1)S(1)}, u32[]{:S(2)}, u32[]{:S(2)}) collective-permute-start(bf16[32,88,128]{2,1,0:T(8,128)(2,1)S(1)} %all-to-all-done.1.mine), channel_id=1, source_target_pairs={{0,8},{8,0},{1,9},{9,1},{2,10},{10,2},{3,11},{11,3},{4,12},{12,4},... | collective-permute-start | bytes 2162696 | tf_op jit(solution)/shard_map/ppermute | solution.py:362
  128.1 1.6 half.1
  129.7 0.2 collective-permute-done.1.other
  129.9 2.2 %finish.1.full = bf16[128,512]{1,0:T(8,128)(2,1)S(1)} custom-call(s32[8,128]{1,0:T(8,128)S(1)} %get-tuple-element.18.ints, bf16[64,16,128]{2,1,0:T(8,128)(2,1)S(1)} %all-to-all-done.recv, bf16[32,88,128]{2,1,0:T(8,128)(2,1)S(1)} %all-to-all-done.1.mine, bf16[32,88,128]{2,1,0:T(8,128)(2,1)S(1)} %collective-permute-done.1.other, f32[512,256]{1,0:T(8,128)S(1)} %half.1), custom_call_target="tpu_custom_call" | custom-call | tf_op jit(solution)/shard_map/finish/pallas_call | solution.py:372
  132.1 3.2 %collective-permute-start.3 = (bf16[128,512]{1,0:T(8,128)(2,1)S(1)}, bf16[128,512]{1,0:T(8,128)(2,1)S(1)}, u32[]{:S(2)}, u32[]{:S(2)}) collective-permute-start(bf16[128,512]{1,0:T(8,128)(2,1)S(1)} %finish.1.full), channel_id=1, source_target_pairs={{0,1},{1,0},{2,3},{3,2},{4,5},{5,4},{6,7},{7,6},{8,9},{9,8},{10,11... | collective-permute-start | bytes 393224 | tf_op jit(solution)/shard_map/ppermute | solution.py:380
  135.3 16.2 %collective-permute-done.2.theirs_in = bf16[4,512,512]{2,1,0:T(8,128)(2,1)S(1)} collective-permute-done((bf16[4,512,512]{2,1,0:T(8,128)(2,1)}, bf16[4,512,512]{2,1,0:T(8,128)(2,1)S(1)}, u32[]{:S(2)}, u32[]{:S(2)}) %collective-permute-start.2) | collective-permute-done | bytes 2097184 | tf_op jit(solution)/shard_map/ppermute | solution.py:335
  151.5 2.0 %project_own.1 = (f32[4,128,512]{2,1,0:T(8,128)S(1)}, bf16[4,512,512]{2,1,0:T(8,128)(2,1)S(1)}) custom-call(bf16[128,512]{1,0:T(8,128)(2,1)S(1)} %finish.1.full, bf16[512,4096]{1,0:T(8,128)(2,1)} %weight_in.3, bf16[4,512,512]{2,1,0:T(8,128)(2,1)S(1)} %collective-permute-done.2.theirs_in), custom_call_target="tpu_custom_call" | custom-call | flops 300000000 | bytes 8000000 | tf_op jit(solution)/shard_map/project_own/pallas_call | solution.py:381
  153.5 0.8 collective-permute-done.3.full
  154.3 0.4 project_both.1
  154.7 19.7 %all_to_all.15 = bf16[4,128,512]{2,1,0:T(8,128)(2,1)S(1)} all-to-all(bf16[4,128,512]{2,1,0:T(8,128)(2,1)S(1)} %project_both.1), channel_id=1, replica_groups=mesh['z'=8,'x'=4,'c'=2,'yh'=4,'yl'=2] {'yh'}, dimensions={0} | all-to-all | bytes 1048576 | tf_op jit(solution)/shard_map/all_to_all | solution.py:402
  174.4 0.7 reduce_sum.12
Async XLA Ops:
  66.3 28.0 %all-to-all-start = ((bf16[64,16,128]{2,1,0:T(8,128)(2,1)}), bf16[64,16,128]{2,1,0:T(8,128)(2,1)S(1)}, u32[]{:S(2)}, u32[]{:S(2)}) async-start(bf16[64,16,128]{2,1,0:T(8,128)(2,1)} %get-tuple-element.16), calls=%async_computation | async-start | bytes 524288 | tf_op jit(solution)/shard_map/all_to_all | solution.py:333
  81.2 5.4 %collective-permute-start = (bf16[128,256]{1,0:T(8,128)(2,1)}, bf16[128,256]{1,0:T(8,128)(2,1)S(1)}, u32[]{:S(2)}, u32[]{:S(2)}) collective-permute-start(bf16[128,256]{1,0:T(8,128)(2,1)} %get-tuple-element.14), channel_id=1, source_target_pairs={{0,8},{8,16},{16,24},{24,32},{32,40},{40,48},{48,56},{56,64},{64,7... | collective-permute-start | bytes 196616 | tf_op jit(solution)/shard_map/ppermute | solution.py:334
  86.5 0.6 copy-start.2
  94.4 0.9 copy-start
  95.3 0.7 copy-start.1
  97.1 26.1 %all-to-all-start.1 = ((bf16[32,88,128]{2,1,0:T(8,128)(2,1)}), bf16[32,88,128]{2,1,0:T(8,128)(2,1)S(1)}, u32[]{:S(2)}, u32[]{:S(2)}) async-start(bf16[32,88,128]{2,1,0:T(8,128)(2,1)} %get-tuple-element.19), calls=%async_computation.1 | async-start | bytes 1441792 | tf_op jit(solution)/shard_map/all_to_all | solution.py:361
  103.8 47.7 %collective-permute-start.2 = (bf16[4,512,512]{2,1,0:T(8,128)(2,1)}, bf16[4,512,512]{2,1,0:T(8,128)(2,1)S(1)}, u32[]{:S(2)}, u32[]{:S(2)}) collective-permute-start(bf16[4,512,512]{2,1,0:T(8,128)(2,1)} %get-tuple-element.20), channel_id=1, source_target_pairs={{0,1},{1,0},{2,3},{3,2},{4,5},{5,4},{6,7},{7,6},{8,9},{9,8},{10,11... | collective-permute-start | bytes 6291464 | tf_op jit(solution)/shard_map/ppermute | solution.py:335
  123.1 6.7 %collective-permute-start.1 = (bf16[32,88,128]{2,1,0:T(8,128)(2,1)S(1)}, bf16[32,88,128]{2,1,0:T(8,128)(2,1)S(1)}, u32[]{:S(2)}, u32[]{:S(2)}) collective-permute-start(bf16[32,88,128]{2,1,0:T(8,128)(2,1)S(1)} %all-to-all-done.1.mine), channel_id=1, source_target_pairs={{0,8},{8,0},{1,9},{9,1},{2,10},{10,2},{3,11},{11,3},{4,12},{12,4},... | collective-permute-start | bytes 2162696 | tf_op jit(solution)/shard_map/ppermute | solution.py:362
  132.1 22.2 %collective-permute-start.3 = (bf16[128,512]{1,0:T(8,128)(2,1)S(1)}, bf16[128,512]{1,0:T(8,128)(2,1)S(1)}, u32[]{:S(2)}, u32[]{:S(2)}) collective-permute-start(bf16[128,512]{1,0:T(8,128)(2,1)S(1)} %finish.1.full), channel_id=1, source_target_pairs={{0,1},{1,0},{2,3},{3,2},{4,5},{5,4},{6,7},{7,6},{8,9},{9,8},{10,11... | collective-permute-start | bytes 393224 | tf_op jit(solution)/shard_map/ppermute | solution.py:380

commit v6 on v5

--- a/solution.py
+++ b/solution.py
@@ -75,14 +75,17 @@
 def pack_kernel(
     q_in, keys_in, values_in, order_in, weight_in, out, kv, sent, q, keys, values, order, sems, wsems
 ):
-    load([(q_in, q), (keys_in, keys), (values_in, values), (order_in, order)], sems)
-    parity = lax.axis_index("yl")
+    parity, core = lax.axis_index("yl"), lax.axis_index("c")
+    share = sent.shape[0]
     moves = [
-        pltpu.make_async_copy(columns(weight_in, j, 1 - parity), sent.at[j], wsems.at[j])
-        for j in range(sent.shape[0])
+        pltpu.make_async_copy(
+            columns(weight_in, core * share + j, 1 - parity), sent.at[j], wsems.at[j]
+        )
+        for j in range(share)
     ]
     for move in moves:
         move.start()
+    load([(q_in, q), (keys_in, keys), (values_in, values), (order_in, order)], sems)
     rows = q.shape[0]
     heads = q.shape[1] // HEAD
     count = rows // 2
@@ -283,27 +286,26 @@
         out[:, h * HEAD : (h + 1) * HEAD] = rows_h
 
 
-def own_kernel(full, weight_in, theirs_in, out, theirs, weight, sems):
-    n = out.shape[0]
+def own_kernel(full, weight_in, out, weight, sems):
     parity = lax.axis_index("yl")
     moves = [
         pltpu.make_async_copy(columns(weight_in, j, parity), weight.at[j], sems.at[j])
-        for j in range(n)
+        for j in range(out.shape[0])
     ]
-    late = pltpu.make_async_copy(theirs_in, theirs, sems.at[n])
     for move in moves:
         move.start()
-    late.start()
-    for j in range(n):
-        moves[j].wait()
+    for j, move in enumerate(moves):
+        move.wait()
         out[j] = jnp.dot(full[...], weight[j], preferred_element_type=F32)
-    late.wait()
-
-
-def both_kernel(own, full, weight, out):
-    for j in range(out.shape[0]):
-        part = own[j] + jnp.dot(full[...], weight[j], preferred_element_type=F32)
-        out[j] = part.astype(BF16)
+
+
+def both_kernel(own, full, near, far, out):
+    core = lax.axis_index("c")
+    share = near.shape[0]
+    for weight, first in ((near, core * share), (far, (1 - core) * share)):
+        for i in range(share):
+            part = own[first + i] + jnp.dot(full[...], weight[i], preferred_element_type=F32)
+            out[first + i] = part.astype(BF16)
 
 
 def local(queries, keys, values, vertical, offsets, send_order, out_weight):
@@ -314,7 +316,7 @@
     large = pltpu.CompilerParams(vmem_limit_bytes=60 * MIB)
     small = pltpu.CompilerParams(vmem_limit_bytes=16 * MIB)
     width = out_weight.shape[1] // (2 * pairs)
-    quarter = (pairs, out_weight.shape[0], width)
+    columns_half = (pairs // c_n, out_weight.shape[0], width)
     held = [pltpu.VMEM(a.shape, a.dtype) for a in (queries, keys, values, send_order)]
 
     packed, kv, sent = pl.pallas_call(
@@ -322,17 +324,18 @@
         out_shape=[
             jax.ShapeDtypeStruct((n_ctx, 16, HEAD), BF16),
             jax.ShapeDtypeStruct((rows, 2 * HEAD), BF16),
-            jax.ShapeDtypeStruct(quarter, BF16),
+            jax.ShapeDtypeStruct(columns_half, BF16),
         ],
         in_specs=[HBM] * 5,
-        out_specs=[VMEM, VMEM, HBM],
-        scratch_shapes=held + [pltpu.SemaphoreType.DMA((4,)), pltpu.SemaphoreType.DMA((pairs,))],
+        out_specs=[VMEM, VMEM, VMEM],
+        scratch_shapes=held + [pltpu.SemaphoreType.DMA((4,)), pltpu.SemaphoreType.DMA((pairs // c_n,))],
         name="pack",
         compiler_params=large,
     )(queries, keys, values, send_order, out_weight)
     recv = lax.all_to_all(packed, CTX, 0, 0, tiled=True)
     prev = lax.ppermute(kv, CTX, [(i, i + 1) for i in range(n_ctx - 1)])
-    theirs = lax.ppermute(sent, "yl", [(0, 1), (1, 0)])
+    swap = [(0, 1), (1, 0)]
+    near = lax.ppermute(sent, "yl", swap)
     slash, ints = pl.pallas_call(
         band_kernel,
         out_shape=[
@@ -358,8 +361,11 @@
         name="select",
         compiler_params=small,
     )(ints, recv, slash)
+    parts, near = lax.optimization_barrier((parts, near))
+    far = lax.ppermute(near, "c", swap)
     mine = lax.all_to_all(parts, ("z", "x"), 0, 0, tiled=True)
-    other = lax.ppermute(mine, "c", [(0, 1), (1, 0)])
+    mine, far = lax.optimization_barrier((mine, far))
+    other = lax.ppermute(mine, "c", swap)
     half = pl.pallas_call(
         half_kernel,
         out_shape=jax.ShapeDtypeStruct((8 * n_ctx, 2 * HEAD), F32),
@@ -377,28 +383,28 @@
         name="finish",
         compiler_params=pltpu.CompilerParams(vmem_limit_bytes=32 * MIB),
     )(ints, recv, mine, other, half)
-    theirs_full = lax.ppermute(full, "yl", [(0, 1), (1, 0)])
-    own, weight = pl.pallas_call(
+    theirs_full = lax.ppermute(full, "yl", swap)
+    own = pl.pallas_call(
         own_kernel,
-        out_shape=[
-            jax.ShapeDtypeStruct((pairs, rows, width), F32),
-            jax.ShapeDtypeStruct(quarter, BF16),
+        out_shape=jax.ShapeDtypeStruct((pairs, rows, width), F32),
+        in_specs=[VMEM, HBM],
+        out_specs=VMEM,
+        scratch_shapes=[
+            pltpu.VMEM((pairs, out_weight.shape[0], width), BF16),
+            pltpu.SemaphoreType.DMA((pairs,)),
         ],
-        in_specs=[VMEM, HBM, HBM],
-        out_specs=[VMEM, VMEM],
-        scratch_shapes=[pltpu.VMEM(quarter, BF16), pltpu.SemaphoreType.DMA((pairs + 1,))],
         name="project_own",
-        compiler_params=pltpu.CompilerParams(vmem_limit_bytes=48 * MIB),
+        compiler_params=pltpu.CompilerParams(vmem_limit_bytes=52 * MIB),
         cost_estimate=pl.CostEstimate(flops=300000000, bytes_accessed=8000000, transcendentals=0),
-    )(full, out_weight, theirs)
+    )(full, out_weight)
     partial = pl.pallas_call(
         both_kernel,
         out_shape=jax.ShapeDtypeStruct((pairs, rows, width), BF16),
-        in_specs=[VMEM] * 3,
+        in_specs=[VMEM] * 4,
         out_specs=VMEM,
         name="project_both",
         compiler_params=pltpu.CompilerParams(vmem_limit_bytes=32 * MIB),
-    )(own, theirs_full, weight)
+    )(own, theirs_full, near, far)
     sums = lax.all_to_all(partial, "yh", 0, 0, tiled=True)
     return jnp.sum(sums.astype(F32), axis=0).astype(BF16)
 

time: 178 us -> 103 us (0.58)
  the two profiles are of different devices: /device:TPU:1 before, /device:TPU:2 now
where the time goes in v6:
time: 103 us; the launch traced here: 102 us
  starting transfers between devices  34.6 us (34%)
  waiting for transfers between devices  28.4 us (28%)
  blocking collectives  22.5 us (22%)
  Pallas kernels  13.5 us (13%)
  local copies, waits for them, and re-layouts  2.23 us (2%)
    all_to_all x1, blocking collectives, local(): sums = lax.all_to_all(partial, 'yh', 0, 0, tiled=True)  22.5 us
    all_to_all x1, waiting for transfers between devices, local(): mine = lax.all_to_all(parts, ('z', 'x'), 0, 0, tiled=True)  15.9 us
    all_to_all x1, starting transfers between devices, local(): recv = lax.all_to_all(packed, CTX, 0, 0, tiled=True)  13.9 us
    all_to_all x1, starting transfers between devices, local(): mine = lax.all_to_all(parts, ('z', 'x'), 0, 0, tiled=True)  8.99 us
    ppermute x1, waiting for transfers between devices, local(): prev = lax.ppermute(kv, CTX, [(i, i + 1) for i in range(n_ctx - 1)])  4.24 us
    ppermute x1, starting transfers between devices, local(): near = lax.ppermute(sent, 'yl', swap)  3.48 us
    pallas_call x1, Pallas kernels, local(): pl.pallas_call(band_kernel, out_shape=[jax.ShapeDtypeStruct((chips, 24, H...  3.23 us
    ppermute x1, waiting for transfers between devices, local(): theirs_full = lax.ppermute(full, 'yl', swap)  3.02 us
  transfers between devices with their start and end apart: 7, of which 6 were waited for; matrix products, arithmetic and copies ran while one was open for 0% of the time, Pallas kernels for 8%

profile of v6, /device:TPU:2, one launch (start us, length us, event | category | flops | bytes accessed | tf_op | source)
XLA Modules:
  0.0 102.1 jit_solution(18011445141607073135)
XLA Ops:
  0.0 2.8 %pack.1 = (bf16[64,16,128]{2,1,0:T(8,128)(2,1)}, bf16[128,256]{1,0:T(8,128)(2,1)}, bf16[2,512,512]{2,1,0:T(8,128)(2,1)}) custom-call(bf16[128,512]{1,0:T(8,128)(2,1)} %q_in.3, bf16[128,128]{1,0:T(8,128)(2,1)} %keys_in.3, bf16[128,128]{1,0:T(8,128)(2,1)} %values_in.3, s32[1,64]{1,0:T(1,128)} %order_in.3, bf16[512,4096]{1,0:T(8,128)(2,1)} %weight_in.3), custom_call_target="tpu_custom_call" | custom-call | tf_op jit(solution)/shard_map/pack/pallas_call | solution.py:322
  2.9 3.5 %collective-permute-start.1 = (bf16[2,512,512]{2,1,0:T(8,128)(2,1)}, bf16[2,512,512]{2,1,0:T(8,128)(2,1)S(1)}, u32[]{:S(2)}, u32[]{:S(2)}) collective-permute-start(bf16[2,512,512]{2,1,0:T(8,128)(2,1)} %get-tuple-element.22), channel_id=1, source_target_pairs={{0,1},{1,0},{2,3},{3,2},{4,5},{5,4},{6,7},{7,6},{8,9},{9,8},{10,11... | collective-permute-start | bytes 3145736 | tf_op jit(solution)/shard_map/ppermute | solution.py:338
  6.3 13.9 %all-to-all-start = ((bf16[64,16,128]{2,1,0:T(8,128)(2,1)}), bf16[64,16,128]{2,1,0:T(8,128)(2,1)S(1)}, u32[]{:S(2)}, u32[]{:S(2)}) async-start(bf16[64,16,128]{2,1,0:T(8,128)(2,1)} %get-tuple-element.18), calls=%async_computation | async-start | bytes 524288 | tf_op jit(solution)/shard_map/all_to_all | solution.py:335
  20.2 2.1 %collective-permute-start = (bf16[128,256]{1,0:T(8,128)(2,1)}, bf16[128,256]{1,0:T(8,128)(2,1)S(1)}, u32[]{:S(2)}, u32[]{:S(2)}) collective-permute-start(bf16[128,256]{1,0:T(8,128)(2,1)} %get-tuple-element.16), channel_id=1, source_target_pairs={{0,8},{8,16},{16,24},{24,32},{32,40},{40,48},{48,56},{56,64},{64,7... | collective-permute-start | bytes 196616 | tf_op jit(solution)/shard_map/ppermute | solution.py:336
  22.3 4.2 %collective-permute-done.prev_in = bf16[128,256]{1,0:T(8,128)(2,1)S(1)} collective-permute-done((bf16[128,256]{1,0:T(8,128)(2,1)}, bf16[128,256]{1,0:T(8,128)(2,1)S(1)}, u32[]{:S(2)}, u32[]{:S(2)}) %collective-permute-start) | collective-permute-done | bytes 65568 | tf_op jit(solution)/shard_map/ppermute | solution.py:336
  26.5 0.0 copy-start.2
  26.5 0.6 copy-done.2
  27.2 3.2 %slash.1 = (bf16[32,24,128]{2,1,0:T(8,128)(2,1)}, s32[8,128]{1,0:T(8,128)}) custom-call(bf16[128,512]{1,0:T(8,128)(2,1)} %q_in.3, bf16[128,128]{1,0:T(8,128)(2,1)} %keys_in.3, bf16[128,128]{1,0:T(8,128)(2,1)} %values_in.3, s32[1,64]{1,0:T(1,128)} %order_in.3, s32[4,64]{1,0:T(4,128)} %offsets_in.1, s32[1,32]{1,0:T(1,128)} %vert_in.1, bf16[128,256]{1,0:T(8,128)(2,1)} %copy-done.2), custom_call_target="tpu_custom_call" | custom-call | tf_op jit(solution)/shard_map/slash/pallas_call | solution.py:339
  30.4 2.0 %all-to-all-done.recv = bf16[64,16,128]{2,1,0:T(8,128)(2,1)S(1)} async-done(((bf16[64,16,128]{2,1,0:T(8,128)(2,1)}), bf16[64,16,128]{2,1,0:T(8,128)(2,1)S(1)}, u32[]{:S(2)}, u32[]{:S(2)}) %all-to-all-start) | async-done | bytes 262176 | tf_op jit(solution)/shard_map/all_to_all | solution.py:335
  32.5 0.0 copy-start
  32.5 0.9 copy-done
  33.4 0.0 copy-start.1
  33.4 0.7 copy-done.1
  34.1 1.1 %select.1 = (bf16[32,88,128]{2,1,0:T(8,128)(2,1)}, s32[8,128]{1,0:T(8,128)S(1)}) custom-call(s32[8,128]{1,0:T(8,128)S(1)} %copy-done.1, bf16[64,16,128]{2,1,0:T(8,128)(2,1)S(1)} %all-to-all-done.recv, bf16[32,24,128]{2,1,0:T(8,128)(2,1)S(1)} %copy-done), custom_call_target="tpu_custom_call" | custom-call | tf_op jit(solution)/shard_map/select/pallas_call | solution.py:353
  35.2 0.0 collective-permute-done.1.near
  35.2 9.0 %all-to-all-start.1 = ((bf16[32,88,128]{2,1,0:T(8,128)(2,1)}), bf16[32,88,128]{2,1,0:T(8,128)(2,1)S(1)}, u32[]{:S(2)}, u32[]{:S(2)}) async-start(bf16[32,88,128]{2,1,0:T(8,128)(2,1)} %get-tuple-element.23), calls=%async_computation.1 | async-start | bytes 1441792 | tf_op jit(solution)/shard_map/all_to_all | solution.py:366
  44.2 1.9 %collective-permute-start.2 = (bf16[2,512,512]{2,1,0:T(8,128)(2,1)S(1)}, bf16[2,512,512]{2,1,0:T(8,128)(2,1)S(1)}, u32[]{:S(2)}, u32[]{:S(2)}) collective-permute-start(bf16[2,512,512]{2,1,0:T(8,128)(2,1)S(1)} %collective-permute-done.1.near), channel_id=1, source_target_pairs={{0,8},{8,0},{1,9},{9,1},{2,10},{10,2},{3,11},{11,3},{4,12},{12,4},... | collective-permute-start | bytes 3145736 | tf_op jit(solution)/shard_map/ppermute | solution.py:365
  46.1 2.6 %collective-permute-done.2.far = bf16[2,512,512]{2,1,0:T(8,128)(2,1)S(1)} collective-permute-done((bf16[2,512,512]{2,1,0:T(8,128)(2,1)S(1)}, bf16[2,512,512]{2,1,0:T(8,128)(2,1)S(1)}, u32[]{:S(2)}, u32[]{:S(2)}) %collective-permute-start.2) | collective-permute-done | bytes 1048608 | tf_op jit(solution)/shard_map/ppermute | solution.py:365
  48.7 15.9 %all-to-all-done.1.mine = bf16[32,88,128]{2,1,0:T(8,128)(2,1)S(1)} async-done(((bf16[32,88,128]{2,1,0:T(8,128)(2,1)}), bf16[32,88,128]{2,1,0:T(8,128)(2,1)S(1)}, u32[]{:S(2)}, u32[]{:S(2)}) %all-to-all-start.1) | async-done | bytes 720928 | tf_op jit(solution)/shard_map/all_to_all | solution.py:366
  64.6 1.9 %collective-permute-start.3 = (bf16[32,88,128]{2,1,0:T(8,128)(2,1)S(1)}, bf16[32,88,128]{2,1,0:T(8,128)(2,1)S(1)}, u32[]{:S(2)}, u32[]{:S(2)}) collective-permute-start(bf16[32,88,128]{2,1,0:T(8,128)(2,1)S(1)} %all-to-all-done.1.mine), channel_id=1, source_target_pairs={{0,8},{8,0},{1,9},{9,1},{2,10},{10,2},{3,11},{11,3},{4,12},{12,4},... | collective-permute-start | bytes 2162696 | tf_op jit(solution)/shard_map/ppermute | solution.py:368
  66.5 1.6 %half.1 = f32[512,256]{1,0:T(8,128)S(1)} custom-call(s32[8,128]{1,0:T(8,128)S(1)} %get-tuple-element.20.ints, bf16[64,16,128]{2,1,0:T(8,128)(2,1)S(1)} %all-to-all-done.recv, bf16[32,88,128]{2,1,0:T(8,128)(2,1)S(1)} %all-to-all-done.1.mine), custom_call_target="tpu_custom_call" | custom-call | flops 300000000 | bytes 2000000 | tf_op jit(solution)/shard_map/half/pallas_call | solution.py:369
  68.1 0.6 collective-permute-done.3.other
  68.7 2.2 %finish.1.full = bf16[128,512]{1,0:T(8,128)(2,1)S(1)} custom-call(s32[8,128]{1,0:T(8,128)S(1)} %get-tuple-element.20.ints, bf16[64,16,128]{2,1,0:T(8,128)(2,1)S(1)} %all-to-all-done.recv, bf16[32,88,128]{2,1,0:T(8,128)(2,1)S(1)} %all-to-all-done.1.mine, bf16[32,88,128]{2,1,0:T(8,128)(2,1)S(1)} %collective-permute-done.3.other, f32[512,256]{1,0:T(8,128)S(1)} %half.1), custom_call_target="tpu_custom_call" | custom-call | tf_op jit(solution)/shard_map/finish/pallas_call | solution.py:378
  70.9 2.4 %collective-permute-start.4 = (bf16[128,512]{1,0:T(8,128)(2,1)S(1)}, bf16[128,512]{1,0:T(8,128)(2,1)S(1)}, u32[]{:S(2)}, u32[]{:S(2)}) collective-permute-start(bf16[128,512]{1,0:T(8,128)(2,1)S(1)} %finish.1.full), channel_id=1, source_target_pairs={{0,1},{1,0},{2,3},{3,2},{4,5},{5,4},{6,7},{7,6},{8,9},{9,8},{10,11... | collective-permute-start | bytes 393224 | tf_op jit(solution)/shard_map/ppermute | solution.py:386
  73.3 2.0 %project_own.1.own = f32[4,128,512]{2,1,0:T(8,128)S(1)} custom-call(bf16[128,512]{1,0:T(8,128)(2,1)S(1)} %finish.1.full, bf16[512,4096]{1,0:T(8,128)(2,1)} %weight_in.3), custom_call_target="tpu_custom_call" | custom-call | flops 300000000 | bytes 8000000 | tf_op jit(solution)/shard_map/project_own/pallas_call | solution.py:387
  75.3 3.0 %collective-permute-done.4.full = bf16[128,512]{1,0:T(8,128)(2,1)S(1)} collective-permute-done((bf16[128,512]{1,0:T(8,128)(2,1)S(1)}, bf16[128,512]{1,0:T(8,128)(2,1)S(1)}, u32[]{:S(2)}, u32[]{:S(2)}) %collective-permute-start.4) | collective-permute-done | bytes 131104 | tf_op jit(solution)/shard_map/ppermute | solution.py:386
  78.3 0.5 project_both.1
  78.8 22.5 %all_to_all.15 = bf16[4,128,512]{2,1,0:T(8,128)(2,1)S(1)} all-to-all(bf16[4,128,512]{2,1,0:T(8,128)(2,1)S(1)} %project_both.1), channel_id=1, replica_groups=mesh['z'=8,'x'=4,'c'=2,'yh'=4,'yl'=2] {'yh'}, dimensions={0} | all-to-all | bytes 1048576 | tf_op jit(solution)/shard_map/all_to_all | solution.py:408
  101.3 0.7 reduce_sum.12
Async XLA Ops:
  2.9 32.3 %collective-permute-start.1 = (bf16[2,512,512]{2,1,0:T(8,128)(2,1)}, bf16[2,512,512]{2,1,0:T(8,128)(2,1)S(1)}, u32[]{:S(2)}, u32[]{:S(2)}) collective-permute-start(bf16[2,512,512]{2,1,0:T(8,128)(2,1)} %get-tuple-element.22), channel_id=1, source_target_pairs={{0,1},{1,0},{2,3},{3,2},{4,5},{5,4},{6,7},{7,6},{8,9},{9,8},{10,11... | collective-permute-start | bytes 3145736 | tf_op jit(solution)/shard_map/ppermute | solution.py:338
  6.3 26.1 %all-to-all-start = ((bf16[64,16,128]{2,1,0:T(8,128)(2,1)}), bf16[64,16,128]{2,1,0:T(8,128)(2,1)S(1)}, u32[]{:S(2)}, u32[]{:S(2)}) async-start(bf16[64,16,128]{2,1,0:T(8,128)(2,1)} %get-tuple-element.18), calls=%async_computation | async-start | bytes 524288 | tf_op jit(solution)/shard_map/all_to_all | solution.py:335
  20.2 6.3 %collective-permute-start = (bf16[128,256]{1,0:T(8,128)(2,1)}, bf16[128,256]{1,0:T(8,128)(2,1)S(1)}, u32[]{:S(2)}, u32[]{:S(2)}) collective-permute-start(bf16[128,256]{1,0:T(8,128)(2,1)} %get-tuple-element.16), channel_id=1, source_target_pairs={{0,8},{8,16},{16,24},{24,32},{32,40},{40,48},{48,56},{56,64},{64,7... | collective-permute-start | bytes 196616 | tf_op jit(solution)/shard_map/ppermute | solution.py:336
  26.5 0.6 copy-start.2
  32.5 0.9 copy-start
  33.4 0.7 copy-start.1
  35.2 29.4 %all-to-all-start.1 = ((bf16[32,88,128]{2,1,0:T(8,128)(2,1)}), bf16[32,88,128]{2,1,0:T(8,128)(2,1)S(1)}, u32[]{:S(2)}, u32[]{:S(2)}) async-start(bf16[32,88,128]{2,1,0:T(8,128)(2,1)} %get-tuple-element.23), calls=%async_computation.1 | async-start | bytes 1441792 | tf_op jit(solution)/shard_map/all_to_all | solution.py:366
  44.2 4.6 %collective-permute-start.2 = (bf16[2,512,512]{2,1,0:T(8,128)(2,1)S(1)}, bf16[2,512,512]{2,1,0:T(8,128)(2,1)S(1)}, u32[]{:S(2)}, u32[]{:S(2)}) collective-permute-start(bf16[2,512,512]{2,1,0:T(8,128)(2,1)S(1)} %collective-permute-done.1.near), channel_id=1, source_target_pairs={{0,8},{8,0},{1,9},{9,1},{2,10},{10,2},{3,11},{11,3},{4,12},{12,4},... | collective-permute-start | bytes 3145736 | tf_op jit(solution)/shard_map/ppermute | solution.py:365
  64.6 4.1 %collective-permute-start.3 = (bf16[32,88,128]{2,1,0:T(8,128)(2,1)S(1)}, bf16[32,88,128]{2,1,0:T(8,128)(2,1)S(1)}, u32[]{:S(2)}, u32[]{:S(2)}) collective-permute-start(bf16[32,88,128]{2,1,0:T(8,128)(2,1)S(1)} %all-to-all-done.1.mine), channel_id=1, source_target_pairs={{0,8},{8,0},{1,9},{9,1},{2,10},{10,2},{3,11},{11,3},{4,12},{12,4},... | collective-permute-start | bytes 2162696 | tf_op jit(solution)/shard_map/ppermute | solution.py:368
  70.9 7.4 %collective-permute-start.4 = (bf16[128,512]{1,0:T(8,128)(2,1)S(1)}, bf16[128,512]{1,0:T(8,128)(2,1)S(1)}, u32[]{:S(2)}, u32[]{:S(2)}) collective-permute-start(bf16[128,512]{1,0:T(8,128)(2,1)S(1)} %finish.1.full), channel_id=1, source_target_pairs={{0,1},{1,0},{2,3},{3,2},{4,5},{5,4},{6,7},{7,6},{8,9},{9,8},{10,11... | collective-permute-start | bytes 393224 | tf_op jit(solution)/shard_map/ppermute | solution.py:386

commit v7 on v6

--- a/solution.py
+++ b/solution.py
@@ -19,7 +19,7 @@
 LOW = -1e30
 FACTOR = math.log2(math.e) / math.sqrt(HEAD)
 MIB = 1024 * 1024
-VERT, WANT, CORE = 0, 1, 2
+NUMBER, VERT = 4, 5
 
 
 def iota(shape, dim):
@@ -72,8 +72,20 @@
     return ref.at[:, pl.ds(start, width)]
 
 
+def tiled_vertical(vertical):
+    spread = bits(iota((NV, HEAD), 0) == iota((NV, HEAD), 1) % NV)
+    return jnp.dot(vertical[...].astype(F32).astype(BF16), spread, preferred_element_type=F32)
+
+
+def vertical_of(recv):
+    tail = recv[0, 8:].astype(F32)
+    here = iota(tail.shape, 0) == VERT
+    return jnp.sum(jnp.where(here, tail, 0.0), axis=0, keepdims=True).astype(jnp.int32)
+
+
 def pack_kernel(
-    q_in, keys_in, values_in, order_in, weight_in, out, kv, sent, q, keys, values, order, sems, wsems
+    q_in, keys_in, values_in, order_in, vert_in, weight_in, out, kv, sent,
+    q, keys, values, order, vertical, sems, wsems,
 ):
     parity, core = lax.axis_index("yl"), lax.axis_index("c")
     share = sent.shape[0]
@@ -85,7 +97,10 @@
     ]
     for move in moves:
         move.start()
-    load([(q_in, q), (keys_in, keys), (values_in, values), (order_in, order)], sems)
+    load(
+        [(q_in, q), (keys_in, keys), (values_in, values), (order_in, order), (vert_in, vertical)],
+        sems,
+    )
     rows = q.shape[0]
     heads = q.shape[1] // HEAD
     count = rows // 2
@@ -104,10 +119,11 @@
     diagonal = iota((count, count), 0) == iota((count, count), 1)
     number = jnp.sum(jnp.where(diagonal, order[...].astype(F32), 0.0), axis=1, keepdims=True)
     number = jnp.broadcast_to(number, (count, HEAD)).astype(BF16)
-    owner = jnp.where(slot == 4, new // 8, -1)
+    owner = jnp.where(slot == NUMBER, new // 8, -1)
     numbers = jnp.dot(
         bits(iota((8 * count, count), 1) == owner), number, preferred_element_type=F32
     )
+    numbers += jnp.where(slot == VERT, tiled_vertical(vertical), 0.0)
     out[:, 8:] = (kv_rows + numbers).astype(BF16).reshape(count, 8, HEAD)
     for move in moves:
         move.wait()
@@ -120,7 +136,7 @@
 
 
 def band_kernel(
-    q_in, keys_in, values_in, order_in, offsets_in, vert_in, prev_in, out, ints,
+    q_in, keys_in, values_in, order_in, offsets_in, vert_in, prev_in, out,
     q, keys, values, order, offsets, vertical, prev, sems,
 ):
     load(
@@ -132,16 +148,8 @@
     count = rows // 2
     chips = out.shape[0]
     band = 2 * rows
-    ctx, core = lax.axis_index(CTX), lax.axis_index("c")
-    spread = bits(iota((NV, HEAD), 0) == iota((NV, HEAD), 1) % NV)
-    vert = jnp.dot(
-        vertical[...].astype(F32).astype(BF16), spread, preferred_element_type=F32
-    ).astype(jnp.int32)
-    table_row = iota(ints.shape, 0)
-    want = (vert // 2) * 8 + (vert % 2) * 2 + iota((1, HEAD), 1) // NV
-    ints[...] = jnp.where(
-        table_row == VERT, vert, jnp.where(table_row == WANT, want, jnp.where(table_row == CORE, core, 0))
-    )
+    ctx = lax.axis_index(CTX)
+    vert = tiled_vertical(vertical).astype(jnp.int32)
     closed = jnp.zeros((1, band), F32)
     part = iota((1, band), 1) // BLK
     for j in range(band // BLK):
@@ -183,9 +191,9 @@
     out[:, 16:] = sums.reshape(chips, 8, HEAD)
 
 
-def select_kernel(ints, recv, slash, out, kept):
-    kept[...] = ints[...]
-    want = ints[WANT : WANT + 1, : 2 * NV]
+def select_kernel(recv, slash, out):
+    vert = vertical_of(recv)
+    want = ((vert // 2) * 8 + (vert % 2) * 2 + iota((1, HEAD), 1) // NV)[:, : 2 * NV]
     held = recv[:, 8:].reshape(-1, HEAD)
     picked = pick_t(iota((held.shape[0], 2 * NV), 0) == want, held)
     out[:, 2 * NV :] = slash[...]
@@ -193,8 +201,8 @@
         out[chip, : 2 * NV] = picked
 
 
-def key_positions(ints, core, chips):
-    vpos = ints[VERT : VERT + 1, :] * BLK + (iota((1, HEAD), 1) // NV) * 2 + core
+def key_positions(vert, core, chips):
+    vpos = vert * BLK + (iota((1, HEAD), 1) // NV) * 2 + core
     step = 2 * HEAD // NV
     return jnp.concatenate([vpos + m * step for m in range(chips * NV // HEAD)], axis=1)
 
@@ -202,17 +210,17 @@
 def row_positions(recv, rows):
     tail = recv[:, 8:].astype(F32)
     size = 8 * tail.shape[0]
-    number = jnp.sum(jnp.where(iota(tail.shape, 1) == 4, tail, 0.0), axis=1, keepdims=True)
+    number = jnp.sum(jnp.where(iota(tail.shape, 1) == NUMBER, tail, 0.0), axis=1, keepdims=True)
     number = jnp.broadcast_to(number, tail.shape).reshape(size, HEAD)[:, :1]
     at = iota((size, 1), 0)
     return (at // 8) * rows + number.astype(jnp.int32) * 2 + at % 2
 
 
-def half_kernel(ints, recv, mine, out):
-    core = ints[CORE : CORE + 1, :1]
+def half_kernel(recv, mine, out):
+    core = lax.axis_index("c")
     size = out.shape[0]
     rows = 2 * recv.shape[0]
-    pos = key_positions(ints, core, mine.shape[0])
+    pos = key_positions(vertical_of(recv), core, mine.shape[0])
     qpos = row_positions(recv, rows)
     q = recv[:, :8].reshape(size, HEAD)
     keys = mine[:, :NV].reshape(-1, HEAD)
@@ -228,14 +236,14 @@
         out[cut, HEAD:] = jnp.where(lane == 0, top, total)
 
 
-def finish_kernel(ints, recv, mine, other, half, out):
+def finish_kernel(recv, mine, other, half, out):
     count = recv.shape[0]
     size = 8 * count
     rows = out.shape[0]
     heads = size // rows
-    core = ints[CORE : CORE + 1, :1]
+    core = lax.axis_index("c")
     first = core == 0
-    pos = key_positions(ints, 1 - core, mine.shape[0])
+    pos = key_positions(vertical_of(recv), 1 - core, mine.shape[0])
     qpos = row_positions(recv, rows)
 
     def by_owner(cut):
@@ -299,13 +307,17 @@
         out[j] = jnp.dot(full[...], weight[j], preferred_element_type=F32)
 
 
-def both_kernel(own, full, near, far, out):
+def arrange_kernel(near, far, out):
     core = lax.axis_index("c")
     share = near.shape[0]
-    for weight, first in ((near, core * share), (far, (1 - core) * share)):
-        for i in range(share):
-            part = own[first + i] + jnp.dot(full[...], weight[i], preferred_element_type=F32)
-            out[first + i] = part.astype(BF16)
+    out[pl.ds(core * share, share)] = near[...]
+    out[pl.ds((1 - core) * share, share)] = far[...]
+
+
+def both_kernel(own, full, weight, out):
+    for j in range(out.shape[0]):
+        part = own[j] + jnp.dot(full[...], weight[j], preferred_element_type=F32)
+        out[j] = part.astype(BF16)
 
 
 def local(queries, keys, values, vertical, offsets, send_order, out_weight):
@@ -326,63 +338,67 @@
             jax.ShapeDtypeStruct((rows, 2 * HEAD), BF16),
             jax.ShapeDtypeStruct(columns_half, BF16),
         ],
-        in_specs=[HBM] * 5,
+        in_specs=[HBM] * 6,
         out_specs=[VMEM, VMEM, VMEM],
-        scratch_shapes=held + [pltpu.SemaphoreType.DMA((4,)), pltpu.SemaphoreType.DMA((pairs // c_n,))],
+        scratch_shapes=held + [pltpu.VMEM(vertical.shape, jnp.int32), pltpu.SemaphoreType.DMA((5,)), pltpu.SemaphoreType.DMA((pairs // c_n,))],
         name="pack",
         compiler_params=large,
-    )(queries, keys, values, send_order, out_weight)
+    )(queries, keys, values, send_order, vertical, out_weight)
     recv = lax.all_to_all(packed, CTX, 0, 0, tiled=True)
     prev = lax.ppermute(kv, CTX, [(i, i + 1) for i in range(n_ctx - 1)])
     swap = [(0, 1), (1, 0)]
+    sent, prev = lax.optimization_barrier((sent, prev))
     near = lax.ppermute(sent, "yl", swap)
-    slash, ints = pl.pallas_call(
+    slash = pl.pallas_call(
         band_kernel,
-        out_shape=[
-            jax.ShapeDtypeStruct((chips, 24, HEAD), BF16),
-            jax.ShapeDtypeStruct((8, HEAD), jnp.int32),
-        ],
+        out_shape=jax.ShapeDtypeStruct((chips, 24, HEAD), BF16),
         in_specs=[HBM] * 7,
-        out_specs=[VMEM, VMEM],
+        out_specs=VMEM,
         scratch_shapes=held
         + [pltpu.VMEM(a.shape, a.dtype) for a in (offsets, vertical, prev)]
         + [pltpu.SemaphoreType.DMA((7,))],
         name="slash",
         compiler_params=large,
+        cost_estimate=pl.CostEstimate(flops=20000000000, bytes_accessed=1000000, transcendentals=0),
     )(queries, keys, values, send_order, offsets, vertical, prev)
-    parts, ints = pl.pallas_call(
+    parts = pl.pallas_call(
         select_kernel,
-        out_shape=[
-            jax.ShapeDtypeStruct((chips, 2 * NV + 24, HEAD), BF16),
-            jax.ShapeDtypeStruct(ints.shape, jnp.int32),
-        ],
-        in_specs=[VMEM] * 3,
-        out_specs=[VMEM, VMEM],
+        out_shape=jax.ShapeDtypeStruct((chips, 2 * NV + 24, HEAD), BF16),
+        in_specs=[VMEM] * 2,
+        out_specs=VMEM,
         name="select",
         compiler_params=small,
-    )(ints, recv, slash)
-    parts, near = lax.optimization_barrier((parts, near))
+    )(recv, slash)
     far = lax.ppermute(near, "c", swap)
+    theirs = pl.pallas_call(
+        arrange_kernel,
+        out_shape=jax.ShapeDtypeStruct((pairs,) + near.shape[1:], BF16),
+        in_specs=[VMEM] * 2,
+        out_specs=VMEM,
+        name="arrange",
+        compiler_params=small,
+        cost_estimate=pl.CostEstimate(flops=3000000000, bytes_accessed=4000000, transcendentals=0),
+    )(near, far)
     mine = lax.all_to_all(parts, ("z", "x"), 0, 0, tiled=True)
-    mine, far = lax.optimization_barrier((mine, far))
+    mine, theirs = lax.optimization_barrier((mine, theirs))
     other = lax.ppermute(mine, "c", swap)
     half = pl.pallas_call(
         half_kernel,
         out_shape=jax.ShapeDtypeStruct((8 * n_ctx, 2 * HEAD), F32),
-        in_specs=[VMEM] * 3,
+        in_specs=[VMEM] * 2,
         out_specs=VMEM,
         name="half",
         compiler_params=pltpu.CompilerParams(vmem_limit_bytes=32 * MIB),
         cost_estimate=pl.CostEstimate(flops=300000000, bytes_accessed=2000000, transcendentals=500000),
-    )(ints, recv, mine)
+    )(recv, mine)
     full = pl.pallas_call(
         finish_kernel,
         out_shape=jax.ShapeDtypeStruct(queries.shape, BF16),
-        in_specs=[VMEM] * 5,
+        in_specs=[VMEM] * 4,
         out_specs=VMEM,
         name="finish",
         compiler_params=pltpu.CompilerParams(vmem_limit_bytes=32 * MIB),
-    )(ints, recv, mine, other, half)
+    )(recv, mine, other, half)
     theirs_full = lax.ppermute(full, "yl", swap)
     own = pl.pallas_call(
         own_kernel,
@@ -400,11 +416,11 @@
     partial = pl.pallas_call(
         both_kernel,
         out_shape=jax.ShapeDtypeStruct((pairs, rows, width), BF16),
-        in_specs=[VMEM] * 4,
+        in_specs=[VMEM] * 3,
         out_specs=VMEM,
         name="project_both",
         compiler_params=pltpu.CompilerParams(vmem_limit_bytes=32 * MIB),
-    )(own, theirs_full, near, far)
+    )(own, theirs_full, theirs)
     sums = lax.all_to_all(partial, "yh", 0, 0, tiled=True)
     return jnp.sum(sums.astype(F32), axis=0).astype(BF16)
 

time: 103 us -> 98.6 us (0.957)
  the two profiles are of different devices: /device:TPU:2 before, /device:TPU:1 now
where the time goes in v7:
time: 98.6 us; the launch traced here: 97 us
  starting transfers between devices  35.5 us (36%)
  waiting for transfers between devices  22.8 us (23%)
  blocking collectives  21.1 us (21%)
  Pallas kernels  13.6 us (14%)
  local copies, waits for them, and re-layouts  3.12 us (3%)
    all_to_all x1, blocking collectives, local(): sums = lax.all_to_all(partial, 'yh', 0, 0, tiled=True)  21.1 us
    all_to_all x1, starting transfers between devices, local(): recv = lax.all_to_all(packed, CTX, 0, 0, tiled=True)  13.2 us
    ppermute x1, waiting for transfers between devices, local(): near = lax.ppermute(sent, 'yl', swap)  7.26 us
    all_to_all x1, waiting for transfers between devices, local(): recv = lax.all_to_all(packed, CTX, 0, 0, tiled=True)  6.68 us
    all_to_all x1, waiting for transfers between devices, local(): mine = lax.all_to_all(parts, ('z', 'x'), 0, 0, tiled=True)  5.94 us
    ppermute x1, starting transfers between devices, local(): prev = lax.ppermute(kv, CTX, [(i, i + 1) for i in range(n_ctx - 1)])  4.51 us
    ppermute x1, starting transfers between devices, local(): other = lax.ppermute(mine, 'c', swap)  4.28 us
    all_to_all x1, starting transfers between devices, local(): mine = lax.all_to_all(parts, ('z', 'x'), 0, 0, tiled=True)  3.91 us
  transfers between devices with their start and end apart: 7, of which 6 were waited for; matrix products, arithmetic and copies ran while one was open for 0% of the time, Pallas kernels for 8%

profile of v7, /device:TPU:1, one launch (start us, length us, event | category | flops | bytes accessed | tf_op | source)
XLA Modules:
  0.0 97.0 jit_solution(5414390232641702725)
XLA Ops:
  0.0 2.9 %pack.1 = (bf16[64,16,128]{2,1,0:T(8,128)(2,1)}, bf16[128,256]{1,0:T(8,128)(2,1)}, bf16[2,512,512]{2,1,0:T(8,128)(2,1)}) custom-call(bf16[128,512]{1,0:T(8,128)(2,1)} %q_in.3, bf16[128,128]{1,0:T(8,128)(2,1)} %keys_in.3, bf16[128,128]{1,0:T(8,128)(2,1)} %values_in.3, s32[1,64]{1,0:T(1,128)} %order_in.3, s32[1,32]{1,0:T(1,128)} %vert_in.3, ...), custom_call_target="tpu_custom_call" | custom-call | tf_op jit(solution)/shard_map/pack/pallas_call | solution.py:334
  2.9 4.5 %collective-permute-start = (bf16[128,256]{1,0:T(8,128)(2,1)}, bf16[128,256]{1,0:T(8,128)(2,1)S(1)}, u32[]{:S(2)}, u32[]{:S(2)}) collective-permute-start(bf16[128,256]{1,0:T(8,128)(2,1)} %get-tuple-element.14), channel_id=1, source_target_pairs={{0,8},{8,16},{16,24},{24,32},{32,40},{40,48},{48,56},{56,64},{64,7... | collective-permute-start | bytes 196616 | tf_op jit(solution)/shard_map/ppermute | solution.py:348
  7.4 13.2 %all-to-all-start = ((bf16[64,16,128]{2,1,0:T(8,128)(2,1)}), bf16[64,16,128]{2,1,0:T(8,128)(2,1)S(1)}, u32[]{:S(2)}, u32[]{:S(2)}) async-start(bf16[64,16,128]{2,1,0:T(8,128)(2,1)} %get-tuple-element.12), calls=%async_computation | async-start | bytes 524288 | tf_op jit(solution)/shard_map/all_to_all | solution.py:347
  20.6 0.0 collective-permute-done.prev_in
  20.6 0.0 copy-start.3
  20.6 3.2 %collective-permute-start.1 = (bf16[2,512,512]{2,1,0:T(8,128)(2,1)}, bf16[2,512,512]{2,1,0:T(8,128)(2,1)S(1)}, u32[]{:S(2)}, u32[]{:S(2)}) collective-permute-start(bf16[2,512,512]{2,1,0:T(8,128)(2,1)} %get-tuple-element.16), channel_id=1, source_target_pairs={{0,1},{1,0},{2,3},{3,2},{4,5},{5,4},{6,7},{7,6},{8,9},{9,8},{10,11... | collective-permute-start | bytes 3145736 | tf_op jit(solution)/shard_map/ppermute | solution.py:351
  23.8 0.0 copy-done.3
  23.8 3.2 %slash.1 = bf16[32,24,128]{2,1,0:T(8,128)(2,1)} custom-call(bf16[128,512]{1,0:T(8,128)(2,1)} %q_in.3, bf16[128,128]{1,0:T(8,128)(2,1)} %keys_in.3, bf16[128,128]{1,0:T(8,128)(2,1)} %values_in.3, s32[1,64]{1,0:T(1,128)} %order_in.3, s32[4,64]{1,0:T(4,128)} %offsets_in.1, s32[1,32]{1,0:T(1,128)} %vert_in.3, bf16[128,256]{1,0:T(8,128)(2,1)} %copy-done.3), custom_call_target="tpu_custom_call" | custom-call | flops 20000000000 | bytes 1000000 | tf_op jit(solution)/shard_map/slash/pallas_call | solution.py:352
  27.0 6.7 %all-to-all-done.recv = bf16[64,16,128]{2,1,0:T(8,128)(2,1)S(1)} async-done(((bf16[64,16,128]{2,1,0:T(8,128)(2,1)}), bf16[64,16,128]{2,1,0:T(8,128)(2,1)S(1)}, u32[]{:S(2)}, u32[]{:S(2)}) %all-to-all-start) | async-done | bytes 262176 | tf_op jit(solution)/shard_map/all_to_all | solution.py:347
  33.7 0.0 copy-start
  33.7 0.9 copy-done
  34.6 1.1 %select.1 = bf16[32,88,128]{2,1,0:T(8,128)(2,1)} custom-call(bf16[64,16,128]{2,1,0:T(8,128)(2,1)S(1)} %all-to-all-done.recv, bf16[32,24,128]{2,1,0:T(8,128)(2,1)S(1)} %copy-done), custom_call_target="tpu_custom_call" | custom-call | tf_op jit(solution)/shard_map/select/pallas_call | solution.py:364
  35.8 3.9 %all-to-all-start.1 = ((bf16[32,88,128]{2,1,0:T(8,128)(2,1)}), bf16[32,88,128]{2,1,0:T(8,128)(2,1)S(1)}, u32[]{:S(2)}, u32[]{:S(2)}) async-start(bf16[32,88,128]{2,1,0:T(8,128)(2,1)} %select.1), calls=%async_computation.1 | async-start | bytes 1441792 | tf_op jit(solution)/shard_map/all_to_all | solution.py:382
  39.7 7.3 %collective-permute-done.1.near = bf16[2,512,512]{2,1,0:T(8,128)(2,1)S(1)} collective-permute-done((bf16[2,512,512]{2,1,0:T(8,128)(2,1)}, bf16[2,512,512]{2,1,0:T(8,128)(2,1)S(1)}, u32[]{:S(2)}, u32[]{:S(2)}) %collective-permute-start.1) | collective-permute-done | bytes 1048608 | tf_op jit(solution)/shard_map/ppermute | solution.py:351
  47.0 3.2 %collective-permute-start.2 = (bf16[2,512,512]{2,1,0:T(8,128)(2,1)S(1)}, bf16[2,512,512]{2,1,0:T(8,128)(2,1)S(1)}, u32[]{:S(2)}, u32[]{:S(2)}) collective-permute-start(bf16[2,512,512]{2,1,0:T(8,128)(2,1)S(1)} %collective-permute-done.1.near), channel_id=1, source_target_pairs={{0,8},{8,0},{1,9},{9,1},{2,10},{10,2},{3,11},{11,3},{4,12},{12,4},... | collective-permute-start | bytes 3145736 | tf_op jit(solution)/shard_map/ppermute | solution.py:372
  50.2 0.0 copy-start.1
  50.2 1.0 copy-done.1
  51.1 1.3 %collective-permute-done.2.far = bf16[2,512,512]{2,1,0:T(8,128)(2,1)S(1)} collective-permute-done((bf16[2,512,512]{2,1,0:T(8,128)(2,1)S(1)}, bf16[2,512,512]{2,1,0:T(8,128)(2,1)S(1)}, u32[]{:S(2)}, u32[]{:S(2)}) %collective-permute-start.2) | collective-permute-done | bytes 1048608 | tf_op jit(solution)/shard_map/ppermute | solution.py:372
  52.4 0.0 copy-start.2
  52.4 1.2 %copy-done.2 = bf16[2,512,512]{2,1,0:T(8,128)(2,1)S(1)} copy-done((bf16[2,512,512]{2,1,0:T(8,128)(2,1)S(1)}, bf16[2,512,512]{2,1,0:T(8,128)(2,1)}, u32[]{:S(2)}) %copy-start.2) | copy-done | bytes 1048600
  53.6 0.1 arrange.1.weight
  53.8 5.9 %all-to-all-done.1.mine = bf16[32,88,128]{2,1,0:T(8,128)(2,1)S(1)} async-done(((bf16[32,88,128]{2,1,0:T(8,128)(2,1)}), bf16[32,88,128]{2,1,0:T(8,128)(2,1)S(1)}, u32[]{:S(2)}, u32[]{:S(2)}) %all-to-all-start.1) | async-done | bytes 720928 | tf_op jit(solution)/shard_map/all_to_all | solution.py:382
  59.7 4.3 %collective-permute-start.3 = (bf16[32,88,128]{2,1,0:T(8,128)(2,1)S(1)}, bf16[32,88,128]{2,1,0:T(8,128)(2,1)S(1)}, u32[]{:S(2)}, u32[]{:S(2)}) collective-permute-start(bf16[32,88,128]{2,1,0:T(8,128)(2,1)S(1)} %all-to-all-done.1.mine), channel_id=1, source_target_pairs={{0,8},{8,0},{1,9},{9,1},{2,10},{10,2},{3,11},{11,3},{4,12},{12,4},... | collective-permute-start | bytes 2162696 | tf_op jit(solution)/shard_map/ppermute | solution.py:384
  64.0 1.6 %half.1 = f32[512,256]{1,0:T(8,128)S(1)} custom-call(bf16[64,16,128]{2,1,0:T(8,128)(2,1)S(1)} %all-to-all-done.recv, bf16[32,88,128]{2,1,0:T(8,128)(2,1)S(1)} %all-to-all-done.1.mine), custom_call_target="tpu_custom_call" | custom-call | flops 300000000 | bytes 2000000 | tf_op jit(solution)/shard_map/half/pallas_call | solution.py:385
  65.6 0.2 collective-permute-done.3.other
  65.8 2.2 %finish.1.full = bf16[128,512]{1,0:T(8,128)(2,1)S(1)} custom-call(bf16[64,16,128]{2,1,0:T(8,128)(2,1)S(1)} %all-to-all-done.recv, bf16[32,88,128]{2,1,0:T(8,128)(2,1)S(1)} %all-to-all-done.1.mine, bf16[32,88,128]{2,1,0:T(8,128)(2,1)S(1)} %collective-permute-done.3.other, f32[512,256]{1,0:T(8,128)S(1)} %half.1), custom_call_target="tpu_custom_call" | custom-call | tf_op jit(solution)/shard_map/finish/pallas_call | solution.py:394
  68.1 3.2 %collective-permute-start.4 = (bf16[128,512]{1,0:T(8,128)(2,1)S(1)}, bf16[128,512]{1,0:T(8,128)(2,1)S(1)}, u32[]{:S(2)}, u32[]{:S(2)}) collective-permute-start(bf16[128,512]{1,0:T(8,128)(2,1)S(1)} %finish.1.full), channel_id=1, source_target_pairs={{0,1},{1,0},{2,3},{3,2},{4,5},{5,4},{6,7},{7,6},{8,9},{9,8},{10,11... | collective-permute-start | bytes 393224 | tf_op jit(solution)/shard_map/ppermute | solution.py:402
  71.3 2.0 %project_own.1.own = f32[4,128,512]{2,1,0:T(8,128)S(1)} custom-call(bf16[128,512]{1,0:T(8,128)(2,1)S(1)} %finish.1.full, bf16[512,4096]{1,0:T(8,128)(2,1)} %weight_in.3), custom_call_target="tpu_custom_call" | custom-call | flops 300000000 | bytes 8000000 | tf_op jit(solution)/shard_map/project_own/pallas_call | solution.py:403
  73.3 1.4 %collective-permute-done.4.full = bf16[128,512]{1,0:T(8,128)(2,1)S(1)} collective-permute-done((bf16[128,512]{1,0:T(8,128)(2,1)S(1)}, bf16[128,512]{1,0:T(8,128)(2,1)S(1)}, u32[]{:S(2)}, u32[]{:S(2)}) %collective-permute-start.4) | collective-permute-done | bytes 131104 | tf_op jit(solution)/shard_map/ppermute | solution.py:402
  74.7 0.4 project_both.1
  75.1 21.1 %all_to_all.15 = bf16[4,128,512]{2,1,0:T(8,128)(2,1)S(1)} all-to-all(bf16[4,128,512]{2,1,0:T(8,128)(2,1)S(1)} %project_both.1), channel_id=1, replica_groups=mesh['z'=8,'x'=4,'c'=2,'yh'=4,'yl'=2] {'yh'}, dimensions={0} | all-to-all | bytes 1048576 | tf_op jit(solution)/shard_map/all_to_all | solution.py:424
  96.2 0.7 reduce_sum.12
Async XLA Ops:
  2.9 17.7 %collective-permute-start = (bf16[128,256]{1,0:T(8,128)(2,1)}, bf16[128,256]{1,0:T(8,128)(2,1)S(1)}, u32[]{:S(2)}, u32[]{:S(2)}) collective-permute-start(bf16[128,256]{1,0:T(8,128)(2,1)} %get-tuple-element.14), channel_id=1, source_target_pairs={{0,8},{8,16},{16,24},{24,32},{32,40},{40,48},{48,56},{56,64},{64,7... | collective-permute-start | bytes 196616 | tf_op jit(solution)/shard_map/ppermute | solution.py:348
  7.4 26.3 %all-to-all-start = ((bf16[64,16,128]{2,1,0:T(8,128)(2,1)}), bf16[64,16,128]{2,1,0:T(8,128)(2,1)S(1)}, u32[]{:S(2)}, u32[]{:S(2)}) async-start(bf16[64,16,128]{2,1,0:T(8,128)(2,1)} %get-tuple-element.12), calls=%async_computation | async-start | bytes 524288 | tf_op jit(solution)/shard_map/all_to_all | solution.py:347
  20.6 3.2 %copy-start.3 = (bf16[128,256]{1,0:T(8,128)(2,1)}, bf16[128,256]{1,0:T(8,128)(2,1)S(1)}, u32[]{:S(2)}) copy-start(bf16[128,256]{1,0:T(8,128)(2,1)S(1)} %collective-permute-done.prev_in) | copy-start | bytes 196612
  20.6 26.4 %collective-permute-start.1 = (bf16[2,512,512]{2,1,0:T(8,128)(2,1)}, bf16[2,512,512]{2,1,0:T(8,128)(2,1)S(1)}, u32[]{:S(2)}, u32[]{:S(2)}) collective-permute-start(bf16[2,512,512]{2,1,0:T(8,128)(2,1)} %get-tuple-element.16), channel_id=1, source_target_pairs={{0,1},{1,0},{2,3},{3,2},{4,5},{5,4},{6,7},{7,6},{8,9},{9,8},{10,11... | collective-permute-start | bytes 3145736 | tf_op jit(solution)/shard_map/ppermute | solution.py:351
  33.7 0.9 copy-start
  35.8 24.0 %all-to-all-start.1 = ((bf16[32,88,128]{2,1,0:T(8,128)(2,1)}), bf16[32,88,128]{2,1,0:T(8,128)(2,1)S(1)}, u32[]{:S(2)}, u32[]{:S(2)}) async-start(bf16[32,88,128]{2,1,0:T(8,128)(2,1)} %select.1), calls=%async_computation.1 | async-start | bytes 1441792 | tf_op jit(solution)/shard_map/all_to_all | solution.py:382
  47.0 5.5 %collective-permute-start.2 = (bf16[2,512,512]{2,1,0:T(8,128)(2,1)S(1)}, bf16[2,512,512]{2,1,0:T(8,128)(2,1)S(1)}, u32[]{:S(2)}, u32[]{:S(2)}) collective-permute-start(bf16[2,512,512]{2,1,0:T(8,128)(2,1)S(1)} %collective-permute-done.1.near), channel_id=1, source_target_pairs={{0,8},{8,0},{1,9},{9,1},{2,10},{10,2},{3,11},{11,3},{4,12},{12,4},... | collective-permute-start | bytes 3145736 | tf_op jit(solution)/shard_map/ppermute | solution.py:372
  50.2 1.0 %copy-start.1 = (bf16[2,512,512]{2,1,0:T(8,128)(2,1)}, bf16[2,512,512]{2,1,0:T(8,128)(2,1)S(1)}, u32[]{:S(2)}) copy-start(bf16[2,512,512]{2,1,0:T(8,128)(2,1)S(1)} %collective-permute-done.1.near) | copy-start | bytes 3145732
  52.4 1.2 %copy-start.2 = (bf16[2,512,512]{2,1,0:T(8,128)(2,1)S(1)}, bf16[2,512,512]{2,1,0:T(8,128)(2,1)}, u32[]{:S(2)}) copy-start(bf16[2,512,512]{2,1,0:T(8,128)(2,1)} %copy-done.1) | copy-start | bytes 3145732
  59.7 6.1 %collective-permute-start.3 = (bf16[32,88,128]{2,1,0:T(8,128)(2,1)S(1)}, bf16[32,88,128]{2,1,0:T(8,128)(2,1)S(1)}, u32[]{:S(2)}, u32[]{:S(2)}) collective-permute-start(bf16[32,88,128]{2,1,0:T(8,128)(2,1)S(1)} %all-to-all-done.1.mine), channel_id=1, source_target_pairs={{0,8},{8,0},{1,9},{9,1},{2,10},{10,2},{3,11},{11,3},{4,12},{12,4},... | collective-permute-start | bytes 2162696 | tf_op jit(solution)/shard_map/ppermute | solution.py:384
  68.1 6.6 %collective-permute-start.4 = (bf16[128,512]{1,0:T(8,128)(2,1)S(1)}, bf16[128,512]{1,0:T(8,128)(2,1)S(1)}, u32[]{:S(2)}, u32[]{:S(2)}) collective-permute-start(bf16[128,512]{1,0:T(8,128)(2,1)S(1)} %finish.1.full), channel_id=1, source_target_pairs={{0,1},{1,0},{2,3},{3,2},{4,5},{5,4},{6,7},{7,6},{8,9},{9,8},{10,11... | collective-permute-start | bytes 393224 | tf_op jit(solution)/shard_map/ppermute | solution.py:402

commit v8 on v7

--- a/solution.py
+++ b/solution.py
@@ -95,36 +95,38 @@
         )
         for j in range(share)
     ]
-    for move in moves:
+    loads = [(order_in, order), (vert_in, vertical), (keys_in, keys), (values_in, values), (q_in, q)]
+    loads = [pltpu.make_async_copy(a, b, sems.at[i]) for i, (a, b) in enumerate(loads)]
+    for move in loads + moves:
         move.start()
-    load(
-        [(q_in, q), (keys_in, keys), (values_in, values), (order_in, order), (vert_in, vertical)],
-        sems,
-    )
     rows = q.shape[0]
     heads = q.shape[1] // HEAD
     count = rows // 2
-    kv[:, :HEAD] = keys[...]
-    kv[:, HEAD:] = values[...]
-    moved = pick_t(by_destination(order[...], rows, heads), head_rows(q, heads))
-    out[:, :8] = moved.reshape(count, 8, HEAD)
     new = iota((8 * count, 1), 0)
     slot = new % 8
     source = jnp.where(slot < 4, (slot % 2) * rows + (slot // 2) * BLK + new // 8, -1)
-    kv_rows = jnp.dot(
-        bits(iota((8 * count, 2 * rows), 1) == source),
-        jnp.concatenate([keys[...], values[...]], axis=0),
-        preferred_element_type=F32,
-    )
+    source = bits(iota((8 * count, 2 * rows), 1) == source)
+    owner = bits(iota((8 * count, count), 1) == jnp.where(slot == NUMBER, new // 8, -1))
     diagonal = iota((count, count), 0) == iota((count, count), 1)
+    for move in loads[:2]:
+        move.wait()
     number = jnp.sum(jnp.where(diagonal, order[...].astype(F32), 0.0), axis=1, keepdims=True)
     number = jnp.broadcast_to(number, (count, HEAD)).astype(BF16)
-    owner = jnp.where(slot == NUMBER, new // 8, -1)
-    numbers = jnp.dot(
-        bits(iota((8 * count, count), 1) == owner), number, preferred_element_type=F32
+    numbers = jnp.dot(owner, number, preferred_element_type=F32)
+    numbers += jnp.where(slot == VERT, tiled_vertical(vertical), 0.0)
+    target = bits(by_destination(order[...], rows, heads))
+    for move in loads[2:]:
+        move.wait()
+    kv[:, :HEAD] = keys[...]
+    kv[:, HEAD:] = values[...]
+    kv_rows = jnp.dot(
+        source, jnp.concatenate([keys[...], values[...]], axis=0), preferred_element_type=F32
     )
-    numbers += jnp.where(slot == VERT, tiled_vertical(vertical), 0.0)
     out[:, 8:] = (kv_rows + numbers).astype(BF16).reshape(count, 8, HEAD)
+    moved = lax.dot_general(
+        target, head_rows(q, heads), (((0,), (0,)), ((), ())), preferred_element_type=F32
+    )
+    out[:, :8] = moved.astype(BF16).reshape(count, 8, HEAD)
     for move in moves:
         move.wait()
 
@@ -139,10 +141,13 @@
     q_in, keys_in, values_in, order_in, offsets_in, vert_in, prev_in, out,
     q, keys, values, order, offsets, vertical, prev, sems,
 ):
-    load(
-        [(q_in, q), (keys_in, keys), (values_in, values), (order_in, order), (offsets_in, offsets), (vert_in, vertical), (prev_in, prev)],
-        sems,
-    )
+    pairs = [(offsets_in, offsets), (vert_in, vertical), (keys_in, keys), (prev_in, prev)]
+    pairs += [(values_in, values), (q_in, q), (order_in, order)]
+    moves = [pltpu.make_async_copy(a, b, sems.at[i]) for i, (a, b) in enumerate(pairs)]
+    for move in moves:
+        move.start()
+    for move in moves[:2]:
+        move.wait()
     rows = q.shape[0]
     heads = q.shape[1] // HEAD
     count = rows // 2
@@ -162,6 +167,8 @@
     offs = offsets[...]
     for k in range(offs.shape[1]):
         table = jnp.where(offs[:, k : k + 1] == lag, 1.0, table)
+    for move in moves[2:]:
+        move.wait()
     kb = jnp.concatenate([prev[:, :HEAD], keys[...]], axis=0)
     vb = jnp.concatenate([prev[:, HEAD:], values[...]], axis=0)
     lanes = iota((rows, HEAD), 1) % 8
@@ -187,8 +194,8 @@
     new = iota((8 * chips, 1), 0)
     owner = jnp.where(new % 8 < 2, (new // 8) * 2 + new % 8, -1)
     sums = pick(iota((8 * chips, size), 1) // 8 == owner, sums)
-    out[:, :16] = moved[:, :HEAD].reshape(chips, 16, HEAD)
-    out[:, 16:] = sums.reshape(chips, 8, HEAD)
+    out[:, :16] = moved[:, :HEAD].astype(F32).reshape(chips, 16, HEAD)
+    out[:, 16:] = sums.astype(F32).reshape(chips, 8, HEAD)
 
 
 def select_kernel(recv, slash, out):
@@ -351,7 +358,7 @@
     near = lax.ppermute(sent, "yl", swap)
     slash = pl.pallas_call(
         band_kernel,
-        out_shape=jax.ShapeDtypeStruct((chips, 24, HEAD), BF16),
+        out_shape=jax.ShapeDtypeStruct((chips, 24, HEAD), F32),
         in_specs=[HBM] * 7,
         out_specs=VMEM,
         scratch_shapes=held
@@ -368,7 +375,7 @@
         out_specs=VMEM,
         name="select",
         compiler_params=small,
-    )(recv, slash)
+    )(recv, slash.astype(BF16))
     far = lax.ppermute(near, "c", swap)
     theirs = pl.pallas_call(
         arrange_kernel,

time: 98.6 us -> 97.4 us (0.988)
  waiting for transfers between devices: 22.8 us -> 21.7 us
  other arithmetic: 0.75 us -> 1.77 us
    convert_element_type x0 -> x1, other arithmetic: none -> 1.02 us  [local(): slash.astype(BF16)]
    all_to_all x1, waiting for transfers between devices: 6.68 us -> 5.66 us  [local(): recv = lax.all_to_all(packed, CTX, 0, 0, tiled=True)]
    unnamed x8 -> x6, local copies, waits for them, and re-layouts: 3.12 us -> 2.2 us
  transfers between devices with their start and end apart: 7 -> 7, of which waited for: 6 -> 6; matrix products, arithmetic and copies ran while one was open for 0% -> 1% of each run, Pallas kernels for 8% -> 8%
where the time goes in v8:
time: 97.4 us; the launch traced here: 95.8 us
  starting transfers between devices  35.5 us (36%)
  waiting for transfers between devices  21.7 us (22%)
  blocking collectives  21.1 us (22%)
  Pallas kernels  13.4 us (14%)
  local copies, waits for them, and re-layouts  2.2 us (2%)
  other arithmetic  1.77 us (2%)
    all_to_all x1, blocking collectives, local(): sums = lax.all_to_all(partial, 'yh', 0, 0, tiled=True)  21.1 us
    all_to_all x1, starting transfers between devices, local(): recv = lax.all_to_all(packed, CTX, 0, 0, tiled=True)  13.2 us
    ppermute x1, waiting for transfers between devices, local(): near = lax.ppermute(sent, 'yl', swap)  8.18 us
    all_to_all x1, waiting for transfers between devices, local(): recv = lax.all_to_all(packed, CTX, 0, 0, tiled=True)  5.66 us
    all_to_all x1, waiting for transfers between devices, local(): mine = lax.all_to_all(parts, ('z', 'x'), 0, 0, tiled=True)  4.95 us
    ppermute x1, starting transfers between devices, local(): prev = lax.ppermute(kv, CTX, [(i, i + 1) for i in range(n_ctx - 1)])  4.51 us
    ppermute x1, starting transfers between devices, local(): other = lax.ppermute(mine, 'c', swap)  4.4 us
    all_to_all x1, starting transfers between devices, local(): mine = lax.all_to_all(parts, ('z', 'x'), 0, 0, tiled=True)  3.9 us
  transfers between devices with their start and end apart: 7, of which 6 were waited for; matrix products, arithmetic and copies ran while one was open for 1% of the time, Pallas kernels for 8%

profile of v8, /device:TPU:1, one launch (start us, length us, event | category | flops | bytes accessed | tf_op | source)
XLA Modules:
  0.0 95.8 jit_solution(16362287308264481228)
XLA Ops:
  0.0 2.6 %pack.1 = (bf16[64,16,128]{2,1,0:T(8,128)(2,1)}, bf16[128,256]{1,0:T(8,128)(2,1)}, bf16[2,512,512]{2,1,0:T(8,128)(2,1)}) custom-call(bf16[128,512]{1,0:T(8,128)(2,1)} %q_in.3, bf16[128,128]{1,0:T(8,128)(2,1)} %keys_in.3, bf16[128,128]{1,0:T(8,128)(2,1)} %values_in.3, s32[1,64]{1,0:T(1,128)} %order_in.3, s32[1,32]{1,0:T(1,128)} %vert_in.3, ...), custom_call_target="tpu_custom_call" | custom-call | tf_op jit(solution)/shard_map/pack/pallas_call | solution.py:341
  2.6 4.5 %collective-permute-start = (bf16[128,256]{1,0:T(8,128)(2,1)}, bf16[128,256]{1,0:T(8,128)(2,1)S(1)}, u32[]{:S(2)}, u32[]{:S(2)}) collective-permute-start(bf16[128,256]{1,0:T(8,128)(2,1)} %get-tuple-element.14), channel_id=1, source_target_pairs={{0,8},{8,16},{16,24},{24,32},{32,40},{40,48},{48,56},{56,64},{64,7... | collective-permute-start | bytes 196616 | tf_op jit(solution)/shard_map/ppermute | solution.py:355
  7.1 13.2 %all-to-all-start = ((bf16[64,16,128]{2,1,0:T(8,128)(2,1)}), bf16[64,16,128]{2,1,0:T(8,128)(2,1)S(1)}, u32[]{:S(2)}, u32[]{:S(2)}) async-start(bf16[64,16,128]{2,1,0:T(8,128)(2,1)} %get-tuple-element.12), calls=%async_computation | async-start | bytes 524288 | tf_op jit(solution)/shard_map/all_to_all | solution.py:354
  20.3 0.0 collective-permute-done.prev_in
  20.3 0.0 copy-start.2
  20.3 3.2 %collective-permute-start.1 = (bf16[2,512,512]{2,1,0:T(8,128)(2,1)}, bf16[2,512,512]{2,1,0:T(8,128)(2,1)S(1)}, u32[]{:S(2)}, u32[]{:S(2)}) collective-permute-start(bf16[2,512,512]{2,1,0:T(8,128)(2,1)} %get-tuple-element.16), channel_id=1, source_target_pairs={{0,1},{1,0},{2,3},{3,2},{4,5},{5,4},{6,7},{7,6},{8,9},{9,8},{10,11... | collective-permute-start | bytes 3145736 | tf_op jit(solution)/shard_map/ppermute | solution.py:358
  23.5 0.0 copy-done.2
  23.5 3.2 %slash.1 = f32[32,24,128]{2,1,0:T(8,128)} custom-call(bf16[128,512]{1,0:T(8,128)(2,1)} %q_in.3, bf16[128,128]{1,0:T(8,128)(2,1)} %keys_in.3, bf16[128,128]{1,0:T(8,128)(2,1)} %values_in.3, s32[1,64]{1,0:T(1,128)} %order_in.3, s32[4,64]{1,0:T(4,128)} %offsets_in.1, s32[1,32]{1,0:T(1,128)} %vert_in.3, bf16[128,256]{1,0:T(8,128)(2,1)} %copy-done.2), custom_call_target="tpu_custom_call" | custom-call | flops 20000000000 | bytes 1000000 | tf_op jit(solution)/shard_map/slash/pallas_call | solution.py:359
  26.7 1.0 %convert_element_type.2.slash = bf16[32,24,128]{2,1,0:T(8,128)(2,1)S(1)} convert(f32[32,24,128]{2,1,0:T(8,128)} %slash.1) | non-fusion elementwise | flops 98304 | bytes 589824 | tf_op jit(solution)/shard_map/convert_element_type | solution.py:378
  27.8 5.7 %all-to-all-done.recv = bf16[64,16,128]{2,1,0:T(8,128)(2,1)S(1)} async-done(((bf16[64,16,128]{2,1,0:T(8,128)(2,1)}), bf16[64,16,128]{2,1,0:T(8,128)(2,1)S(1)}, u32[]{:S(2)}, u32[]{:S(2)}) %all-to-all-start) | async-done | bytes 262176 | tf_op jit(solution)/shard_map/all_to_all | solution.py:354
  33.4 1.1 %select.1 = bf16[32,88,128]{2,1,0:T(8,128)(2,1)} custom-call(bf16[64,16,128]{2,1,0:T(8,128)(2,1)S(1)} %all-to-all-done.recv, bf16[32,24,128]{2,1,0:T(8,128)(2,1)S(1)} %convert_element_type.2.slash), custom_call_target="tpu_custom_call" | custom-call | tf_op jit(solution)/shard_map/select/pallas_call | solution.py:371
  34.6 3.9 %all-to-all-start.1 = ((bf16[32,88,128]{2,1,0:T(8,128)(2,1)}), bf16[32,88,128]{2,1,0:T(8,128)(2,1)S(1)}, u32[]{:S(2)}, u32[]{:S(2)}) async-start(bf16[32,88,128]{2,1,0:T(8,128)(2,1)} %select.1), calls=%async_computation.1 | async-start | bytes 1441792 | tf_op jit(solution)/shard_map/all_to_all | solution.py:389
  38.5 8.2 %collective-permute-done.1.near = bf16[2,512,512]{2,1,0:T(8,128)(2,1)S(1)} collective-permute-done((bf16[2,512,512]{2,1,0:T(8,128)(2,1)}, bf16[2,512,512]{2,1,0:T(8,128)(2,1)S(1)}, u32[]{:S(2)}, u32[]{:S(2)}) %collective-permute-start.1) | collective-permute-done | bytes 1048608 | tf_op jit(solution)/shard_map/ppermute | solution.py:358
  46.7 3.2 %collective-permute-start.2 = (bf16[2,512,512]{2,1,0:T(8,128)(2,1)S(1)}, bf16[2,512,512]{2,1,0:T(8,128)(2,1)S(1)}, u32[]{:S(2)}, u32[]{:S(2)}) collective-permute-start(bf16[2,512,512]{2,1,0:T(8,128)(2,1)S(1)} %collective-permute-done.1.near), channel_id=1, source_target_pairs={{0,8},{8,0},{1,9},{9,1},{2,10},{10,2},{3,11},{11,3},{4,12},{12,4},... | collective-permute-start | bytes 3145736 | tf_op jit(solution)/shard_map/ppermute | solution.py:379
  49.9 0.0 copy-start
  49.9 1.0 %copy-done = bf16[2,512,512]{2,1,0:T(8,128)(2,1)} copy-done((bf16[2,512,512]{2,1,0:T(8,128)(2,1)}, bf16[2,512,512]{2,1,0:T(8,128)(2,1)S(1)}, u32[]{:S(2)}) %copy-start) | copy-done | bytes 1048600
  50.9 1.3 %collective-permute-done.2.far = bf16[2,512,512]{2,1,0:T(8,128)(2,1)S(1)} collective-permute-done((bf16[2,512,512]{2,1,0:T(8,128)(2,1)S(1)}, bf16[2,512,512]{2,1,0:T(8,128)(2,1)S(1)}, u32[]{:S(2)}, u32[]{:S(2)}) %collective-permute-start.2) | collective-permute-done | bytes 1048608 | tf_op jit(solution)/shard_map/ppermute | solution.py:379
  52.1 0.0 copy-start.1
  52.1 1.2 %copy-done.1 = bf16[2,512,512]{2,1,0:T(8,128)(2,1)S(1)} copy-done((bf16[2,512,512]{2,1,0:T(8,128)(2,1)S(1)}, bf16[2,512,512]{2,1,0:T(8,128)(2,1)}, u32[]{:S(2)}) %copy-start.1) | copy-done | bytes 1048600
  53.4 0.1 arrange.1.weight
  53.5 5.0 %all-to-all-done.1.mine = bf16[32,88,128]{2,1,0:T(8,128)(2,1)S(1)} async-done(((bf16[32,88,128]{2,1,0:T(8,128)(2,1)}), bf16[32,88,128]{2,1,0:T(8,128)(2,1)S(1)}, u32[]{:S(2)}, u32[]{:S(2)}) %all-to-all-start.1) | async-done | bytes 720928 | tf_op jit(solution)/shard_map/all_to_all | solution.py:389
  58.5 4.4 %collective-permute-start.3 = (bf16[32,88,128]{2,1,0:T(8,128)(2,1)S(1)}, bf16[32,88,128]{2,1,0:T(8,128)(2,1)S(1)}, u32[]{:S(2)}, u32[]{:S(2)}) collective-permute-start(bf16[32,88,128]{2,1,0:T(8,128)(2,1)S(1)} %all-to-all-done.1.mine), channel_id=1, source_target_pairs={{0,8},{8,0},{1,9},{9,1},{2,10},{10,2},{3,11},{11,3},{4,12},{12,4},... | collective-permute-start | bytes 2162696 | tf_op jit(solution)/shard_map/ppermute | solution.py:391
  62.9 1.6 %half.1 = f32[512,256]{1,0:T(8,128)S(1)} custom-call(bf16[64,16,128]{2,1,0:T(8,128)(2,1)S(1)} %all-to-all-done.recv, bf16[32,88,128]{2,1,0:T(8,128)(2,1)S(1)} %all-to-all-done.1.mine), custom_call_target="tpu_custom_call" | custom-call | flops 300000000 | bytes 2000000 | tf_op jit(solution)/shard_map/half/pallas_call | solution.py:392
  64.5 0.2 collective-permute-done.3.other
  64.7 2.2 %finish.1.full = bf16[128,512]{1,0:T(8,128)(2,1)S(1)} custom-call(bf16[64,16,128]{2,1,0:T(8,128)(2,1)S(1)} %all-to-all-done.recv, bf16[32,88,128]{2,1,0:T(8,128)(2,1)S(1)} %all-to-all-done.1.mine, bf16[32,88,128]{2,1,0:T(8,128)(2,1)S(1)} %collective-permute-done.3.other, f32[512,256]{1,0:T(8,128)S(1)} %half.1), custom_call_target="tpu_custom_call" | custom-call | tf_op jit(solution)/shard_map/finish/pallas_call | solution.py:401
  66.9 3.1 %collective-permute-start.4 = (bf16[128,512]{1,0:T(8,128)(2,1)S(1)}, bf16[128,512]{1,0:T(8,128)(2,1)S(1)}, u32[]{:S(2)}, u32[]{:S(2)}) collective-permute-start(bf16[128,512]{1,0:T(8,128)(2,1)S(1)} %finish.1.full), channel_id=1, source_target_pairs={{0,1},{1,0},{2,3},{3,2},{4,5},{5,4},{6,7},{7,6},{8,9},{9,8},{10,11... | collective-permute-start | bytes 393224 | tf_op jit(solution)/shard_map/ppermute | solution.py:409
  70.1 2.0 %project_own.1.own = f32[4,128,512]{2,1,0:T(8,128)S(1)} custom-call(bf16[128,512]{1,0:T(8,128)(2,1)S(1)} %finish.1.full, bf16[512,4096]{1,0:T(8,128)(2,1)} %weight_in.3), custom_call_target="tpu_custom_call" | custom-call | flops 300000000 | bytes 8000000 | tf_op jit(solution)/shard_map/project_own/pallas_call | solution.py:410
  72.1 1.4 %collective-permute-done.4.full = bf16[128,512]{1,0:T(8,128)(2,1)S(1)} collective-permute-done((bf16[128,512]{1,0:T(8,128)(2,1)S(1)}, bf16[128,512]{1,0:T(8,128)(2,1)S(1)}, u32[]{:S(2)}, u32[]{:S(2)}) %collective-permute-start.4) | collective-permute-done | bytes 131104 | tf_op jit(solution)/shard_map/ppermute | solution.py:409
  73.5 0.4 project_both.1
  74.0 21.1 %all_to_all.15 = bf16[4,128,512]{2,1,0:T(8,128)(2,1)S(1)} all-to-all(bf16[4,128,512]{2,1,0:T(8,128)(2,1)S(1)} %project_both.1), channel_id=1, replica_groups=mesh['z'=8,'x'=4,'c'=2,'yh'=4,'yl'=2] {'yh'}, dimensions={0} | all-to-all | bytes 1048576 | tf_op jit(solution)/shard_map/all_to_all | solution.py:431
  95.0 0.7 reduce_sum.12
Async XLA Ops:
  2.6 17.7 %collective-permute-start = (bf16[128,256]{1,0:T(8,128)(2,1)}, bf16[128,256]{1,0:T(8,128)(2,1)S(1)}, u32[]{:S(2)}, u32[]{:S(2)}) collective-permute-start(bf16[128,256]{1,0:T(8,128)(2,1)} %get-tuple-element.14), channel_id=1, source_target_pairs={{0,8},{8,16},{16,24},{24,32},{32,40},{40,48},{48,56},{56,64},{64,7... | collective-permute-start | bytes 196616 | tf_op jit(solution)/shard_map/ppermute | solution.py:355
  7.1 26.3 %all-to-all-start = ((bf16[64,16,128]{2,1,0:T(8,128)(2,1)}), bf16[64,16,128]{2,1,0:T(8,128)(2,1)S(1)}, u32[]{:S(2)}, u32[]{:S(2)}) async-start(bf16[64,16,128]{2,1,0:T(8,128)(2,1)} %get-tuple-element.12), calls=%async_computation | async-start | bytes 524288 | tf_op jit(solution)/shard_map/all_to_all | solution.py:354
  20.3 3.2 %copy-start.2 = (bf16[128,256]{1,0:T(8,128)(2,1)}, bf16[128,256]{1,0:T(8,128)(2,1)S(1)}, u32[]{:S(2)}) copy-start(bf16[128,256]{1,0:T(8,128)(2,1)S(1)} %collective-permute-done.prev_in) | copy-start | bytes 196612
  20.3 26.4 %collective-permute-start.1 = (bf16[2,512,512]{2,1,0:T(8,128)(2,1)}, bf16[2,512,512]{2,1,0:T(8,128)(2,1)S(1)}, u32[]{:S(2)}, u32[]{:S(2)}) collective-permute-start(bf16[2,512,512]{2,1,0:T(8,128)(2,1)} %get-tuple-element.16), channel_id=1, source_target_pairs={{0,1},{1,0},{2,3},{3,2},{4,5},{5,4},{6,7},{7,6},{8,9},{9,8},{10,11... | collective-permute-start | bytes 3145736 | tf_op jit(solution)/shard_map/ppermute | solution.py:358
  34.6 23.9 %all-to-all-start.1 = ((bf16[32,88,128]{2,1,0:T(8,128)(2,1)}), bf16[32,88,128]{2,1,0:T(8,128)(2,1)S(1)}, u32[]{:S(2)}, u32[]{:S(2)}) async-start(bf16[32,88,128]{2,1,0:T(8,128)(2,1)} %select.1), calls=%async_computation.1 | async-start | bytes 1441792 | tf_op jit(solution)/shard_map/all_to_all | solution.py:389
  46.7 5.5 %collective-permute-start.2 = (bf16[2,512,512]{2,1,0:T(8,128)(2,1)S(1)}, bf16[2,512,512]{2,1,0:T(8,128)(2,1)S(1)}, u32[]{:S(2)}, u32[]{:S(2)}) collective-permute-start(bf16[2,512,512]{2,1,0:T(8,128)(2,1)S(1)} %collective-permute-done.1.near), channel_id=1, source_target_pairs={{0,8},{8,0},{1,9},{9,1},{2,10},{10,2},{3,11},{11,3},{4,12},{12,4},... | collective-permute-start | bytes 3145736 | tf_op jit(solution)/shard_map/ppermute | solution.py:379
  49.9 1.0 %copy-start = (bf16[2,512,512]{2,1,0:T(8,128)(2,1)}, bf16[2,512,512]{2,1,0:T(8,128)(2,1)S(1)}, u32[]{:S(2)}) copy-start(bf16[2,512,512]{2,1,0:T(8,128)(2,1)S(1)} %collective-permute-done.1.near) | copy-start | bytes 3145732
  52.1 1.2 %copy-start.1 = (bf16[2,512,512]{2,1,0:T(8,128)(2,1)S(1)}, bf16[2,512,512]{2,1,0:T(8,128)(2,1)}, u32[]{:S(2)}) copy-start(bf16[2,512,512]{2,1,0:T(8,128)(2,1)} %copy-done) | copy-start | bytes 3145732
  58.5 6.2 %collective-permute-start.3 = (bf16[32,88,128]{2,1,0:T(8,128)(2,1)S(1)}, bf16[32,88,128]{2,1,0:T(8,128)(2,1)S(1)}, u32[]{:S(2)}, u32[]{:S(2)}) collective-permute-start(bf16[32,88,128]{2,1,0:T(8,128)(2,1)S(1)} %all-to-all-done.1.mine), channel_id=1, source_target_pairs={{0,8},{8,0},{1,9},{9,1},{2,10},{10,2},{3,11},{11,3},{4,12},{12,4},... | collective-permute-start | bytes 2162696 | tf_op jit(solution)/shard_map/ppermute | solution.py:391
  66.9 6.6 %collective-permute-start.4 = (bf16[128,512]{1,0:T(8,128)(2,1)S(1)}, bf16[128,512]{1,0:T(8,128)(2,1)S(1)}, u32[]{:S(2)}, u32[]{:S(2)}) collective-permute-start(bf16[128,512]{1,0:T(8,128)(2,1)S(1)} %finish.1.full), channel_id=1, source_target_pairs={{0,1},{1,0},{2,3},{3,2},{4,5},{5,4},{6,7},{7,6},{8,9},{9,8},{10,11... | collective-permute-start | bytes 393224 | tf_op jit(solution)/shard_map/ppermute | solution.py:409

commit v9 on v8

--- a/solution.py
+++ b/solution.py
@@ -301,24 +301,24 @@
         out[:, h * HEAD : (h + 1) * HEAD] = rows_h
 
 
-def own_kernel(full, weight_in, out, weight, sems):
-    parity = lax.axis_index("yl")
+def own_kernel(full, weight_in, near, far, out, theirs, weight, sems, tsems):
+    parity, core = lax.axis_index("yl"), lax.axis_index("c")
+    share = near.shape[0]
     moves = [
         pltpu.make_async_copy(columns(weight_in, j, parity), weight.at[j], sems.at[j])
         for j in range(out.shape[0])
     ]
-    for move in moves:
+    late = [
+        pltpu.make_async_copy(part, theirs.at[pl.ds(first, share)], tsems.at[i])
+        for i, (part, first) in enumerate(((near, core * share), (far, (1 - core) * share)))
+    ]
+    for move in moves + late:
         move.start()
     for j, move in enumerate(moves):
         move.wait()
         out[j] = jnp.dot(full[...], weight[j], preferred_element_type=F32)
-
-
-def arrange_kernel(near, far, out):
-    core = lax.axis_index("c")
-    share = near.shape[0]
-    out[pl.ds(core * share, share)] = near[...]
-    out[pl.ds((1 - core) * share, share)] = far[...]
+    for move in late:
+        move.wait()
 
 
 def both_kernel(own, full, weight, out):
@@ -377,17 +377,8 @@
         compiler_params=small,
     )(recv, slash.astype(BF16))
     far = lax.ppermute(near, "c", swap)
-    theirs = pl.pallas_call(
-        arrange_kernel,
-        out_shape=jax.ShapeDtypeStruct((pairs,) + near.shape[1:], BF16),
-        in_specs=[VMEM] * 2,
-        out_specs=VMEM,
-        name="arrange",
-        compiler_params=small,
-        cost_estimate=pl.CostEstimate(flops=3000000000, bytes_accessed=4000000, transcendentals=0),
-    )(near, far)
     mine = lax.all_to_all(parts, ("z", "x"), 0, 0, tiled=True)
-    mine, theirs = lax.optimization_barrier((mine, theirs))
+    mine, far = lax.optimization_barrier((mine, far))
     other = lax.ppermute(mine, "c", swap)
     half = pl.pallas_call(
         half_kernel,
@@ -407,19 +398,23 @@
         compiler_params=pltpu.CompilerParams(vmem_limit_bytes=32 * MIB),
     )(recv, mine, other, half)
     theirs_full = lax.ppermute(full, "yl", swap)
-    own = pl.pallas_call(
+    own, theirs = pl.pallas_call(
         own_kernel,
-        out_shape=jax.ShapeDtypeStruct((pairs, rows, width), F32),
-        in_specs=[VMEM, HBM],
-        out_specs=VMEM,
+        out_shape=[
+            jax.ShapeDtypeStruct((pairs, rows, width), F32),
+            jax.ShapeDtypeStruct((pairs,) + near.shape[1:], BF16),
+        ],
+        in_specs=[VMEM, HBM, HBM, HBM],
+        out_specs=[VMEM, VMEM],
         scratch_shapes=[
             pltpu.VMEM((pairs, out_weight.shape[0], width), BF16),
             pltpu.SemaphoreType.DMA((pairs,)),
+            pltpu.SemaphoreType.DMA((2,)),
         ],
         name="project_own",
-        compiler_params=pltpu.CompilerParams(vmem_limit_bytes=52 * MIB),
+        compiler_params=pltpu.CompilerParams(vmem_limit_bytes=48 * MIB),
         cost_estimate=pl.CostEstimate(flops=300000000, bytes_accessed=8000000, transcendentals=0),
-    )(full, out_weight)
+    )(full, out_weight, near, far)
     partial = pl.pallas_call(
         both_kernel,
         out_shape=jax.ShapeDtypeStruct((pairs, rows, width), BF16),

time: 97.4 us -> 97.4 us (level)
  waiting for transfers between devices: 21.7 us -> 24.1 us
  local copies, waits for them, and re-layouts: 2.2 us -> 0.01 us
    all_to_all x1, waiting for transfers between devices: 4.95 us -> 8.58 us  [local(): mine = lax.all_to_all(parts, ('z', 'x'), 0, 0, tiled=True)]
    unnamed x6 -> x2, local copies, waits for them, and re-layouts: 2.2 us -> 0.01 us
    ppermute x1, waiting for transfers between devices: 1.29 us -> 0.01 us  [local(): far = lax.ppermute(near, 'c', swap)]
    pallas_call x2 -> x1, Pallas kernels: 2.17 us -> 2.05 us  [local(): pl.pallas_call(own_kernel, out_shape=[jax.ShapeDtypeStruct((pairs, rows,...]
  transfers between devices with their start and end apart: 7 -> 7, of which waited for: 6 -> 5; matrix products, arithmetic and copies ran while one was open for 1% -> 1% of each run, Pallas kernels for 8% -> 8%
where the time goes in v9:
time: 97.4 us; the launch traced here: 95.8 us
  starting transfers between devices  35.5 us (36%)
  waiting for transfers between devices  24.1 us (25%)
  blocking collectives  21 us (22%)
  Pallas kernels  13.2 us (14%)
  other arithmetic  1.77 us (2%)
    all_to_all x1, blocking collectives, local(): sums = lax.all_to_all(partial, 'yh', 0, 0, tiled=True)  21 us
    all_to_all x1, starting transfers between devices, local(): recv = lax.all_to_all(packed, CTX, 0, 0, tiled=True)  13.2 us
    all_to_all x1, waiting for transfers between devices, local(): mine = lax.all_to_all(parts, ('z', 'x'), 0, 0, tiled=True)  8.58 us
    ppermute x1, waiting for transfers between devices, local(): near = lax.ppermute(sent, 'yl', swap)  8.19 us
    all_to_all x1, waiting for transfers between devices, local(): recv = lax.all_to_all(packed, CTX, 0, 0, tiled=True)  5.66 us
    ppermute x1, starting transfers between devices, local(): prev = lax.ppermute(kv, CTX, [(i, i + 1) for i in range(n_ctx - 1)])  4.51 us
    ppermute x1, starting transfers between devices, local(): other = lax.ppermute(mine, 'c', swap)  4.43 us
    all_to_all x1, starting transfers between devices, local(): mine = lax.all_to_all(parts, ('z', 'x'), 0, 0, tiled=True)  3.9 us
  transfers between devices with their start and end apart: 7, of which 5 were waited for; matrix products, arithmetic and copies ran while one was open for 1% of the time, Pallas kernels for 8%

profile of v9, /device:TPU:1, one launch (start us, length us, event | category | flops | bytes accessed | tf_op | source)
XLA Modules:
  0.0 95.8 jit_solution(8427172825873421770)
XLA Ops:
  0.0 2.6 %pack.1 = (bf16[64,16,128]{2,1,0:T(8,128)(2,1)}, bf16[128,256]{1,0:T(8,128)(2,1)}, bf16[2,512,512]{2,1,0:T(8,128)(2,1)}) custom-call(bf16[128,512]{1,0:T(8,128)(2,1)} %q_in.3, bf16[128,128]{1,0:T(8,128)(2,1)} %keys_in.3, bf16[128,128]{1,0:T(8,128)(2,1)} %values_in.3, s32[1,64]{1,0:T(1,128)} %order_in.3, s32[1,32]{1,0:T(1,128)} %vert_in.3, ...), custom_call_target="tpu_custom_call" | custom-call | tf_op jit(solution)/shard_map/pack/pallas_call | solution.py:341
  2.6 4.5 %collective-permute-start = (bf16[128,256]{1,0:T(8,128)(2,1)}, bf16[128,256]{1,0:T(8,128)(2,1)S(1)}, u32[]{:S(2)}, u32[]{:S(2)}) collective-permute-start(bf16[128,256]{1,0:T(8,128)(2,1)} %get-tuple-element.16), channel_id=1, source_target_pairs={{0,8},{8,16},{16,24},{24,32},{32,40},{40,48},{48,56},{56,64},{64,7... | collective-permute-start | bytes 196616 | tf_op jit(solution)/shard_map/ppermute | solution.py:355
  7.1 13.2 %all-to-all-start = ((bf16[64,16,128]{2,1,0:T(8,128)(2,1)}), bf16[64,16,128]{2,1,0:T(8,128)(2,1)S(1)}, u32[]{:S(2)}, u32[]{:S(2)}) async-start(bf16[64,16,128]{2,1,0:T(8,128)(2,1)} %get-tuple-element.14), calls=%async_computation | async-start | bytes 524288 | tf_op jit(solution)/shard_map/all_to_all | solution.py:354
  20.3 0.0 collective-permute-done.prev_in
  20.3 0.0 copy-start
  20.3 3.2 %collective-permute-start.1 = (bf16[2,512,512]{2,1,0:T(8,128)(2,1)}, bf16[2,512,512]{2,1,0:T(8,128)(2,1)S(1)}, u32[]{:S(2)}, u32[]{:S(2)}) collective-permute-start(bf16[2,512,512]{2,1,0:T(8,128)(2,1)} %get-tuple-element.18), channel_id=1, source_target_pairs={{0,1},{1,0},{2,3},{3,2},{4,5},{5,4},{6,7},{7,6},{8,9},{9,8},{10,11... | collective-permute-start | bytes 3145736 | tf_op jit(solution)/shard_map/ppermute | solution.py:358
  23.5 0.0 copy-done
  23.5 3.2 %slash.1 = f32[32,24,128]{2,1,0:T(8,128)} custom-call(bf16[128,512]{1,0:T(8,128)(2,1)} %q_in.3, bf16[128,128]{1,0:T(8,128)(2,1)} %keys_in.3, bf16[128,128]{1,0:T(8,128)(2,1)} %values_in.3, s32[1,64]{1,0:T(1,128)} %order_in.3, s32[4,64]{1,0:T(4,128)} %offsets_in.1, s32[1,32]{1,0:T(1,128)} %vert_in.3, bf16[128,256]{1,0:T(8,128)(2,1)} %copy-done), custom_call_target="tpu_custom_call" | custom-call | flops 20000000000 | bytes 1000000 | tf_op jit(solution)/shard_map/slash/pallas_call | solution.py:359
  26.7 1.0 %convert_element_type.2.slash = bf16[32,24,128]{2,1,0:T(8,128)(2,1)S(1)} convert(f32[32,24,128]{2,1,0:T(8,128)} %slash.1) | non-fusion elementwise | flops 98304 | bytes 589824 | tf_op jit(solution)/shard_map/convert_element_type | solution.py:378
  27.8 5.7 %all-to-all-done.recv = bf16[64,16,128]{2,1,0:T(8,128)(2,1)S(1)} async-done(((bf16[64,16,128]{2,1,0:T(8,128)(2,1)}), bf16[64,16,128]{2,1,0:T(8,128)(2,1)S(1)}, u32[]{:S(2)}, u32[]{:S(2)}) %all-to-all-start) | async-done | bytes 262176 | tf_op jit(solution)/shard_map/all_to_all | solution.py:354
  33.4 1.1 %select.1 = bf16[32,88,128]{2,1,0:T(8,128)(2,1)} custom-call(bf16[64,16,128]{2,1,0:T(8,128)(2,1)S(1)} %all-to-all-done.recv, bf16[32,24,128]{2,1,0:T(8,128)(2,1)S(1)} %convert_element_type.2.slash), custom_call_target="tpu_custom_call" | custom-call | tf_op jit(solution)/shard_map/select/pallas_call | solution.py:371
  34.6 3.9 %all-to-all-start.1 = ((bf16[32,88,128]{2,1,0:T(8,128)(2,1)}), bf16[32,88,128]{2,1,0:T(8,128)(2,1)S(1)}, u32[]{:S(2)}, u32[]{:S(2)}) async-start(bf16[32,88,128]{2,1,0:T(8,128)(2,1)} %select.1), calls=%async_computation.1 | async-start | bytes 1441792 | tf_op jit(solution)/shard_map/all_to_all | solution.py:380
  38.5 8.2 %collective-permute-done.1.near = bf16[2,512,512]{2,1,0:T(8,128)(2,1)S(1)} collective-permute-done((bf16[2,512,512]{2,1,0:T(8,128)(2,1)}, bf16[2,512,512]{2,1,0:T(8,128)(2,1)S(1)}, u32[]{:S(2)}, u32[]{:S(2)}) %collective-permute-start.1) | collective-permute-done | bytes 1048608 | tf_op jit(solution)/shard_map/ppermute | solution.py:358
  46.7 3.2 %collective-permute-start.2 = (bf16[2,512,512]{2,1,0:T(8,128)(2,1)S(1)}, bf16[2,512,512]{2,1,0:T(8,128)(2,1)S(1)}, u32[]{:S(2)}, u32[]{:S(2)}) collective-permute-start(bf16[2,512,512]{2,1,0:T(8,128)(2,1)S(1)} %collective-permute-done.1.near), channel_id=1, source_target_pairs={{0,8},{8,0},{1,9},{9,1},{2,10},{10,2},{3,11},{11,3},{4,12},{12,4},... | collective-permute-start | bytes 3145736 | tf_op jit(solution)/shard_map/ppermute | solution.py:379
  49.9 8.6 %all-to-all-done.1.mine = bf16[32,88,128]{2,1,0:T(8,128)(2,1)S(1)} async-done(((bf16[32,88,128]{2,1,0:T(8,128)(2,1)}), bf16[32,88,128]{2,1,0:T(8,128)(2,1)S(1)}, u32[]{:S(2)}, u32[]{:S(2)}) %all-to-all-start.1) | async-done | bytes 720928 | tf_op jit(solution)/shard_map/all_to_all | solution.py:380
  58.4 0.0 collective-permute-done.2.far
  58.5 4.4 %collective-permute-start.3 = (bf16[32,88,128]{2,1,0:T(8,128)(2,1)S(1)}, bf16[32,88,128]{2,1,0:T(8,128)(2,1)S(1)}, u32[]{:S(2)}, u32[]{:S(2)}) collective-permute-start(bf16[32,88,128]{2,1,0:T(8,128)(2,1)S(1)} %all-to-all-done.1.mine), channel_id=1, source_target_pairs={{0,8},{8,0},{1,9},{9,1},{2,10},{10,2},{3,11},{11,3},{4,12},{12,4},... | collective-permute-start | bytes 2162696 | tf_op jit(solution)/shard_map/ppermute | solution.py:382
  62.9 1.6 %half.1 = f32[512,256]{1,0:T(8,128)S(1)} custom-call(bf16[64,16,128]{2,1,0:T(8,128)(2,1)S(1)} %all-to-all-done.recv, bf16[32,88,128]{2,1,0:T(8,128)(2,1)S(1)} %all-to-all-done.1.mine), custom_call_target="tpu_custom_call" | custom-call | flops 300000000 | bytes 2000000 | tf_op jit(solution)/shard_map/half/pallas_call | solution.py:383
  64.5 0.2 collective-permute-done.3.other
  64.7 2.2 %finish.1.full = bf16[128,512]{1,0:T(8,128)(2,1)S(1)} custom-call(bf16[64,16,128]{2,1,0:T(8,128)(2,1)S(1)} %all-to-all-done.recv, bf16[32,88,128]{2,1,0:T(8,128)(2,1)S(1)} %all-to-all-done.1.mine, bf16[32,88,128]{2,1,0:T(8,128)(2,1)S(1)} %collective-permute-done.3.other, f32[512,256]{1,0:T(8,128)S(1)} %half.1), custom_call_target="tpu_custom_call" | custom-call | tf_op jit(solution)/shard_map/finish/pallas_call | solution.py:392
  66.9 3.1 %collective-permute-start.4 = (bf16[128,512]{1,0:T(8,128)(2,1)S(1)}, bf16[128,512]{1,0:T(8,128)(2,1)S(1)}, u32[]{:S(2)}, u32[]{:S(2)}) collective-permute-start(bf16[128,512]{1,0:T(8,128)(2,1)S(1)} %finish.1.full), channel_id=1, source_target_pairs={{0,1},{1,0},{2,3},{3,2},{4,5},{5,4},{6,7},{7,6},{8,9},{9,8},{10,11... | collective-permute-start | bytes 393224 | tf_op jit(solution)/shard_map/ppermute | solution.py:400
  70.1 2.0 %project_own.1 = (f32[4,128,512]{2,1,0:T(8,128)S(1)}, bf16[4,512,512]{2,1,0:T(8,128)(2,1)S(1)}) custom-call(bf16[128,512]{1,0:T(8,128)(2,1)S(1)} %finish.1.full, bf16[512,4096]{1,0:T(8,128)(2,1)} %weight_in.3, bf16[2,512,512]{2,1,0:T(8,128)(2,1)S(1)} %collective-permute-done.1.near, bf16[2,512,512]{2,1,0:T(8,128)(2,1)S(1)} %collective-permute-done.2.far), custom_call_target="tpu_custom_call" | custom-call | flops 300000000 | bytes 8000000 | tf_op jit(solution)/shard_map/project_own/pallas_call | solution.py:401
  72.1 1.4 %collective-permute-done.4.full = bf16[128,512]{1,0:T(8,128)(2,1)S(1)} collective-permute-done((bf16[128,512]{1,0:T(8,128)(2,1)S(1)}, bf16[128,512]{1,0:T(8,128)(2,1)S(1)}, u32[]{:S(2)}, u32[]{:S(2)}) %collective-permute-start.4) | collective-permute-done | bytes 131104 | tf_op jit(solution)/shard_map/ppermute | solution.py:400
  73.5 0.4 project_both.1
  74.0 21.0 %all_to_all.15 = bf16[4,128,512]{2,1,0:T(8,128)(2,1)S(1)} all-to-all(bf16[4,128,512]{2,1,0:T(8,128)(2,1)S(1)} %project_both.1), channel_id=1, replica_groups=mesh['z'=8,'x'=4,'c'=2,'yh'=4,'yl'=2] {'yh'}, dimensions={0} | all-to-all | bytes 1048576 | tf_op jit(solution)/shard_map/all_to_all | solution.py:426
  95.0 0.7 reduce_sum.12
Async XLA Ops:
  2.6 17.7 %collective-permute-start = (bf16[128,256]{1,0:T(8,128)(2,1)}, bf16[128,256]{1,0:T(8,128)(2,1)S(1)}, u32[]{:S(2)}, u32[]{:S(2)}) collective-permute-start(bf16[128,256]{1,0:T(8,128)(2,1)} %get-tuple-element.16), channel_id=1, source_target_pairs={{0,8},{8,16},{16,24},{24,32},{32,40},{40,48},{48,56},{56,64},{64,7... | collective-permute-start | bytes 196616 | tf_op jit(solution)/shard_map/ppermute | solution.py:355
  7.1 26.3 %all-to-all-start = ((bf16[64,16,128]{2,1,0:T(8,128)(2,1)}), bf16[64,16,128]{2,1,0:T(8,128)(2,1)S(1)}, u32[]{:S(2)}, u32[]{:S(2)}) async-start(bf16[64,16,128]{2,1,0:T(8,128)(2,1)} %get-tuple-element.14), calls=%async_computation | async-start | bytes 524288 | tf_op jit(solution)/shard_map/all_to_all | solution.py:354
  20.3 3.2 %copy-start = (bf16[128,256]{1,0:T(8,128)(2,1)}, bf16[128,256]{1,0:T(8,128)(2,1)S(1)}, u32[]{:S(2)}) copy-start(bf16[128,256]{1,0:T(8,128)(2,1)S(1)} %collective-permute-done.prev_in) | copy-start | bytes 196612
  20.3 26.4 %collective-permute-start.1 = (bf16[2,512,512]{2,1,0:T(8,128)(2,1)}, bf16[2,512,512]{2,1,0:T(8,128)(2,1)S(1)}, u32[]{:S(2)}, u32[]{:S(2)}) collective-permute-start(bf16[2,512,512]{2,1,0:T(8,128)(2,1)} %get-tuple-element.18), channel_id=1, source_target_pairs={{0,1},{1,0},{2,3},{3,2},{4,5},{5,4},{6,7},{7,6},{8,9},{9,8},{10,11... | collective-permute-start | bytes 3145736 | tf_op jit(solution)/shard_map/ppermute | solution.py:358
  34.6 23.9 %all-to-all-start.1 = ((bf16[32,88,128]{2,1,0:T(8,128)(2,1)}), bf16[32,88,128]{2,1,0:T(8,128)(2,1)S(1)}, u32[]{:S(2)}, u32[]{:S(2)}) async-start(bf16[32,88,128]{2,1,0:T(8,128)(2,1)} %select.1), calls=%async_computation.1 | async-start | bytes 1441792 | tf_op jit(solution)/shard_map/all_to_all | solution.py:380
  46.7 11.8 %collective-permute-start.2 = (bf16[2,512,512]{2,1,0:T(8,128)(2,1)S(1)}, bf16[2,512,512]{2,1,0:T(8,128)(2,1)S(1)}, u32[]{:S(2)}, u32[]{:S(2)}) collective-permute-start(bf16[2,512,512]{2,1,0:T(8,128)(2,1)S(1)} %collective-permute-done.1.near), channel_id=1, source_target_pairs={{0,8},{8,0},{1,9},{9,1},{2,10},{10,2},{3,11},{11,3},{4,12},{12,4},... | collective-permute-start | bytes 3145736 | tf_op jit(solution)/shard_map/ppermute | solution.py:379
  58.5 6.2 %collective-permute-start.3 = (bf16[32,88,128]{2,1,0:T(8,128)(2,1)S(1)}, bf16[32,88,128]{2,1,0:T(8,128)(2,1)S(1)}, u32[]{:S(2)}, u32[]{:S(2)}) collective-permute-start(bf16[32,88,128]{2,1,0:T(8,128)(2,1)S(1)} %all-to-all-done.1.mine), channel_id=1, source_target_pairs={{0,8},{8,0},{1,9},{9,1},{2,10},{10,2},{3,11},{11,3},{4,12},{12,4},... | collective-permute-start | bytes 2162696 | tf_op jit(solution)/shard_map/ppermute | solution.py:382
  66.9 6.6 %collective-permute-start.4 = (bf16[128,512]{1,0:T(8,128)(2,1)S(1)}, bf16[128,512]{1,0:T(8,128)(2,1)S(1)}, u32[]{:S(2)}, u32[]{:S(2)}) collective-permute-start(bf16[128,512]{1,0:T(8,128)(2,1)S(1)} %finish.1.full), channel_id=1, source_target_pairs={{0,1},{1,0},{2,3},{3,2},{4,5},{5,4},{6,7},{7,6},{8,9},{9,8},{10,11... | collective-permute-start | bytes 393224 | tf_op jit(solution)/shard_map/ppermute | solution.py:400

commit v10 on v9

--- a/solution.py
+++ b/solution.py
@@ -303,14 +303,20 @@
 
 def own_kernel(full, weight_in, near, far, out, theirs, weight, sems, tsems):
     parity, core = lax.axis_index("yl"), lax.axis_index("c")
-    share = near.shape[0]
+    pair = lax.axis_index("yh")
+    share, pairs = near.shape[0], out.shape[0]
     moves = [
-        pltpu.make_async_copy(columns(weight_in, j, parity), weight.at[j], sems.at[j])
-        for j in range(out.shape[0])
+        pltpu.make_async_copy(
+            columns(weight_in, lax.rem(pair + d, pairs), parity), weight.at[d], sems.at[d]
+        )
+        for d in range(pairs)
     ]
     late = [
-        pltpu.make_async_copy(part, theirs.at[pl.ds(first, share)], tsems.at[i])
-        for i, (part, first) in enumerate(((near, core * share), (far, (1 - core) * share)))
+        pltpu.make_async_copy(
+            part.at[i], theirs.at[lax.rem(first + i + pairs - pair, pairs)], tsems.at[n * share + i]
+        )
+        for n, (part, first) in enumerate(((near, core * share), (far, (1 - core) * share)))
+        for i in range(share)
     ]
     for move in moves + late:
         move.start()
@@ -321,10 +327,10 @@
         move.wait()
 
 
-def both_kernel(own, full, weight, out):
-    for j in range(out.shape[0]):
-        part = own[j] + jnp.dot(full[...], weight[j], preferred_element_type=F32)
-        out[j] = part.astype(BF16)
+def both_kernel(own, full, weight, *outs):
+    for d, out in enumerate(outs):
+        part = own[d] + jnp.dot(full[...], weight[d], preferred_element_type=F32)
+        out[...] = part.astype(BF16)
 
 
 def local(queries, keys, values, vertical, offsets, send_order, out_weight):
@@ -409,7 +415,7 @@
         scratch_shapes=[
             pltpu.VMEM((pairs, out_weight.shape[0], width), BF16),
             pltpu.SemaphoreType.DMA((pairs,)),
-            pltpu.SemaphoreType.DMA((2,)),
+            pltpu.SemaphoreType.DMA((pairs,)),
         ],
         name="project_own",
         compiler_params=pltpu.CompilerParams(vmem_limit_bytes=48 * MIB),
@@ -417,14 +423,17 @@
     )(full, out_weight, near, far)
     partial = pl.pallas_call(
         both_kernel,
-        out_shape=jax.ShapeDtypeStruct((pairs, rows, width), BF16),
+        out_shape=[jax.ShapeDtypeStruct((rows, width), BF16)] * pairs,
         in_specs=[VMEM] * 3,
-        out_specs=VMEM,
+        out_specs=[VMEM] * pairs,
         name="project_both",
         compiler_params=pltpu.CompilerParams(vmem_limit_bytes=32 * MIB),
     )(own, theirs_full, theirs)
-    sums = lax.all_to_all(partial, "yh", 0, 0, tiled=True)
-    return jnp.sum(sums.astype(F32), axis=0).astype(BF16)
+    total = partial[0].astype(F32)
+    for d in range(1, pairs):
+        route = [(p, (p + d) % pairs) for p in range(pairs)]
+        total = total + lax.ppermute(partial[d], "yh", route).astype(F32)
+    return total.astype(BF16)
 
 
 def solution(mesh):

time: 97.4 us -> 98.6 us (1.012); the launches traced: 95.8 us -> 98 us
  blocking collectives: 21 us -> 0 us
  starting transfers between devices: 35.5 us -> 50.3 us
  waiting for transfers between devices: 24.1 us -> 32.6 us
    all_to_all x1 -> x0, blocking collectives: 21 us -> none  [local(): sums = lax.all_to_all(partial, 'yh', 0, 0, tiled=True)]
    ppermute x0 -> x3, starting transfers between devices: none -> 14.8 us  [local(): total = total + lax.ppermute(partial[d], 'yh', route).astype(F32)]
    ppermute x0 -> x3, waiting for transfers between devices: none -> 8.52 us  [local(): total = total + lax.ppermute(partial[d], 'yh', route).astype(F32)]
  transfers between devices with their start and end apart: 7 -> 10, of which waited for: 5 -> 7; matrix products, arithmetic and copies ran while one was open for 1% -> 1% of each run, Pallas kernels for 8% -> 8%
where the time goes in v10:
time: 98.6 us; the launch traced here: 98 us
  starting transfers between devices  50.3 us (51%)
  waiting for transfers between devices  32.6 us (33%)
  Pallas kernels  13.3 us (13%)
  other arithmetic  1.75 us (2%)
    ppermute x3, starting transfers between devices, local(): total = total + lax.ppermute(partial[d], 'yh', route).astype(F32)  14.8 us
    all_to_all x1, starting transfers between devices, local(): recv = lax.all_to_all(packed, CTX, 0, 0, tiled=True)  13.2 us
    all_to_all x1, waiting for transfers between devices, local(): mine = lax.all_to_all(parts, ('z', 'x'), 0, 0, tiled=True)  8.6 us
    ppermute x3, waiting for transfers between devices, local(): total = total + lax.ppermute(partial[d], 'yh', route).astype(F32)  8.52 us
    ppermute x1, waiting for transfers between devices, local(): near = lax.ppermute(sent, 'yl', swap)  8.18 us
    all_to_all x1, waiting for transfers between devices, local(): recv = lax.all_to_all(packed, CTX, 0, 0, tiled=True)  5.66 us
    ppermute x1, starting transfers between devices, local(): prev = lax.ppermute(kv, CTX, [(i, i + 1) for i in range(n_ctx - 1)])  4.51 us
    ppermute x1, starting transfers between devices, local(): other = lax.ppermute(mine, 'c', swap)  4.4 us
  transfers between devices with their start and end apart: 10, of which 7 were waited for; matrix products, arithmetic and copies ran while one was open for 1% of the time, Pallas kernels for 8%

profile of v10, /device:TPU:1, one launch (start us, length us, event | category | flops | bytes accessed | tf_op | source)
XLA Modules:
  0.0 98.0 jit_solution(97143319029568368)
XLA Ops:
  0.0 2.6 %pack.1 = (bf16[64,16,128]{2,1,0:T(8,128)(2,1)}, bf16[128,256]{1,0:T(8,128)(2,1)}, bf16[2,512,512]{2,1,0:T(8,128)(2,1)}) custom-call(bf16[128,512]{1,0:T(8,128)(2,1)} %q_in.3, bf16[128,128]{1,0:T(8,128)(2,1)} %keys_in.3, bf16[128,128]{1,0:T(8,128)(2,1)} %values_in.3, s32[1,64]{1,0:T(1,128)} %order_in.3, s32[1,32]{1,0:T(1,128)} %vert_in.3, ...), custom_call_target="tpu_custom_call" | custom-call | tf_op jit(solution)/shard_map/pack/pallas_call | solution.py:347
  2.6 4.5 %collective-permute-start = (bf16[128,256]{1,0:T(8,128)(2,1)}, bf16[128,256]{1,0:T(8,128)(2,1)S(1)}, u32[]{:S(2)}, u32[]{:S(2)}) collective-permute-start(bf16[128,256]{1,0:T(8,128)(2,1)} %get-tuple-element.20), channel_id=1, source_target_pairs={{0,8},{8,16},{16,24},{24,32},{32,40},{40,48},{48,56},{56,64},{64,7... | collective-permute-start | bytes 196616 | tf_op jit(solution)/shard_map/ppermute | solution.py:361
  7.1 13.2 %all-to-all-start = ((bf16[64,16,128]{2,1,0:T(8,128)(2,1)}), bf16[64,16,128]{2,1,0:T(8,128)(2,1)S(1)}, u32[]{:S(2)}, u32[]{:S(2)}) async-start(bf16[64,16,128]{2,1,0:T(8,128)(2,1)} %get-tuple-element.18), calls=%async_computation | async-start | bytes 524288 | tf_op jit(solution)/shard_map/all_to_all | solution.py:360
  20.3 0.0 collective-permute-done.prev_in
  20.3 0.0 copy-start
  20.3 3.2 %collective-permute-start.1 = (bf16[2,512,512]{2,1,0:T(8,128)(2,1)}, bf16[2,512,512]{2,1,0:T(8,128)(2,1)S(1)}, u32[]{:S(2)}, u32[]{:S(2)}) collective-permute-start(bf16[2,512,512]{2,1,0:T(8,128)(2,1)} %get-tuple-element.22), channel_id=1, source_target_pairs={{0,1},{1,0},{2,3},{3,2},{4,5},{5,4},{6,7},{7,6},{8,9},{9,8},{10,11... | collective-permute-start | bytes 3145736 | tf_op jit(solution)/shard_map/ppermute | solution.py:364
  23.5 0.0 copy-done
  23.5 3.2 %slash.1 = f32[32,24,128]{2,1,0:T(8,128)} custom-call(bf16[128,512]{1,0:T(8,128)(2,1)} %q_in.3, bf16[128,128]{1,0:T(8,128)(2,1)} %keys_in.3, bf16[128,128]{1,0:T(8,128)(2,1)} %values_in.3, s32[1,64]{1,0:T(1,128)} %order_in.3, s32[4,64]{1,0:T(4,128)} %offsets_in.1, s32[1,32]{1,0:T(1,128)} %vert_in.3, bf16[128,256]{1,0:T(8,128)(2,1)} %copy-done), custom_call_target="tpu_custom_call" | custom-call | flops 20000000000 | bytes 1000000 | tf_op jit(solution)/shard_map/slash/pallas_call | solution.py:365
  26.7 1.0 %convert_element_type.18.slash = bf16[32,24,128]{2,1,0:T(8,128)(2,1)S(1)} convert(f32[32,24,128]{2,1,0:T(8,128)} %slash.1) | non-fusion elementwise | flops 98304 | bytes 589824 | tf_op jit(solution)/shard_map/convert_element_type | solution.py:384
  27.8 5.7 %all-to-all-done.recv = bf16[64,16,128]{2,1,0:T(8,128)(2,1)S(1)} async-done(((bf16[64,16,128]{2,1,0:T(8,128)(2,1)}), bf16[64,16,128]{2,1,0:T(8,128)(2,1)S(1)}, u32[]{:S(2)}, u32[]{:S(2)}) %all-to-all-start) | async-done | bytes 262176 | tf_op jit(solution)/shard_map/all_to_all | solution.py:360
  33.4 1.2 %select.1 = bf16[32,88,128]{2,1,0:T(8,128)(2,1)} custom-call(bf16[64,16,128]{2,1,0:T(8,128)(2,1)S(1)} %all-to-all-done.recv, bf16[32,24,128]{2,1,0:T(8,128)(2,1)S(1)} %convert_element_type.18.slash), custom_call_target="tpu_custom_call" | custom-call | tf_op jit(solution)/shard_map/select/pallas_call | solution.py:377
  34.6 3.9 %all-to-all-start.1 = ((bf16[32,88,128]{2,1,0:T(8,128)(2,1)}), bf16[32,88,128]{2,1,0:T(8,128)(2,1)S(1)}, u32[]{:S(2)}, u32[]{:S(2)}) async-start(bf16[32,88,128]{2,1,0:T(8,128)(2,1)} %select.1), calls=%async_computation.1 | async-start | bytes 1441792 | tf_op jit(solution)/shard_map/all_to_all | solution.py:386
  38.5 8.2 %collective-permute-done.1.near = bf16[2,512,512]{2,1,0:T(8,128)(2,1)S(1)} collective-permute-done((bf16[2,512,512]{2,1,0:T(8,128)(2,1)}, bf16[2,512,512]{2,1,0:T(8,128)(2,1)S(1)}, u32[]{:S(2)}, u32[]{:S(2)}) %collective-permute-start.1) | collective-permute-done | bytes 1048608 | tf_op jit(solution)/shard_map/ppermute | solution.py:364
  46.7 3.2 %collective-permute-start.2 = (bf16[2,512,512]{2,1,0:T(8,128)(2,1)S(1)}, bf16[2,512,512]{2,1,0:T(8,128)(2,1)S(1)}, u32[]{:S(2)}, u32[]{:S(2)}) collective-permute-start(bf16[2,512,512]{2,1,0:T(8,128)(2,1)S(1)} %collective-permute-done.1.near), channel_id=1, source_target_pairs={{0,8},{8,0},{1,9},{9,1},{2,10},{10,2},{3,11},{11,3},{4,12},{12,4},... | collective-permute-start | bytes 3145736 | tf_op jit(solution)/shard_map/ppermute | solution.py:385
  49.9 8.6 %all-to-all-done.1.mine = bf16[32,88,128]{2,1,0:T(8,128)(2,1)S(1)} async-done(((bf16[32,88,128]{2,1,0:T(8,128)(2,1)}), bf16[32,88,128]{2,1,0:T(8,128)(2,1)S(1)}, u32[]{:S(2)}, u32[]{:S(2)}) %all-to-all-start.1) | async-done | bytes 720928 | tf_op jit(solution)/shard_map/all_to_all | solution.py:386
  58.5 0.0 collective-permute-done.2.far
  58.5 4.4 %collective-permute-start.3 = (bf16[32,88,128]{2,1,0:T(8,128)(2,1)S(1)}, bf16[32,88,128]{2,1,0:T(8,128)(2,1)S(1)}, u32[]{:S(2)}, u32[]{:S(2)}) collective-permute-start(bf16[32,88,128]{2,1,0:T(8,128)(2,1)S(1)} %all-to-all-done.1.mine), channel_id=1, source_target_pairs={{0,8},{8,0},{1,9},{9,1},{2,10},{10,2},{3,11},{11,3},{4,12},{12,4},... | collective-permute-start | bytes 2162696 | tf_op jit(solution)/shard_map/ppermute | solution.py:388
  62.9 1.6 %half.1 = f32[512,256]{1,0:T(8,128)S(1)} custom-call(bf16[64,16,128]{2,1,0:T(8,128)(2,1)S(1)} %all-to-all-done.recv, bf16[32,88,128]{2,1,0:T(8,128)(2,1)S(1)} %all-to-all-done.1.mine), custom_call_target="tpu_custom_call" | custom-call | flops 300000000 | bytes 2000000 | tf_op jit(solution)/shard_map/half/pallas_call | solution.py:389
  64.5 0.2 collective-permute-done.3.other
  64.7 2.2 %finish.1.full = bf16[128,512]{1,0:T(8,128)(2,1)S(1)} custom-call(bf16[64,16,128]{2,1,0:T(8,128)(2,1)S(1)} %all-to-all-done.recv, bf16[32,88,128]{2,1,0:T(8,128)(2,1)S(1)} %all-to-all-done.1.mine, bf16[32,88,128]{2,1,0:T(8,128)(2,1)S(1)} %collective-permute-done.3.other, f32[512,256]{1,0:T(8,128)S(1)} %half.1), custom_call_target="tpu_custom_call" | custom-call | tf_op jit(solution)/shard_map/finish/pallas_call | solution.py:398
  66.9 3.1 %collective-permute-start.4 = (bf16[128,512]{1,0:T(8,128)(2,1)S(1)}, bf16[128,512]{1,0:T(8,128)(2,1)S(1)}, u32[]{:S(2)}, u32[]{:S(2)}) collective-permute-start(bf16[128,512]{1,0:T(8,128)(2,1)S(1)} %finish.1.full), channel_id=1, source_target_pairs={{0,1},{1,0},{2,3},{3,2},{4,5},{5,4},{6,7},{7,6},{8,9},{9,8},{10,11... | collective-permute-start | bytes 393224 | tf_op jit(solution)/shard_map/ppermute | solution.py:406
  70.1 2.1 %project_own.1 = (f32[4,128,512]{2,1,0:T(8,128)S(1)}, bf16[4,512,512]{2,1,0:T(8,128)(2,1)S(1)}) custom-call(bf16[128,512]{1,0:T(8,128)(2,1)S(1)} %finish.1.full, bf16[512,4096]{1,0:T(8,128)(2,1)} %weight_in.3, bf16[2,512,512]{2,1,0:T(8,128)(2,1)S(1)} %collective-permute-done.1.near, bf16[2,512,512]{2,1,0:T(8,128)(2,1)S(1)} %collective-permute-done.2.far), custom_call_target="tpu_custom_call" | custom-call | flops 300000000 | bytes 8000000 | tf_op jit(solution)/shard_map/project_own/pallas_call | solution.py:407
  72.2 1.4 %collective-permute-done.4.full = bf16[128,512]{1,0:T(8,128)(2,1)S(1)} collective-permute-done((bf16[128,512]{1,0:T(8,128)(2,1)S(1)}, bf16[128,512]{1,0:T(8,128)(2,1)S(1)}, u32[]{:S(2)}, u32[]{:S(2)}) %collective-permute-start.4) | collective-permute-done | bytes 131104 | tf_op jit(solution)/shard_map/ppermute | solution.py:406
  73.5 0.4 project_both.1
  74.0 4.2 %collective-permute-start.5 = (bf16[128,512]{1,0:T(8,128)(2,1)S(1)}, bf16[128,512]{1,0:T(8,128)(2,1)S(1)}, u32[]{:S(2)}, u32[]{:S(2)}) collective-permute-start(bf16[128,512]{1,0:T(8,128)(2,1)S(1)} %get-tuple-element.28), channel_id=1, source_target_pairs={{0,2},{2,4},{4,6},{6,0},{1,3},{3,5},{5,7},{7,1},{8,10},{10,12},{12... | collective-permute-start | bytes 393224 | tf_op jit(solution)/shard_map/ppermute | solution.py:435
  78.2 5.6 %collective-permute-start.6 = (bf16[128,512]{1,0:T(8,128)(2,1)S(1)}, bf16[128,512]{1,0:T(8,128)(2,1)S(1)}, u32[]{:S(2)}, u32[]{:S(2)}) collective-permute-start(bf16[128,512]{1,0:T(8,128)(2,1)S(1)} %get-tuple-element.29), channel_id=1, source_target_pairs={{0,4},{2,6},{4,0},{6,2},{1,5},{3,7},{5,1},{7,3},{8,12},{10,14},{12... | collective-permute-start | bytes 393224 | tf_op jit(solution)/shard_map/ppermute | solution.py:435
  83.8 5.0 %collective-permute-start.7 = (bf16[128,512]{1,0:T(8,128)(2,1)S(1)}, bf16[128,512]{1,0:T(8,128)(2,1)S(1)}, u32[]{:S(2)}, u32[]{:S(2)}) collective-permute-start(bf16[128,512]{1,0:T(8,128)(2,1)S(1)} %get-tuple-element.30), channel_id=1, source_target_pairs={{0,6},{2,0},{4,2},{6,4},{1,7},{3,1},{5,3},{7,5},{8,14},{10,8},{12,... | collective-permute-start | bytes 393224 | tf_op jit(solution)/shard_map/ppermute | solution.py:435
  88.8 0.0 collective-permute-done.5
  88.8 3.2 %collective-permute-done.6 = bf16[128,512]{1,0:T(8,128)(2,1)S(1)} collective-permute-done((bf16[128,512]{1,0:T(8,128)(2,1)S(1)}, bf16[128,512]{1,0:T(8,128)(2,1)S(1)}, u32[]{:S(2)}, u32[]{:S(2)}) %collective-permute-start.6) | collective-permute-done | bytes 131104 | tf_op jit(solution)/shard_map/ppermute | solution.py:435
  92.0 5.3 %collective-permute-done.7 = bf16[128,512]{1,0:T(8,128)(2,1)S(1)} collective-permute-done((bf16[128,512]{1,0:T(8,128)(2,1)S(1)}, bf16[128,512]{1,0:T(8,128)(2,1)S(1)}, u32[]{:S(2)}, u32[]{:S(2)}) %collective-permute-start.7) | collective-permute-done | bytes 131104 | tf_op jit(solution)/shard_map/ppermute | solution.py:435
  97.3 0.7 add_convert_fusion
Async XLA Ops:
  2.6 17.7 %collective-permute-start = (bf16[128,256]{1,0:T(8,128)(2,1)}, bf16[128,256]{1,0:T(8,128)(2,1)S(1)}, u32[]{:S(2)}, u32[]{:S(2)}) collective-permute-start(bf16[128,256]{1,0:T(8,128)(2,1)} %get-tuple-element.20), channel_id=1, source_target_pairs={{0,8},{8,16},{16,24},{24,32},{32,40},{40,48},{48,56},{56,64},{64,7... | collective-permute-start | bytes 196616 | tf_op jit(solution)/shard_map/ppermute | solution.py:361
  7.1 26.3 %all-to-all-start = ((bf16[64,16,128]{2,1,0:T(8,128)(2,1)}), bf16[64,16,128]{2,1,0:T(8,128)(2,1)S(1)}, u32[]{:S(2)}, u32[]{:S(2)}) async-start(bf16[64,16,128]{2,1,0:T(8,128)(2,1)} %get-tuple-element.18), calls=%async_computation | async-start | bytes 524288 | tf_op jit(solution)/shard_map/all_to_all | solution.py:360
  20.3 3.2 %copy-start = (bf16[128,256]{1,0:T(8,128)(2,1)}, bf16[128,256]{1,0:T(8,128)(2,1)S(1)}, u32[]{:S(2)}) copy-start(bf16[128,256]{1,0:T(8,128)(2,1)S(1)} %collective-permute-done.prev_in) | copy-start | bytes 196612
  20.3 26.4 %collective-permute-start.1 = (bf16[2,512,512]{2,1,0:T(8,128)(2,1)}, bf16[2,512,512]{2,1,0:T(8,128)(2,1)S(1)}, u32[]{:S(2)}, u32[]{:S(2)}) collective-permute-start(bf16[2,512,512]{2,1,0:T(8,128)(2,1)} %get-tuple-element.22), channel_id=1, source_target_pairs={{0,1},{1,0},{2,3},{3,2},{4,5},{5,4},{6,7},{7,6},{8,9},{9,8},{10,11... | collective-permute-start | bytes 3145736 | tf_op jit(solution)/shard_map/ppermute | solution.py:364
  34.6 23.9 %all-to-all-start.1 = ((bf16[32,88,128]{2,1,0:T(8,128)(2,1)}), bf16[32,88,128]{2,1,0:T(8,128)(2,1)S(1)}, u32[]{:S(2)}, u32[]{:S(2)}) async-start(bf16[32,88,128]{2,1,0:T(8,128)(2,1)} %select.1), calls=%async_computation.1 | async-start | bytes 1441792 | tf_op jit(solution)/shard_map/all_to_all | solution.py:386
  46.7 11.8 %collective-permute-start.2 = (bf16[2,512,512]{2,1,0:T(8,128)(2,1)S(1)}, bf16[2,512,512]{2,1,0:T(8,128)(2,1)S(1)}, u32[]{:S(2)}, u32[]{:S(2)}) collective-permute-start(bf16[2,512,512]{2,1,0:T(8,128)(2,1)S(1)} %collective-permute-done.1.near), channel_id=1, source_target_pairs={{0,8},{8,0},{1,9},{9,1},{2,10},{10,2},{3,11},{11,3},{4,12},{12,4},... | collective-permute-start | bytes 3145736 | tf_op jit(solution)/shard_map/ppermute | solution.py:385
  58.5 6.2 %collective-permute-start.3 = (bf16[32,88,128]{2,1,0:T(8,128)(2,1)S(1)}, bf16[32,88,128]{2,1,0:T(8,128)(2,1)S(1)}, u32[]{:S(2)}, u32[]{:S(2)}) collective-permute-start(bf16[32,88,128]{2,1,0:T(8,128)(2,1)S(1)} %all-to-all-done.1.mine), channel_id=1, source_target_pairs={{0,8},{8,0},{1,9},{9,1},{2,10},{10,2},{3,11},{11,3},{4,12},{12,4},... | collective-permute-start | bytes 2162696 | tf_op jit(solution)/shard_map/ppermute | solution.py:388
  66.9 6.6 %collective-permute-start.4 = (bf16[128,512]{1,0:T(8,128)(2,1)S(1)}, bf16[128,512]{1,0:T(8,128)(2,1)S(1)}, u32[]{:S(2)}, u32[]{:S(2)}) collective-permute-start(bf16[128,512]{1,0:T(8,128)(2,1)S(1)} %finish.1.full), channel_id=1, source_target_pairs={{0,1},{1,0},{2,3},{3,2},{4,5},{5,4},{6,7},{7,6},{8,9},{9,8},{10,11... | collective-permute-start | bytes 393224 | tf_op jit(solution)/shard_map/ppermute | solution.py:406
  74.0 14.8 %collective-permute-start.5 = (bf16[128,512]{1,0:T(8,128)(2,1)S(1)}, bf16[128,512]{1,0:T(8,128)(2,1)S(1)}, u32[]{:S(2)}, u32[]{:S(2)}) collective-permute-start(bf16[128,512]{1,0:T(8,128)(2,1)S(1)} %get-tuple-element.28), channel_id=1, source_target_pairs={{0,2},{2,4},{4,6},{6,0},{1,3},{3,5},{5,7},{7,1},{8,10},{10,12},{12... | collective-permute-start | bytes 393224 | tf_op jit(solution)/shard_map/ppermute | solution.py:435
  78.2 13.8 %collective-permute-start.6 = (bf16[128,512]{1,0:T(8,128)(2,1)S(1)}, bf16[128,512]{1,0:T(8,128)(2,1)S(1)}, u32[]{:S(2)}, u32[]{:S(2)}) collective-permute-start(bf16[128,512]{1,0:T(8,128)(2,1)S(1)} %get-tuple-element.29), channel_id=1, source_target_pairs={{0,4},{2,6},{4,0},{6,2},{1,5},{3,7},{5,1},{7,3},{8,12},{10,14},{12... | collective-permute-start | bytes 393224 | tf_op jit(solution)/shard_map/ppermute | solution.py:435
  83.8 13.5 %collective-permute-start.7 = (bf16[128,512]{1,0:T(8,128)(2,1)S(1)}, bf16[128,512]{1,0:T(8,128)(2,1)S(1)}, u32[]{:S(2)}, u32[]{:S(2)}) collective-permute-start(bf16[128,512]{1,0:T(8,128)(2,1)S(1)} %get-tuple-element.30), channel_id=1, source_target_pairs={{0,6},{2,0},{4,2},{6,4},{1,7},{3,1},{5,3},{7,5},{8,14},{10,8},{12,... | collective-permute-start | bytes 393224 | tf_op jit(solution)/shard_map/ppermute | solution.py:435

commit v11 on v9

--- a/solution.py
+++ b/solution.py
@@ -354,7 +354,6 @@
     recv = lax.all_to_all(packed, CTX, 0, 0, tiled=True)
     prev = lax.ppermute(kv, CTX, [(i, i + 1) for i in range(n_ctx - 1)])
     swap = [(0, 1), (1, 0)]
-    sent, prev = lax.optimization_barrier((sent, prev))
     near = lax.ppermute(sent, "yl", swap)
     slash = pl.pallas_call(
         band_kernel,
@@ -366,7 +365,7 @@
         + [pltpu.SemaphoreType.DMA((7,))],
         name="slash",
         compiler_params=large,
-        cost_estimate=pl.CostEstimate(flops=20000000000, bytes_accessed=1000000, transcendentals=0),
+        cost_estimate=pl.CostEstimate(flops=100000000, bytes_accessed=1000000, transcendentals=0),
     )(queries, keys, values, send_order, offsets, vertical, prev)
     parts = pl.pallas_call(
         select_kernel,
@@ -375,6 +374,9 @@
         out_specs=VMEM,
         name="select",
         compiler_params=small,
+        cost_estimate=pl.CostEstimate(
+            flops=10000000000, bytes_accessed=1000000, transcendentals=0
+        ),
     )(recv, slash.astype(BF16))
     far = lax.ppermute(near, "c", swap)
     mine = lax.all_to_all(parts, ("z", "x"), 0, 0, tiled=True)

time: 97.4 us -> 98.4 us (1.010)
  starting transfers between devices: 35.5 us -> 39.4 us
  waiting for transfers between devices: 24.1 us -> 20.5 us
    all_to_all x1, waiting for transfers between devices: 5.66 us -> 1.5 us  [local(): recv = lax.all_to_all(packed, CTX, 0, 0, tiled=True)]
    all_to_all x1, starting transfers between devices: 3.9 us -> 7.73 us  [local(): mine = lax.all_to_all(parts, ('z', 'x'), 0, 0, tiled=True)]
    all_to_all x1, starting transfers between devices: 13.2 us -> 14.8 us  [local(): recv = lax.all_to_all(packed, CTX, 0, 0, tiled=True)]
    ppermute x1, starting transfers between devices: 3.19 us -> 1.91 us  [local(): far = lax.ppermute(near, 'c', swap)]
where the time goes in v11:
time: 98.4 us; the launch traced here: 96.7 us
  starting transfers between devices  39.4 us (40%)
  blocking collectives  21.1 us (21%)
  waiting for transfers between devices  20.5 us (21%)
  Pallas kernels  13.2 us (13%)
  other arithmetic  1.77 us (2%)
    all_to_all x1, blocking collectives, local(): sums = lax.all_to_all(partial, 'yh', 0, 0, tiled=True)  21.1 us
    all_to_all x1, starting transfers between devices, local(): recv = lax.all_to_all(packed, CTX, 0, 0, tiled=True)  14.8 us
    all_to_all x1, waiting for transfers between devices, local(): mine = lax.all_to_all(parts, ('z', 'x'), 0, 0, tiled=True)  9.3 us
    ppermute x1, waiting for transfers between devices, local(): near = lax.ppermute(sent, 'yl', swap)  8.11 us
    all_to_all x1, starting transfers between devices, local(): mine = lax.all_to_all(parts, ('z', 'x'), 0, 0, tiled=True)  7.73 us
    ppermute x1, starting transfers between devices, local(): other = lax.ppermute(mine, 'c', swap)  4.94 us
    ppermute x1, starting transfers between devices, local(): prev = lax.ppermute(kv, CTX, [(i, i + 1) for i in range(n_ctx - 1)])  3.54 us
    pallas_call x1, Pallas kernels, local(): pl.pallas_call(band_kernel, out_shape=jax.ShapeDtypeStruct((chips, 24, HE...  3.22 us
  transfers between devices with their start and end apart: 7, of which 5 were waited for; matrix products, arithmetic and copies ran while one was open for 1% of the time, Pallas kernels for 8%

profile of v11, /device:TPU:1, one launch (start us, length us, event | category | flops | bytes accessed | tf_op | source)
XLA Modules:
  0.0 96.7 jit_solution(563857200902967739)
XLA Ops:
  0.0 2.6 %pack.1 = (bf16[64,16,128]{2,1,0:T(8,128)(2,1)}, bf16[128,256]{1,0:T(8,128)(2,1)}, bf16[2,512,512]{2,1,0:T(8,128)(2,1)}) custom-call(bf16[128,512]{1,0:T(8,128)(2,1)} %q_in.3, bf16[128,128]{1,0:T(8,128)(2,1)} %keys_in.3, bf16[128,128]{1,0:T(8,128)(2,1)} %values_in.3, s32[1,64]{1,0:T(1,128)} %order_in.3, s32[1,32]{1,0:T(1,128)} %vert_in.3, ...), custom_call_target="tpu_custom_call" | custom-call | tf_op jit(solution)/shard_map/pack/pallas_call | solution.py:341
  2.6 14.8 %all-to-all-start = ((bf16[64,16,128]{2,1,0:T(8,128)(2,1)}), bf16[64,16,128]{2,1,0:T(8,128)(2,1)S(1)}, u32[]{:S(2)}, u32[]{:S(2)}) async-start(bf16[64,16,128]{2,1,0:T(8,128)(2,1)} %get-tuple-element.12), calls=%async_computation | async-start | bytes 524288 | tf_op jit(solution)/shard_map/all_to_all | solution.py:354
  17.4 3.5 %collective-permute-start = (bf16[128,256]{1,0:T(8,128)(2,1)}, bf16[128,256]{1,0:T(8,128)(2,1)S(1)}, u32[]{:S(2)}, u32[]{:S(2)}) collective-permute-start(bf16[128,256]{1,0:T(8,128)(2,1)} %get-tuple-element.13), channel_id=1, source_target_pairs={{0,8},{8,16},{16,24},{24,32},{32,40},{40,48},{48,56},{56,64},{64,7... | collective-permute-start | bytes 196616 | tf_op jit(solution)/shard_map/ppermute | solution.py:355
  21.0 3.2 %collective-permute-start.1 = (bf16[2,512,512]{2,1,0:T(8,128)(2,1)}, bf16[2,512,512]{2,1,0:T(8,128)(2,1)S(1)}, u32[]{:S(2)}, u32[]{:S(2)}) collective-permute-start(bf16[2,512,512]{2,1,0:T(8,128)(2,1)} %get-tuple-element.14), channel_id=1, source_target_pairs={{0,1},{1,0},{2,3},{3,2},{4,5},{5,4},{6,7},{7,6},{8,9},{9,8},{10,11... | collective-permute-start | bytes 3145736 | tf_op jit(solution)/shard_map/ppermute | solution.py:357
  24.2 0.0 collective-permute-done.prev_in
  24.2 0.0 copy-start
  24.2 0.6 copy-done
  24.8 3.2 %slash.1 = f32[32,24,128]{2,1,0:T(8,128)} custom-call(bf16[128,512]{1,0:T(8,128)(2,1)} %q_in.3, bf16[128,128]{1,0:T(8,128)(2,1)} %keys_in.3, bf16[128,128]{1,0:T(8,128)(2,1)} %values_in.3, s32[1,64]{1,0:T(1,128)} %order_in.3, s32[4,64]{1,0:T(4,128)} %offsets_in.1, s32[1,32]{1,0:T(1,128)} %vert_in.3, bf16[128,256]{1,0:T(8,128)(2,1)} %copy-done), custom_call_target="tpu_custom_call" | custom-call | flops 100000000 | bytes 1000000 | tf_op jit(solution)/shard_map/slash/pallas_call | solution.py:358
  28.1 1.0 %convert_element_type.2.slash = bf16[32,24,128]{2,1,0:T(8,128)(2,1)S(1)} convert(f32[32,24,128]{2,1,0:T(8,128)} %slash.1) | non-fusion elementwise | flops 98304 | bytes 589824 | tf_op jit(solution)/shard_map/convert_element_type | solution.py:380
  29.1 1.5 %all-to-all-done.recv = bf16[64,16,128]{2,1,0:T(8,128)(2,1)S(1)} async-done(((bf16[64,16,128]{2,1,0:T(8,128)(2,1)}), bf16[64,16,128]{2,1,0:T(8,128)(2,1)S(1)}, u32[]{:S(2)}, u32[]{:S(2)}) %all-to-all-start) | async-done | bytes 262176 | tf_op jit(solution)/shard_map/all_to_all | solution.py:354
  30.6 1.1 %select.1 = bf16[32,88,128]{2,1,0:T(8,128)(2,1)} custom-call(bf16[64,16,128]{2,1,0:T(8,128)(2,1)S(1)} %all-to-all-done.recv, bf16[32,24,128]{2,1,0:T(8,128)(2,1)S(1)} %convert_element_type.2.slash), custom_call_target="tpu_custom_call" | custom-call | flops 10000000000 | bytes 1000000 | tf_op jit(solution)/shard_map/select/pallas_call | solution.py:370
  31.7 7.7 %all-to-all-start.1 = ((bf16[32,88,128]{2,1,0:T(8,128)(2,1)}), bf16[32,88,128]{2,1,0:T(8,128)(2,1)S(1)}, u32[]{:S(2)}, u32[]{:S(2)}) async-start(bf16[32,88,128]{2,1,0:T(8,128)(2,1)} %select.1), calls=%async_computation.1 | async-start | bytes 1441792 | tf_op jit(solution)/shard_map/all_to_all | solution.py:382
  39.5 8.1 %collective-permute-done.1.near = bf16[2,512,512]{2,1,0:T(8,128)(2,1)S(1)} collective-permute-done((bf16[2,512,512]{2,1,0:T(8,128)(2,1)}, bf16[2,512,512]{2,1,0:T(8,128)(2,1)S(1)}, u32[]{:S(2)}, u32[]{:S(2)}) %collective-permute-start.1) | collective-permute-done | bytes 1048608 | tf_op jit(solution)/shard_map/ppermute | solution.py:357
  47.6 1.9 %collective-permute-start.2 = (bf16[2,512,512]{2,1,0:T(8,128)(2,1)S(1)}, bf16[2,512,512]{2,1,0:T(8,128)(2,1)S(1)}, u32[]{:S(2)}, u32[]{:S(2)}) collective-permute-start(bf16[2,512,512]{2,1,0:T(8,128)(2,1)S(1)} %collective-permute-done.1.near), channel_id=1, source_target_pairs={{0,8},{8,0},{1,9},{9,1},{2,10},{10,2},{3,11},{11,3},{4,12},{12,4},... | collective-permute-start | bytes 3145736 | tf_op jit(solution)/shard_map/ppermute | solution.py:381
  49.5 9.3 %all-to-all-done.1.mine = bf16[32,88,128]{2,1,0:T(8,128)(2,1)S(1)} async-done(((bf16[32,88,128]{2,1,0:T(8,128)(2,1)}), bf16[32,88,128]{2,1,0:T(8,128)(2,1)S(1)}, u32[]{:S(2)}, u32[]{:S(2)}) %all-to-all-start.1) | async-done | bytes 720928 | tf_op jit(solution)/shard_map/all_to_all | solution.py:382
  58.8 0.0 collective-permute-done.2.far
  58.8 4.9 %collective-permute-start.3 = (bf16[32,88,128]{2,1,0:T(8,128)(2,1)S(1)}, bf16[32,88,128]{2,1,0:T(8,128)(2,1)S(1)}, u32[]{:S(2)}, u32[]{:S(2)}) collective-permute-start(bf16[32,88,128]{2,1,0:T(8,128)(2,1)S(1)} %all-to-all-done.1.mine), channel_id=1, source_target_pairs={{0,8},{8,0},{1,9},{9,1},{2,10},{10,2},{3,11},{11,3},{4,12},{12,4},... | collective-permute-start | bytes 2162696 | tf_op jit(solution)/shard_map/ppermute | solution.py:384
  63.8 1.6 %half.1 = f32[512,256]{1,0:T(8,128)S(1)} custom-call(bf16[64,16,128]{2,1,0:T(8,128)(2,1)S(1)} %all-to-all-done.recv, bf16[32,88,128]{2,1,0:T(8,128)(2,1)S(1)} %all-to-all-done.1.mine), custom_call_target="tpu_custom_call" | custom-call | flops 300000000 | bytes 2000000 | tf_op jit(solution)/shard_map/half/pallas_call | solution.py:385
  65.3 0.2 collective-permute-done.3.other
  65.6 2.2 %finish.1.full = bf16[128,512]{1,0:T(8,128)(2,1)S(1)} custom-call(bf16[64,16,128]{2,1,0:T(8,128)(2,1)S(1)} %all-to-all-done.recv, bf16[32,88,128]{2,1,0:T(8,128)(2,1)S(1)} %all-to-all-done.1.mine, bf16[32,88,128]{2,1,0:T(8,128)(2,1)S(1)} %collective-permute-done.3.other, f32[512,256]{1,0:T(8,128)S(1)} %half.1), custom_call_target="tpu_custom_call" | custom-call | tf_op jit(solution)/shard_map/finish/pallas_call | solution.py:394
  67.8 3.2 %collective-permute-start.4 = (bf16[128,512]{1,0:T(8,128)(2,1)S(1)}, bf16[128,512]{1,0:T(8,128)(2,1)S(1)}, u32[]{:S(2)}, u32[]{:S(2)}) collective-permute-start(bf16[128,512]{1,0:T(8,128)(2,1)S(1)} %finish.1.full), channel_id=1, source_target_pairs={{0,1},{1,0},{2,3},{3,2},{4,5},{5,4},{6,7},{7,6},{8,9},{9,8},{10,11... | collective-permute-start | bytes 393224 | tf_op jit(solution)/shard_map/ppermute | solution.py:402
  71.0 2.0 %project_own.1 = (f32[4,128,512]{2,1,0:T(8,128)S(1)}, bf16[4,512,512]{2,1,0:T(8,128)(2,1)S(1)}) custom-call(bf16[128,512]{1,0:T(8,128)(2,1)S(1)} %finish.1.full, bf16[512,4096]{1,0:T(8,128)(2,1)} %weight_in.3, bf16[2,512,512]{2,1,0:T(8,128)(2,1)S(1)} %collective-permute-done.1.near, bf16[2,512,512]{2,1,0:T(8,128)(2,1)S(1)} %collective-permute-done.2.far), custom_call_target="tpu_custom_call" | custom-call | flops 300000000 | bytes 8000000 | tf_op jit(solution)/shard_map/project_own/pallas_call | solution.py:403
  73.1 1.3 %collective-permute-done.4.full = bf16[128,512]{1,0:T(8,128)(2,1)S(1)} collective-permute-done((bf16[128,512]{1,0:T(8,128)(2,1)S(1)}, bf16[128,512]{1,0:T(8,128)(2,1)S(1)}, u32[]{:S(2)}, u32[]{:S(2)}) %collective-permute-start.4) | collective-permute-done | bytes 131104 | tf_op jit(solution)/shard_map/ppermute | solution.py:402
  74.4 0.4 project_both.1
  74.8 21.1 %all_to_all.15 = bf16[4,128,512]{2,1,0:T(8,128)(2,1)S(1)} all-to-all(bf16[4,128,512]{2,1,0:T(8,128)(2,1)S(1)} %project_both.1), channel_id=1, replica_groups=mesh['z'=8,'x'=4,'c'=2,'yh'=4,'yl'=2] {'yh'}, dimensions={0} | all-to-all | bytes 1048576 | tf_op jit(solution)/shard_map/all_to_all | solution.py:428
  95.9 0.7 reduce_sum.12
Async XLA Ops:
  2.6 28.0 %all-to-all-start = ((bf16[64,16,128]{2,1,0:T(8,128)(2,1)}), bf16[64,16,128]{2,1,0:T(8,128)(2,1)S(1)}, u32[]{:S(2)}, u32[]{:S(2)}) async-start(bf16[64,16,128]{2,1,0:T(8,128)(2,1)} %get-tuple-element.12), calls=%async_computation | async-start | bytes 524288 | tf_op jit(solution)/shard_map/all_to_all | solution.py:354
  17.4 6.8 %collective-permute-start = (bf16[128,256]{1,0:T(8,128)(2,1)}, bf16[128,256]{1,0:T(8,128)(2,1)S(1)}, u32[]{:S(2)}, u32[]{:S(2)}) collective-permute-start(bf16[128,256]{1,0:T(8,128)(2,1)} %get-tuple-element.13), channel_id=1, source_target_pairs={{0,8},{8,16},{16,24},{24,32},{32,40},{40,48},{48,56},{56,64},{64,7... | collective-permute-start | bytes 196616 | tf_op jit(solution)/shard_map/ppermute | solution.py:355
  21.0 26.6 %collective-permute-start.1 = (bf16[2,512,512]{2,1,0:T(8,128)(2,1)}, bf16[2,512,512]{2,1,0:T(8,128)(2,1)S(1)}, u32[]{:S(2)}, u32[]{:S(2)}) collective-permute-start(bf16[2,512,512]{2,1,0:T(8,128)(2,1)} %get-tuple-element.14), channel_id=1, source_target_pairs={{0,1},{1,0},{2,3},{3,2},{4,5},{5,4},{6,7},{7,6},{8,9},{9,8},{10,11... | collective-permute-start | bytes 3145736 | tf_op jit(solution)/shard_map/ppermute | solution.py:357
  24.2 0.6 copy-start
  31.7 27.1 %all-to-all-start.1 = ((bf16[32,88,128]{2,1,0:T(8,128)(2,1)}), bf16[32,88,128]{2,1,0:T(8,128)(2,1)S(1)}, u32[]{:S(2)}, u32[]{:S(2)}) async-start(bf16[32,88,128]{2,1,0:T(8,128)(2,1)} %select.1), calls=%async_computation.1 | async-start | bytes 1441792 | tf_op jit(solution)/shard_map/all_to_all | solution.py:382
  47.6 11.2 %collective-permute-start.2 = (bf16[2,512,512]{2,1,0:T(8,128)(2,1)S(1)}, bf16[2,512,512]{2,1,0:T(8,128)(2,1)S(1)}, u32[]{:S(2)}, u32[]{:S(2)}) collective-permute-start(bf16[2,512,512]{2,1,0:T(8,128)(2,1)S(1)} %collective-permute-done.1.near), channel_id=1, source_target_pairs={{0,8},{8,0},{1,9},{9,1},{2,10},{10,2},{3,11},{11,3},{4,12},{12,4},... | collective-permute-start | bytes 3145736 | tf_op jit(solution)/shard_map/ppermute | solution.py:381
  58.8 6.7 %collective-permute-start.3 = (bf16[32,88,128]{2,1,0:T(8,128)(2,1)S(1)}, bf16[32,88,128]{2,1,0:T(8,128)(2,1)S(1)}, u32[]{:S(2)}, u32[]{:S(2)}) collective-permute-start(bf16[32,88,128]{2,1,0:T(8,128)(2,1)S(1)} %all-to-all-done.1.mine), channel_id=1, source_target_pairs={{0,8},{8,0},{1,9},{9,1},{2,10},{10,2},{3,11},{11,3},{4,12},{12,4},... | collective-permute-start | bytes 2162696 | tf_op jit(solution)/shard_map/ppermute | solution.py:384
  67.8 6.6 %collective-permute-start.4 = (bf16[128,512]{1,0:T(8,128)(2,1)S(1)}, bf16[128,512]{1,0:T(8,128)(2,1)S(1)}, u32[]{:S(2)}, u32[]{:S(2)}) collective-permute-start(bf16[128,512]{1,0:T(8,128)(2,1)S(1)} %finish.1.full), channel_id=1, source_target_pairs={{0,1},{1,0},{2,3},{3,2},{4,5},{5,4},{6,7},{7,6},{8,9},{9,8},{10,11... | collective-permute-start | bytes 393224 | tf_op jit(solution)/shard_map/ppermute | solution.py:402
